TPU v7x, 32 devices: a whole 2x2x4 slice. The times are simulated.
32 devices in a mesh: section: 4 (over y, x), shard: 8 (over z, core).
Axes of the slice: x: 2, y: 2, z: 4, core: 2. Of those that a mesh axis runs over, the one named last changes fastest.
Arguments:
- rows: bfloat16 [4, 512, 6144], P('section', 'shard'), may hold values from -6 to 6
- expert_ids: int32 [4, 512, 2], P('section', 'shard'), may hold values from 0 to 7, all different within a row; in each aligned block of 64 rows (0 to 63, 64 to 127, ..., all dimensions but the last counted through in order) at most 18 rows name the same one
- gate_probs: float32 [4, 512, 2], P('section', 'shard'), may hold values from 0.1 to 1
- w_gate: bfloat16 [4, 6144, 8192], P('section', None, 'shard'), may hold values from -0.078125 to 0.078125
- w_up: bfloat16 [4, 6144, 8192], P('section', None, 'shard'), may hold values from -0.078125 to 0.078125
- w_down: bfloat16 [4, 8192, 6144], P('section', 'shard'), may hold values from -0.0625 to 0.0625
Outputs:
- handed: bfloat16 [4, 512, 6144], P('section', 'shard')
Inputs may be any that keep to these rules, and one draw needn't show every extreme that they name: `expert_ids`: within each section's block of 64 tokens of one shard index, no expert is named by more than 18 tokens, and each token names 2 different experts.
All inputs are finite; a program needn't handle non-finite values.
Results may differ from a plain program's by a relative error of at most 0.011.
Values may be sent and summed in bfloat16 or wider, within the bound.
No kernel may reach another device: no remote copies, remote signals or barrier semaphores. Data moves between devices by JAX's collectives and lax.ppermute only.
A program may use at most 128 MiB of HBM per device.

v0:
```python
import jax
import jax.numpy as jnp
from jax import lax
from jax.sharding import PartitionSpec as P

CAP = 18


def from_behind(value, axis, steps):
    count = lax.axis_size(axis)
    pairs = [(source, (source + steps) % count) for source in range(count)]
    return lax.ppermute(value, axis, pairs)


def unpack_rows(slot_values, expert_out, capacity):
    marks = jnp.arange(capacity, dtype=jnp.float32)[:, None]
    placed = (slot_values[None, :] == marks).astype(jnp.bfloat16)
    return lax.dot_general(
        placed, expert_out, (((0,), (0,)), ((), ())), preferred_element_type=jnp.float32
    )


def on_device(rows, expert_ids, gate_probs, w_gate, w_up, w_down):
    tokens = rows[0]
    chosen_ids = expert_ids[0]
    probs = gate_probs[0]
    gate_w = w_gate[0]
    up_w = w_up[0]
    down_w = w_down[0]
    section_num = lax.axis_index("section")
    hit = chosen_ids == section_num
    routed = jnp.any(hit, axis=-1)
    weight = jnp.sum(jnp.where(hit, probs, jnp.float32(0.0)), axis=-1)
    slot = jnp.cumsum(routed.astype(jnp.int32)) - 1
    slot_values = jnp.where(routed, slot, -1).astype(jnp.float32)
    marks = jnp.arange(CAP, dtype=jnp.float32)[:, None]
    placed = (slot_values[None, :] == marks).astype(jnp.bfloat16)
    packed = jnp.dot(placed, tokens, preferred_element_type=jnp.float32).astype(jnp.bfloat16)
    piece = lax.all_gather(packed, "shard", axis=0, tiled=True)
    gate = jnp.dot(piece, gate_w, preferred_element_type=jnp.float32)
    upper = jnp.dot(piece, up_w, preferred_element_type=jnp.float32)
    hidden_all = (jax.nn.silu(gate) * upper).astype(jnp.bfloat16)
    expert_out = lax.psum_scatter(
        jnp.dot(hidden_all, down_w, preferred_element_type=jnp.float32).astype(jnp.bfloat16),
        "shard",
        scatter_dimension=0,
        tiled=True,
    )
    per_token = unpack_rows(slot_values, expert_out, CAP)
    layer_out = (tokens.astype(jnp.float32) + weight[:, None] * per_token).astype(jnp.bfloat16)
    handed = from_behind(layer_out, "section", 1)
    return handed[None]


def solution(mesh):
    in_specs = (
        P("section", "shard", None),
        P("section", "shard", None),
        P("section", "shard", None),
        P("section", None, "shard"),
        P("section", None, "shard"),
        P("section", "shard", None),
    )
    out_specs = P("section", "shard", None)
    return jax.shard_map(
        on_device, mesh=mesh, in_specs=in_specs, out_specs=out_specs, check_vma=False
    )
```

profile of v0, /device:TPU:0, one launch (start us, length us, event | category | flops | bytes accessed | tf_op | source)
XLA Modules:
  0.0 136.0 jit_solution(11000119715441718814)
XLA Ops:
  6.5 0.7 fusion.33
  7.2 0.1 copy.9
  7.3 0.1 reduce-window.8
  7.4 0.1 add_reduce_fusion
  7.6 2.1 %fusion.12 = bf16[1,18,6144]{2,1,0:T(8,128)(2,1)} fusion(bf16[1,64,6144]{2,1,0:T(8,128)(2,1)} %param.6, f32[64]{0:T(128)S(1)} %select_convert_fusion), kind=kOutput, calls=%fused_computation.11 | convolution fusion | flops 14267520 | bytes 1007872 | tf_op jit(solution)/shard_map/dot_general | solution.py:38
  9.6 0.0 all-gather.3.cloned.1.call-update
  9.7 34.5 %all-gather.3.cloned.1.call-done = bf16[8,18,6144]{2,1,0:T(8,128)(2,1)} async-done(((bf16[1,18,6144]{2,1,0:T(8,128)(2,1)}), bf16[8,18,6144]{2,1,0:T(8,128)(2,1)}) %all-gather.3.cloned.1.call-update) | async-done | bytes 1769488 | tf_op jit(solution)/shard_map/all_gather | solution.py:39
  44.1 1.9 %reshape.43 = bf16[144,6144]{1,0:T(8,128)(2,1)S(1)} reshape(bf16[8,18,6144]{2,1,0:T(8,128)(2,1)} %all-gather.3.cloned.1.call-done) | data formatting | bytes 3538944
  46.1 7.4 %fusion.5 = f32[144,1024]{1,0:T(8,128)} fusion(bf16[144,6144]{1,0:T(8,128)(2,1)S(1)} %reshape.43, bf16[1,6144,1024]{2,1,0:T(8,128)(2,1)} %param.9), kind=kOutput, calls=%fused_computation.4 | convolution fusion | flops 1811939328 | bytes 14942208 | tf_op jit(solution)/shard_map/dot_general | solution.py:40
  53.5 12.3 %fusion.7 = bf16[144,6144]{1,0:T(8,128)(2,1)S(1)} fusion(bf16[1,1024,6144]{2,1,0:T(8,128)(2,1)} %param.11, bf16[144,6144]{1,0:T(8,128)(2,1)S(1)} %reshape.43, bf16[1,6144,1024]{2,1,0:T(8,128)(2,1)} %param.10, f32[144,1024]{1,0:T(8,128)} %fusion.5), kind=kOutput, calls=%fused_computation.6 | convolution fusion | flops 3625648128 | bytes 29294592 | tf_op jit(solution)/shard_map/dot_general | solution.py:44
  65.8 0.0 copy-start.3
  65.8 0.0 copy-start.2
  65.8 0.0 copy-start
  65.8 31.1 %fusion = bf16[24,6144]{1,0:T(8,128)(2,1)S(1)} fusion(bf16[144,6144]{1,0:T(8,128)(2,1)S(1)} %fusion.7), kind=kCustom, calls=%all-reduce-scatter | all-reduce-scatter fusion | flops 1179649 | bytes 2064896
  96.9 1.3 collective-permute-start.1
  98.2 0.1 slice
  98.3 1.3 collective-permute-start.2
  99.7 0.6 dynamic-slice.4
  100.9 5.7 %collective-permute-done.2 = bf16[18,6144]{1,0:T(8,128)(2,1)S(1)} collective-permute-done((bf16[18,6144]{1,0:T(8,128)(2,1)S(1)}, bf16[18,6144]{1,0:T(8,128)(2,1)S(1)}, u32[]{:S(2)}, u32[]{:S(2)}) %collective-permute-start.2) | collective-permute-done | bytes 221216
  106.6 1.2 concatenate
  107.8 0.4 fusion.11
  108.3 1.5 %collective-permute-start = (bf16[64,6144]{1,0:T(8,128)(2,1)S(1)}, bf16[64,6144]{1,0:T(8,128)(2,1)S(1)}, u32[]{:S(2)}, u32[]{:S(2)}) collective-permute-start(bf16[64,6144]{1,0:T(8,128)(2,1)S(1)} %fusion.11), channel_id=1, source_target_pairs={{0,8},{8,16},{16,24},{24,0},{1,9},{9,17},{17,25},{25,1},{2,10},{10... | collective-permute-start | bytes 2359304 | tf_op jit(solution)/shard_map/ppermute | solution.py:12
  109.8 18.5 %collective-permute-done = bf16[64,6144]{1,0:T(8,128)(2,1)S(1)} collective-permute-done((bf16[64,6144]{1,0:T(8,128)(2,1)S(1)}, bf16[64,6144]{1,0:T(8,128)(2,1)S(1)}, u32[]{:S(2)}, u32[]{:S(2)}) %collective-permute-start) | collective-permute-done | bytes 786464 | tf_op jit(solution)/shard_map/ppermute | solution.py:12
  128.3 0.9 copy.11
  (10 shorter events, 0.1 us)
Async XLA Ops:
  6.5 37.6 %all-gather.3.cloned.1.call-start = ((), (), s32[]{:S(2)}) async-start(), calls=%async_computation | async-start | bytes 2654208 | tf_op jit(solution)/shard_map/all_gather | solution.py:39
  65.8 33.9 %copy-start.3 = (u32[32]{0:T(128)S(1)}, u32[32]{0:T(128)}, u32[]{:S(2)}) copy-start(u32[32]{0:T(128)} %constant.28) | copy-start | bytes 388
  65.8 35.1 %copy-start.1 = (s32[1,64,2]{1,2,0:T(2,128)S(1)}, s32[1,64,2]{1,2,0:T(2,128)}, u32[]{:S(2)}) copy-start(s32[1,64,2]{1,2,0:T(2,128)} %param.7) | copy-start | bytes 1540
  65.8 35.1 %copy-start.2 = (f32[1,64,2]{1,2,0:T(2,128)S(1)}, f32[1,64,2]{1,2,0:T(2,128)}, u32[]{:S(2)}) copy-start(f32[1,64,2]{1,2,0:T(2,128)} %param.8) | copy-start | bytes 1540
  65.8 42.0 %copy-start = (bf16[1,64,6144]{2,1,0:T(8,128)(2,1)S(1)}, bf16[1,64,6144]{2,1,0:T(8,128)(2,1)}, u32[]{:S(2)}) copy-start(bf16[1,64,6144]{2,1,0:T(8,128)(2,1)} %param.6) | copy-start | bytes 2359300
  96.9 9.7 %collective-permute-start.1 = (bf16[24,6144]{1,0:T(8,128)(2,1)S(1)}, bf16[24,6144]{1,0:T(8,128)(2,1)S(1)}, u32[]{:S(2)}, u32[]{:S(2)}) collective-permute-start(bf16[24,6144]{1,0:T(8,128)(2,1)S(1)} %fusion), channel_id=1, source_target_pairs={{0,1},{1,2},{2,3},{3,4},{4,5},{5,6},{6,7},{8,9},{9,10},{10,11},{11... | collective-permute-start | bytes 884744
  98.3 8.3 %collective-permute-start.2 = (bf16[18,6144]{1,0:T(8,128)(2,1)S(1)}, bf16[18,6144]{1,0:T(8,128)(2,1)S(1)}, u32[]{:S(2)}, u32[]{:S(2)}) collective-permute-start(bf16[18,6144]{1,0:T(8,128)(2,1)S(1)} %slice), channel_id=1, source_target_pairs={{0,2},{1,3},{2,4},{3,5},{4,6},{5,7},{8,10},{9,11},{10,12},{11,13},... | collective-permute-start | bytes 663560
  108.3 20.1 %collective-permute-start = (bf16[64,6144]{1,0:T(8,128)(2,1)S(1)}, bf16[64,6144]{1,0:T(8,128)(2,1)S(1)}, u32[]{:S(2)}, u32[]{:S(2)}) collective-permute-start(bf16[64,6144]{1,0:T(8,128)(2,1)S(1)} %fusion.11), channel_id=1, source_target_pairs={{0,8},{8,16},{16,24},{24,0},{1,9},{9,17},{17,25},{25,1},{2,10},{10... | collective-permute-start | bytes 2359304 | tf_op jit(solution)/shard_map/ppermute | solution.py:12
Sparse Core Ops, SparseCore 0:
  9.8 34.3 all-gather.2
where the time goes:
time: 136 us
  waiting for transfers between devices  58.7 us (43%)
  blocking collectives  31.1 us (23%)
  matrix products  22.2 us (16%)
  between operations  14.2 us (10%)
  local copies, waits for them, and re-layouts  4.78 us (4%)
  starting transfers between devices  4.13 us (3%)
    all_gather x1, waiting for transfers between devices, on_device(): piece = lax.all_gather(packed, 'shard', axis=0, tiled=True)  34.5 us
    unnamed x1, blocking collectives  31.1 us
    ppermute x1, waiting for transfers between devices, from_behind(): return lax.ppermute(value, axis, pairs)  18.5 us
    dot_general x1, matrix products, on_device(): jnp.dot(hidden_all, down_w, preferred_element_type=jnp.float32)  12.3 us
    dot_general x1, matrix products, on_device(): gate = jnp.dot(piece, gate_w, preferred_element_type=jnp.float32)  7.39 us
    unnamed x3, waiting for transfers between devices  5.7 us
    unnamed x13, local copies, waits for them, and re-layouts  4.68 us
  transfers between devices with their start and end apart: 4, of which 3 were waited for; matrix products, arithmetic and copies ran while one was open for 0% of the time, Pallas kernels for 0%

commit v1 on v0

v1 whole, which is shorter than its diff:
```python
import jax
import jax.numpy as jnp
from jax import lax
from jax.experimental import pallas as pl
from jax.experimental.pallas import tpu as pltpu
from jax.sharding import PartitionSpec as P

CAP = 18
MAIN = 16
SLABS = 8
CHUNKS = 2
VMEM_LIMIT = 12 * 1024 * 1024


def params():
    return pltpu.CompilerParams(vmem_limit_bytes=VMEM_LIMIT)


def cost(flops, moved):
    return pl.CostEstimate(flops=flops, bytes_accessed=moved, transcendentals=0)


def whole(count):
    return [pl.BlockSpec(memory_space=pltpu.VMEM)] * count


def pack_kernel(section_ref, ids_ref, probs_ref, tokens_ref, info_ref, *packed_refs):
    section = section_ref[0]
    hit = (ids_ref[...] == section).astype(jnp.float32)
    tokens_count = hit.shape[1]
    routed = jnp.max(hit, axis=0, keepdims=True)
    weight = jnp.sum(hit * probs_ref[...], axis=0, keepdims=True)
    row = lax.broadcasted_iota(jnp.int32, (tokens_count, tokens_count), 0)
    col = lax.broadcasted_iota(jnp.int32, (tokens_count, tokens_count), 1)
    before = (row <= col).astype(jnp.bfloat16)
    counted = jnp.dot(
        jnp.broadcast_to(routed, (MAIN, tokens_count)).astype(jnp.bfloat16),
        before,
        preferred_element_type=jnp.float32,
    )[:1]
    slot = jnp.where(routed > 0.0, counted - 1.0, -1.0)
    out_row = lax.broadcasted_iota(jnp.int32, (2 * MAIN, tokens_count), 0)
    wanted = jnp.where(out_row < MAIN, out_row, MAIN + (out_row - MAIN) // SLABS)
    placed = slot == wanted.astype(jnp.float32)
    width = tokens_ref.shape[1] // CHUNKS
    slab = width // SLABS
    for c in range(CHUNKS):
        rest = jnp.zeros((MAIN, slab), jnp.float32)
        for k in range(SLABS):
            keep = placed & ((out_row < MAIN) | (out_row % SLABS == k))
            mark = jnp.where(keep, 1.0, 0.0).astype(jnp.bfloat16)
            start = c * width + k * slab
            got = jnp.dot(mark, tokens_ref[:, start : start + slab], preferred_element_type=jnp.float32)
            packed_refs[c][:, k * slab : (k + 1) * slab] = got[:MAIN].astype(jnp.bfloat16)
            rest = rest + got[MAIN:]
        packed_refs[c][:, width:] = rest.astype(jnp.bfloat16)
    high = weight.astype(jnp.bfloat16).astype(jnp.float32)
    middle = (weight - high).astype(jnp.bfloat16).astype(jnp.float32)
    low = weight - high - middle
    kind = lax.broadcasted_iota(jnp.int32, (128, tokens_count), 0) % 8
    values = jnp.where(kind == 0, slot, jnp.where(kind == 1, high, jnp.where(kind == 2, middle, low)))
    values = jnp.where(kind < 4, values, 0.0).T
    token = lax.broadcasted_iota(jnp.int32, (tokens_count, 128), 0)
    lane = lax.broadcasted_iota(jnp.int32, (tokens_count, 128), 1)
    values = jnp.where(lane // 8 == token // MAIN, values, 0.0).astype(jnp.bfloat16)
    fold_row = lax.broadcasted_iota(jnp.int32, (MAIN, tokens_count), 0)
    fold_col = lax.broadcasted_iota(jnp.int32, (MAIN, tokens_count), 1)
    fold = (fold_col % MAIN == fold_row).astype(jnp.bfloat16)
    info_ref[...] = jnp.dot(fold, values, preferred_element_type=jnp.float32).astype(jnp.bfloat16)


def fetch_kernel(after_ref, *refs):
    count = len(refs) // 2
    sources, targets, sems = refs[:count], refs[count : 2 * count], refs[-1]
    copies = []
    for a in range(count):
        rows = sources[a].shape[0]
        step = rows // 8
        for i in range(8):
            part = pl.ds(i * step, step)
            copies.append(
                pltpu.make_async_copy(sources[a].at[part], targets[a].at[part], sems.at[a, i])
            )
    for copy in copies:
        copy.start()
    for copy in copies:
        copy.wait()


def regroup(blocks, back):
    size = blocks * 2 * SLABS
    r = lax.broadcasted_iota(jnp.int32, (size, size), 1 if back else 0)
    q = lax.broadcasted_iota(jnp.int32, (size, size), 0 if back else 1)
    slab, pair = r // (2 * blocks), r % (2 * blocks)
    return (q == pair * SLABS + slab).astype(jnp.bfloat16)


def gather_rows(block_refs, x_ref):
    blocks = len(block_refs)
    width = x_ref.shape[1]
    slab = width // SLABS
    for b, ref in enumerate(block_refs):
        x_ref[b * MAIN : (b + 1) * MAIN, :] = ref[:, :width]
    rest = jnp.concatenate([ref[:, width:] for ref in block_refs], axis=0)
    rest = jnp.dot(regroup(blocks, False), rest, preferred_element_type=jnp.float32).astype(jnp.bfloat16)
    for k in range(SLABS):
        x_ref[blocks * MAIN :, k * slab : (k + 1) * slab] = rest[k * 2 * blocks : (k + 1) * 2 * blocks]


def first_kernel(blocks, chunk, *refs):
    block_refs = refs[:blocks]
    w_gate_ref, w_up_ref, gate_ref, up_ref, x_ref = refs[blocks:]
    gather_rows(block_refs, x_ref)
    depth = x_ref.shape[1]
    part = slice(chunk * depth, (chunk + 1) * depth)
    gate_ref[...] = jnp.dot(x_ref[...], w_gate_ref[part, :], preferred_element_type=jnp.float32)
    up_ref[...] = jnp.dot(x_ref[...], w_up_ref[part, :], preferred_element_type=jnp.float32)


def last_kernel(blocks, chunk, *refs):
    block_refs = refs[:blocks]
    w_gate_ref, w_up_ref, gate_ref, up_ref, hidden_ref, x_ref = refs[blocks:]
    gather_rows(block_refs, x_ref)
    depth = x_ref.shape[1]
    part = slice(chunk * depth, (chunk + 1) * depth)
    gate = gate_ref[...] + jnp.dot(x_ref[...], w_gate_ref[part, :], preferred_element_type=jnp.float32)
    upper = up_ref[...] + jnp.dot(x_ref[...], w_up_ref[part, :], preferred_element_type=jnp.float32)
    hidden_ref[...] = (gate / (1.0 + jnp.exp(-gate)) * upper).astype(jnp.bfloat16)


def down_kernel(blocks, chunk, hidden_ref, w_down_ref, own_ref, other_ref):
    half = blocks // 2 * MAIN
    width = w_down_ref.shape[1] // CHUNKS
    slab = width // SLABS
    part = slice(chunk * width, (chunk + 1) * width)
    got = jnp.dot(hidden_ref[...], w_down_ref[:, part], preferred_element_type=jnp.float32)
    main = blocks * MAIN
    own_ref[:, :width] = got[:half].astype(own_ref.dtype)
    other_ref[:, :width] = got[half:main].astype(jnp.bfloat16)
    rest = got[main:].astype(jnp.bfloat16)
    stacked = jnp.concatenate([rest[:, k * slab : (k + 1) * slab] for k in range(SLABS)], axis=0)
    rest = jnp.dot(regroup(blocks, True), stacked, preferred_element_type=jnp.float32)
    own_ref[:, width:] = rest[:half].astype(own_ref.dtype)
    other_ref[:, width:] = rest[half:].astype(jnp.bfloat16)


def add_kernel(own_ref, other_ref, *out_refs):
    total = own_ref[...].astype(jnp.float32) + other_ref[...].astype(jnp.float32)
    for m, ref in enumerate(out_refs):
        ref[...] = total[m * MAIN : (m + 1) * MAIN].astype(ref.dtype)


def sum_kernel(parts, *refs):
    out_ref = refs[-1]
    total = refs[0][...]
    for ref in refs[1:parts]:
        total = total + ref[...].astype(jnp.float32)
    width = total.shape[1]
    out_ref[:, :width] = total.astype(jnp.bfloat16)
    if len(refs) > parts + 1:
        out_ref[:, width:] = refs[parts][...]


def final_kernel(rows_ref, *refs):
    out_ref = refs[-1]
    count = rows_ref.shape[0]
    width = rows_ref.shape[1] // CHUNKS
    slab = width // SLABS
    wide = width + slab
    token = lax.broadcasted_iota(jnp.int32, (count, MAIN), 0)
    column = lax.broadcasted_iota(jnp.int32, (count, MAIN), 1)
    unfold = (token % MAIN == column).astype(jnp.bfloat16)
    info = jnp.dot(unfold, refs[0][:, wide:], preferred_element_type=jnp.float32)
    token = lax.broadcasted_iota(jnp.int32, info.shape, 0)
    lane = lax.broadcasted_iota(jnp.int32, info.shape, 1)
    info = jnp.where(lane // 8 == token // MAIN, info, 0.0)
    slot = jnp.sum(jnp.where(lane % 8 == 0, info, 0.0), axis=1, keepdims=True)
    weight = jnp.sum(jnp.where(lane % 8 == 0, 0.0, info), axis=1, keepdims=True)
    wanted = jnp.where(lane < MAIN, lane, MAIN + (lane - MAIN) // SLABS)
    placed = (slot == wanted.astype(jnp.float32)) & (lane < 2 * MAIN)
    for k in range(SLABS):
        keep = placed & ((lane < MAIN) | (lane % SLABS == k))
        mark = jnp.where(keep, 1.0, 0.0).astype(jnp.bfloat16)[:, : 2 * MAIN]
        for c in range(CHUNKS):
            ref = refs[c]
            values = jnp.concatenate([ref[:, k * slab : (k + 1) * slab], ref[:, width:wide]], axis=0)
            moved = jnp.dot(mark, values, preferred_element_type=jnp.float32)
            span = slice(c * width + k * slab, c * width + (k + 1) * slab)
            out_ref[:, span] = (rows_ref[:, span].astype(jnp.float32) + weight * moved).astype(jnp.bfloat16)


def on_device(rows, expert_ids, gate_probs, w_gate, w_up, w_down):
    bf16, f32 = jnp.bfloat16, jnp.float32
    tokens = rows[0]
    count, model = tokens.shape
    hidden_units = w_gate.shape[2]
    shards = lax.axis_size("shard")
    sections = lax.axis_size("section")
    chips = shards // 2
    width = model // CHUNKS
    wide = width + width // SLABS
    total_rows = shards * CAP

    def along(value, steps):
        return lax.ppermute(value, "shard", [(i, (i + 2 * steps) % shards) for i in range(shards)])

    def swap(value):
        return lax.ppermute(value, "shard", [(i, i ^ 1) for i in range(shards)])

    def onward(value):
        return lax.ppermute(value, "section", [(s, (s + 1) % sections) for s in range(sections)])

    section = lax.axis_index("section").astype(jnp.int32).reshape(1)
    info, *packed = pl.pallas_call(
        pack_kernel,
        out_shape=[jax.ShapeDtypeStruct((MAIN, 128), bf16)]
        + [jax.ShapeDtypeStruct((MAIN, wide), bf16)] * CHUNKS,
        in_specs=[pl.BlockSpec(memory_space=pltpu.SMEM)] + whole(3),
        out_specs=whole(1 + CHUNKS),
        compiler_params=params(),
        cost_estimate=cost(0, 4 * count * model),
        name="pack",
    )(section, expert_ids[0].T, gate_probs[0].T, tokens)

    mine = [[packed[c]] + [along(packed[c], m) for m in range(1, chips)] for c in range(CHUNKS)]
    rows_in = onward(tokens)

    gate_w, up_w, down_w = pl.pallas_call(
        fetch_kernel,
        out_shape=[
            pltpu.VMEM((model, hidden_units), bf16),
            pltpu.VMEM((model, hidden_units), bf16),
            pltpu.VMEM((hidden_units, model), bf16),
        ],
        in_specs=[pl.BlockSpec(memory_space=pl.ANY)] * 4,
        out_specs=whole(3),
        scratch_shapes=[pltpu.SemaphoreType.DMA((3, 8))],
        compiler_params=params(),
        cost_estimate=cost(0, 2 * 3 * 2 * model * hidden_units),
        name="fetch",
    )(packed[0], w_gate[0], w_up[0], w_down[0])

    acc = jax.ShapeDtypeStruct((total_rows, hidden_units), f32)
    state = []
    for c in range(CHUNKS):
        blocks = mine[c] + [swap(block) for block in mine[c]]
        last = c == CHUNKS - 1
        body = last_kernel if last else first_kernel
        state = pl.pallas_call(
            lambda *refs, body=body, c=c: body(shards, c, *refs),
            out_shape=[jax.ShapeDtypeStruct((total_rows, hidden_units), bf16)] if last else [acc, acc],
            in_specs=whole(shards + 2 + len(state)),
            out_specs=whole(1 if last else 2),
            scratch_shapes=[pltpu.VMEM((total_rows, width), bf16)],
            compiler_params=params(),
            cost_estimate=cost(4 * total_rows * width * hidden_units, 4 * width * hidden_units),
            name="hidden" if last else "gate_up",
        )(*blocks, gate_w, up_w, *state)
    hidden = state[0]

    halves = []
    for c in range(CHUNKS):
        own, other = pl.pallas_call(
            lambda *refs, c=c: down_kernel(shards, c, *refs),
            out_shape=[
                jax.ShapeDtypeStruct((chips * MAIN, wide), f32),
                jax.ShapeDtypeStruct((chips * MAIN, wide), bf16),
            ],
            in_specs=whole(2),
            out_specs=whole(2),
            compiler_params=params(),
            cost_estimate=cost(2 * total_rows * width * hidden_units, 2 * width * hidden_units),
            name="down",
        )(hidden, down_w)
        halves.append((own, swap(other)))
    arrived = []
    for c, (own, other) in enumerate(halves):
        kept, *leaving = pl.pallas_call(
            add_kernel,
            out_shape=[jax.ShapeDtypeStruct((MAIN, wide), f32)]
            + [jax.ShapeDtypeStruct((MAIN, wide), bf16)] * (chips - 1),
            in_specs=whole(2),
            out_specs=whole(chips),
            compiler_params=params(),
            name="add_cores",
        )(own, other)
        coming = [along(block, -m) for m, block in enumerate(leaving, 1)]
        extra = [info] if c == 0 else []
        summed = pl.pallas_call(
            lambda *refs: sum_kernel(chips, *refs),
            out_shape=jax.ShapeDtypeStruct((MAIN, wide + 128 * len(extra)), bf16),
            in_specs=whole(chips + len(extra)),
            out_specs=pl.BlockSpec(memory_space=pltpu.VMEM),
            compiler_params=params(),
            name="sum_chips",
        )(kept, *coming, *extra)
        arrived.append(onward(summed))
    out = pl.pallas_call(
        final_kernel,
        out_shape=jax.ShapeDtypeStruct((count, model), bf16),
        in_specs=whole(1 + CHUNKS),
        out_specs=pl.BlockSpec(memory_space=pltpu.VMEM),
        compiler_params=params(),
        name="combine",
    )(rows_in, *arrived)
    return out[None]


def solution(mesh):
    in_specs = (
        P("section", "shard", None),
        P("section", "shard", None),
        P("section", "shard", None),
        P("section", None, "shard"),
        P("section", None, "shard"),
        P("section", "shard", None),
    )
    return jax.shard_map(
        on_device, mesh=mesh, in_specs=in_specs, out_specs=P("section", "shard", None), check_vma=False
    )
```

time: 136 us -> 76.1 us (0.56)
  waiting for transfers between devices: 58.7 us -> 18.4 us
  blocking collectives: 31.1 us -> 0 us
  starting transfers between devices: 4.13 us -> 33.8 us
  matrix products: 22.2 us -> 0 us
  Pallas kernels: 0 us -> 21 us
  between operations: 14.2 us -> 0.13 us
  local copies, waits for them, and re-layouts: 4.78 us -> 2.49 us
    all_gather x1 -> x0, waiting for transfers between devices: 34.5 us -> none  [on_device(): piece = lax.all_gather(packed, 'shard', axis=0, tiled=True)]
    ppermute x1 -> x25, starting transfers between devices: 1.52 us -> 33.8 us  [the longest x12 27 us: along(): lax.ppermute(value, 'shard', [(i, (i + 2 * steps) % shards) for i in rang...]
    unnamed x1 -> x0, blocking collectives: 31.1 us -> none
    dot_general x4 -> x0, matrix products: 22.2 us -> none  [the longest x1 12.3 us: on_device(): jnp.dot(hidden_all, down_w, preferred_element_type=jnp.float32)]
    pallas_call x0 -> x11, Pallas kernels: none -> 21 us  [the longest x1 12.1 us: on_device(): pl.pallas_call(fetch_kernel, out_shape=[pltpu.VMEM((model, hidden_units),...]
    unnamed x3 -> x0, waiting for transfers between devices: 5.7 us -> none
    unnamed x2 -> x0, starting transfers between devices: 2.62 us -> none
    unnamed x13 -> x8, local copies, waits for them, and re-layouts: 4.68 us -> 2.49 us
  transfers between devices with their start and end apart: 4 -> 25, of which waited for: 3 -> 4; matrix products, arithmetic and copies ran while one was open for 0% -> 0% of each run, Pallas kernels for 0% -> 25%
where the time goes in v1:
time: 76.1 us; the launch traced here: 75.9 us
  starting transfers between devices  33.8 us (44%)
  Pallas kernels  21 us (28%)
  waiting for transfers between devices  18.4 us (24%)
  local copies, waits for them, and re-layouts  2.49 us (3%)
    ppermute x12, starting transfers between devices, along(): lax.ppermute(value, 'shard', [(i, (i + 2 * steps) % shards) for i in rang...  27 us
    ppermute x12, waiting for transfers between devices, along(): lax.ppermute(value, 'shard', [(i, (i + 2 * steps) % shards) for i in rang...  14.2 us
    pallas_call x1, Pallas kernels, on_device(): pl.pallas_call(fetch_kernel, out_shape=[pltpu.VMEM((model, hidden_units),...  12.1 us
    ppermute x3, starting transfers between devices, onward(): lax.ppermute(value, 'section', [(s, (s + 1) % sections) for s in range(se...  4.56 us
    pallas_call x2, Pallas kernels, on_device(): pl.pallas_call(lambda *refs, body=body, c=c: body(shards, c, *refs), out_...  4.27 us
    ppermute x3, waiting for transfers between devices, onward(): lax.ppermute(value, 'section', [(s, (s + 1) % sections) for s in range(se...  4.22 us
    pallas_call x2, Pallas kernels, on_device(): pl.pallas_call(lambda *refs, c=c: down_kernel(shards, c, *refs), out_shap...  2.52 us
    unnamed x8, local copies, waits for them, and re-layouts  2.49 us
  transfers between devices with their start and end apart: 25, of which 4 were waited for; matrix products, arithmetic and copies ran while one was open for 0% of the time, Pallas kernels for 25%

profile of v1, /device:TPU:0, one launch (start us, length us, event | category | flops | bytes accessed | tf_op | source)
XLA Modules:
  0.0 75.9 jit_solution(17613796828015330628)
XLA Ops:
  0.0 1.1 %copy-done = bf16[1,64,6144]{2,1,0:T(8,128)(2,1)S(1)} copy-done((bf16[1,64,6144]{2,1,0:T(8,128)(2,1)S(1)}, bf16[1,64,6144]{2,1,0:T(8,128)(2,1)}, u32[]{:S(2)}) %copy-start) | copy-done | bytes 786456
  2.9 3.1 %collective-permute-start.8 = (bf16[16,3456]{1,0:T(8,128)(2,1)S(1)}, bf16[16,3456]{1,0:T(8,128)(2,1)S(1)}, u32[]{:S(2)}, u32[]{:S(2)}) collective-permute-start(bf16[16,3456]{1,0:T(8,128)(2,1)S(1)} %get-tuple-element.26.after_ref.refs_0_), channel_id=1, source_target_pairs={{0,2},{1,3},{2,4},{3,5},{4,6},{5,7},{6,0},{7,1},{8,10},{9,11},{10,... | collective-permute-start | bytes 331784 | tf_op jit(solution)/shard_map/ppermute | solution.py:205
  6.0 2.6 %collective-permute-start.9 = (bf16[16,3456]{1,0:T(8,128)(2,1)S(1)}, bf16[16,3456]{1,0:T(8,128)(2,1)S(1)}, u32[]{:S(2)}, u32[]{:S(2)}) collective-permute-start(bf16[16,3456]{1,0:T(8,128)(2,1)S(1)} %get-tuple-element.26.after_ref.refs_0_), channel_id=1, source_target_pairs={{0,4},{1,5},{2,6},{3,7},{4,0},{5,1},{6,2},{7,3},{8,12},{9,13},{10,... | collective-permute-start | bytes 331784 | tf_op jit(solution)/shard_map/ppermute | solution.py:205
  8.6 1.3 %collective-permute-start.10 = (bf16[16,3456]{1,0:T(8,128)(2,1)S(1)}, bf16[16,3456]{1,0:T(8,128)(2,1)S(1)}, u32[]{:S(2)}, u32[]{:S(2)}) collective-permute-start(bf16[16,3456]{1,0:T(8,128)(2,1)S(1)} %get-tuple-element.26.after_ref.refs_0_), channel_id=1, source_target_pairs={{0,6},{1,7},{2,0},{3,1},{4,2},{5,3},{6,4},{7,5},{8,14},{9,15},{10,... | collective-permute-start | bytes 331784 | tf_op jit(solution)/shard_map/ppermute | solution.py:205
  9.9 0.7 collective-permute-start.1
  10.6 1.4 %collective-permute-done.8.refs_1_ = bf16[16,3456]{1,0:T(8,128)(2,1)S(1)} collective-permute-done((bf16[16,3456]{1,0:T(8,128)(2,1)S(1)}, bf16[16,3456]{1,0:T(8,128)(2,1)S(1)}, u32[]{:S(2)}, u32[]{:S(2)}) %collective-permute-start.8) | collective-permute-done | bytes 110624 | tf_op jit(solution)/shard_map/ppermute | solution.py:205
  12.0 5.9 %collective-permute-start.2 = (bf16[16,3456]{1,0:T(8,128)(2,1)S(1)}, bf16[16,3456]{1,0:T(8,128)(2,1)S(1)}, u32[]{:S(2)}, u32[]{:S(2)}) collective-permute-start(bf16[16,3456]{1,0:T(8,128)(2,1)S(1)} %get-tuple-element.25.refs_0_), channel_id=1, source_target_pairs={{0,4},{1,5},{2,6},{3,7},{4,0},{5,1},{6,2},{7,3},{8,12},{9,13},{10,... | collective-permute-start | bytes 331784 | tf_op jit(solution)/shard_map/ppermute | solution.py:205
  17.9 4.2 %collective-permute-start.3 = (bf16[16,3456]{1,0:T(8,128)(2,1)S(1)}, bf16[16,3456]{1,0:T(8,128)(2,1)S(1)}, u32[]{:S(2)}, u32[]{:S(2)}) collective-permute-start(bf16[16,3456]{1,0:T(8,128)(2,1)S(1)} %get-tuple-element.25.refs_0_), channel_id=1, source_target_pairs={{0,6},{1,7},{2,0},{3,1},{4,2},{5,3},{6,4},{7,5},{8,14},{9,15},{10,... | collective-permute-start | bytes 331784 | tf_op jit(solution)/shard_map/ppermute | solution.py:205
  22.7 12.1 %fetch.1 = (bf16[6144,1024]{1,0:T(8,128)(2,1)S(1)}, bf16[6144,1024]{1,0:T(8,128)(2,1)S(1)}, bf16[1024,6144]{1,0:T(8,128)(2,1)S(1)}) custom-call(bf16[16,3456]{1,0:T(8,128)(2,1)S(1)} %get-tuple-element.26.after_ref.refs_0_, bf16[6144,1024]{1,0:T(8,128)(2,1)} %bitcast.16, bf16[6144,1024]{1,0:T(8,128)(2,1)} %bitcast.17, bf16[1024,6144]{1,0:T(8,128)(2,1)} %bitcast.18), custom_call_target="tpu_custom_call" | custom-call | bytes 75497472 | tf_op jit(solution)/shard_map/fetch/pallas_call | solution.py:228
  35.3 1.5 %collective-permute-start = (bf16[64,6144]{1,0:T(8,128)(2,1)S(1)}, bf16[64,6144]{1,0:T(8,128)(2,1)S(1)}, u32[]{:S(2)}, u32[]{:S(2)}) collective-permute-start(bf16[64,6144]{1,0:T(8,128)(2,1)S(1)} %bitcast.13), channel_id=1, source_target_pairs={{0,8},{8,16},{16,24},{24,0},{1,9},{9,17},{17,25},{25,1},{2,10},{10... | collective-permute-start | bytes 2359304 | tf_op jit(solution)/shard_map/ppermute | solution.py:211
  37.4 2.1 %gate_up.1 = (f32[144,1024]{1,0:T(8,128)S(1)}, f32[144,1024]{1,0:T(8,128)S(1)}) custom-call(bf16[16,3456]{1,0:T(8,128)(2,1)S(1)} %get-tuple-element.26.after_ref.refs_0_, bf16[16,3456]{1,0:T(8,128)(2,1)S(1)} %collective-permute-done.8.refs_1_, bf16[16,3456]{1,0:T(8,128)(2,1)S(1)} %collective-permute-done.9.refs_2_, ...), custom_call_target="tpu_custom_call" | custom-call | flops 1811939328 | bytes 12582912 | tf_op jit(solution)/shard_map/gate_up/pallas_call | solution.py:249
  39.5 2.2 %hidden.1.refs_0_ = bf16[144,1024]{1,0:T(8,128)(2,1)S(1)} custom-call(bf16[16,3456]{1,0:T(8,128)(2,1)S(1)} %get-tuple-element.25.refs_0_, bf16[16,3456]{1,0:T(8,128)(2,1)S(1)} %collective-permute-done.1.refs_1_, bf16[16,3456]{1,0:T(8,128)(2,1)S(1)} %collective-permute-done.2.refs_2_, bf16[16,3456]{1,0:T(8,128)(2,1)S(1)} %collective-permute-done.3.refs_3_, ...), custom_call_target="tpu_custom_call" | custom-call | flops 1811939328 | bytes 12582912 | tf_op jit(solution)/shard_map/hidden/pallas_call | solution.py:249
  41.7 1.3 %down.2 = (f32[64,3456]{1,0:T(8,128)S(1)}, bf16[64,3456]{1,0:T(8,128)(2,1)S(1)}) custom-call(bf16[144,1024]{1,0:T(8,128)(2,1)S(1)} %hidden.1.refs_0_, bf16[1024,6144]{1,0:T(8,128)(2,1)S(1)} %get-tuple-element.31.refs_1_), custom_call_target="tpu_custom_call" | custom-call | flops 905969664 | bytes 6291456 | tf_op jit(solution)/shard_map/down/pallas_call | solution.py:263
  43.5 1.3 %down.3 = (f32[64,3456]{1,0:T(8,128)S(1)}, bf16[64,3456]{1,0:T(8,128)(2,1)S(1)}) custom-call(bf16[144,1024]{1,0:T(8,128)(2,1)S(1)} %hidden.1.refs_0_, bf16[1024,6144]{1,0:T(8,128)(2,1)S(1)} %get-tuple-element.31.refs_1_), custom_call_target="tpu_custom_call" | custom-call | flops 905969664 | bytes 6291456 | tf_op jit(solution)/shard_map/down/pallas_call | solution.py:263
  45.1 3.4 %collective-permute-start.17 = (bf16[16,3456]{1,0:T(8,128)(2,1)S(1)}, bf16[16,3456]{1,0:T(8,128)(2,1)S(1)}, u32[]{:S(2)}, u32[]{:S(2)}) collective-permute-start(bf16[16,3456]{1,0:T(8,128)(2,1)S(1)} %get-tuple-element.36), channel_id=1, source_target_pairs={{0,4},{1,5},{2,6},{3,7},{4,0},{5,1},{6,2},{7,3},{8,12},{9,13},{10,... | collective-permute-start | bytes 331784 | tf_op jit(solution)/shard_map/ppermute | solution.py:205
  48.5 1.9 %collective-permute-start.18 = (bf16[16,3456]{1,0:T(8,128)(2,1)S(1)}, bf16[16,3456]{1,0:T(8,128)(2,1)S(1)}, u32[]{:S(2)}, u32[]{:S(2)}) collective-permute-start(bf16[16,3456]{1,0:T(8,128)(2,1)S(1)} %get-tuple-element.37), channel_id=1, source_target_pairs={{0,2},{1,3},{2,4},{3,5},{4,6},{5,7},{6,0},{7,1},{8,10},{9,11},{10,... | collective-permute-start | bytes 331784 | tf_op jit(solution)/shard_map/ppermute | solution.py:205
  50.5 1.9 %collective-permute-start.21 = (bf16[16,3456]{1,0:T(8,128)(2,1)S(1)}, bf16[16,3456]{1,0:T(8,128)(2,1)S(1)}, u32[]{:S(2)}, u32[]{:S(2)}) collective-permute-start(bf16[16,3456]{1,0:T(8,128)(2,1)S(1)} %get-tuple-element.42), channel_id=1, source_target_pairs={{0,6},{1,7},{2,0},{3,1},{4,2},{5,3},{6,4},{7,5},{8,14},{9,15},{10,... | collective-permute-start | bytes 331784 | tf_op jit(solution)/shard_map/ppermute | solution.py:205
  52.4 1.8 %collective-permute-start.22 = (bf16[16,3456]{1,0:T(8,128)(2,1)S(1)}, bf16[16,3456]{1,0:T(8,128)(2,1)S(1)}, u32[]{:S(2)}, u32[]{:S(2)}) collective-permute-start(bf16[16,3456]{1,0:T(8,128)(2,1)S(1)} %get-tuple-element.43), channel_id=1, source_target_pairs={{0,4},{1,5},{2,6},{3,7},{4,0},{5,1},{6,2},{7,3},{8,12},{9,13},{10,... | collective-permute-start | bytes 331784 | tf_op jit(solution)/shard_map/ppermute | solution.py:205
  54.3 5.2 %collective-permute-done.17.refs_2_ = bf16[16,3456]{1,0:T(8,128)(2,1)S(1)} collective-permute-done((bf16[16,3456]{1,0:T(8,128)(2,1)S(1)}, bf16[16,3456]{1,0:T(8,128)(2,1)S(1)}, u32[]{:S(2)}, u32[]{:S(2)}) %collective-permute-start.17) | collective-permute-done | bytes 110624 | tf_op jit(solution)/shard_map/ppermute | solution.py:205
  59.5 1.5 %collective-permute-start.19 = (bf16[16,3584]{1,0:T(8,128)(2,1)S(1)}, bf16[16,3584]{1,0:T(8,128)(2,1)S(1)}, u32[]{:S(2)}, u32[]{:S(2)}) collective-permute-start(bf16[16,3584]{1,0:T(8,128)(2,1)S(1)} %sum_chips.2), channel_id=1, source_target_pairs={{0,8},{8,16},{16,24},{24,0},{1,9},{9,17},{17,25},{25,1},{2,10},{10... | collective-permute-start | bytes 344072 | tf_op jit(solution)/shard_map/ppermute | solution.py:211
  61.0 7.6 %collective-permute-done.22.refs_2_ = bf16[16,3456]{1,0:T(8,128)(2,1)S(1)} collective-permute-done((bf16[16,3456]{1,0:T(8,128)(2,1)S(1)}, bf16[16,3456]{1,0:T(8,128)(2,1)S(1)}, u32[]{:S(2)}, u32[]{:S(2)}) %collective-permute-start.22) | collective-permute-done | bytes 110624 | tf_op jit(solution)/shard_map/ppermute | solution.py:205
  68.7 1.5 %collective-permute-start.24 = (bf16[16,3456]{1,0:T(8,128)(2,1)S(1)}, bf16[16,3456]{1,0:T(8,128)(2,1)S(1)}, u32[]{:S(2)}, u32[]{:S(2)}) collective-permute-start(bf16[16,3456]{1,0:T(8,128)(2,1)S(1)} %sum_chips.3), channel_id=1, source_target_pairs={{0,8},{8,16},{16,24},{24,0},{1,9},{9,17},{17,25},{25,1},{2,10},{10... | collective-permute-start | bytes 331784 | tf_op jit(solution)/shard_map/ppermute | solution.py:211
  70.2 4.2 %collective-permute-done.24.refs_1_ = bf16[16,3456]{1,0:T(8,128)(2,1)S(1)} collective-permute-done((bf16[16,3456]{1,0:T(8,128)(2,1)S(1)}, bf16[16,3456]{1,0:T(8,128)(2,1)S(1)}, u32[]{:S(2)}, u32[]{:S(2)}) %collective-permute-start.24) | collective-permute-done | bytes 110624 | tf_op jit(solution)/shard_map/ppermute | solution.py:211
  74.5 1.4 %combine.1 = bf16[64,6144]{1,0:T(8,128)(2,1)} custom-call(bf16[64,6144]{1,0:T(8,128)(2,1)S(1)} %collective-permute-done.rows_ref, bf16[16,3584]{1,0:T(8,128)(2,1)S(1)} %collective-permute-done.19.refs_0_, bf16[16,3456]{1,0:T(8,128)(2,1)S(1)} %collective-permute-done.24.refs_1_), custom_call_target="tpu_custom_call" | custom-call | tf_op jit(solution)/shard_map/combine/pallas_call | solution.py:298
  (45 shorter events, 4.5 us)
Async XLA Ops:
  2.9 9.1 %collective-permute-start.8 = (bf16[16,3456]{1,0:T(8,128)(2,1)S(1)}, bf16[16,3456]{1,0:T(8,128)(2,1)S(1)}, u32[]{:S(2)}, u32[]{:S(2)}) collective-permute-start(bf16[16,3456]{1,0:T(8,128)(2,1)S(1)} %get-tuple-element.26.after_ref.refs_0_), channel_id=1, source_target_pairs={{0,2},{1,3},{2,4},{3,5},{4,6},{5,7},{6,0},{7,1},{8,10},{9,11},{10,... | collective-permute-start | bytes 331784 | tf_op jit(solution)/shard_map/ppermute | solution.py:205
  6.0 11.9 %collective-permute-start.9 = (bf16[16,3456]{1,0:T(8,128)(2,1)S(1)}, bf16[16,3456]{1,0:T(8,128)(2,1)S(1)}, u32[]{:S(2)}, u32[]{:S(2)}) collective-permute-start(bf16[16,3456]{1,0:T(8,128)(2,1)S(1)} %get-tuple-element.26.after_ref.refs_0_), channel_id=1, source_target_pairs={{0,4},{1,5},{2,6},{3,7},{4,0},{5,1},{6,2},{7,3},{8,12},{9,13},{10,... | collective-permute-start | bytes 331784 | tf_op jit(solution)/shard_map/ppermute | solution.py:205
  8.6 13.6 %collective-permute-start.10 = (bf16[16,3456]{1,0:T(8,128)(2,1)S(1)}, bf16[16,3456]{1,0:T(8,128)(2,1)S(1)}, u32[]{:S(2)}, u32[]{:S(2)}) collective-permute-start(bf16[16,3456]{1,0:T(8,128)(2,1)S(1)} %get-tuple-element.26.after_ref.refs_0_), channel_id=1, source_target_pairs={{0,6},{1,7},{2,0},{3,1},{4,2},{5,3},{6,4},{7,5},{8,14},{9,15},{10,... | collective-permute-start | bytes 331784 | tf_op jit(solution)/shard_map/ppermute | solution.py:205
  9.9 12.2 %collective-permute-start.11 = (bf16[16,3456]{1,0:T(8,128)(2,1)S(1)}, bf16[16,3456]{1,0:T(8,128)(2,1)S(1)}, u32[]{:S(2)}, u32[]{:S(2)}) collective-permute-start(bf16[16,3456]{1,0:T(8,128)(2,1)S(1)} %get-tuple-element.26.after_ref.refs_0_), channel_id=1, source_target_pairs={{0,1},{1,0},{2,3},{3,2},{4,5},{5,4},{6,7},{7,6},{8,9},{9,8},{10,11... | collective-permute-start | bytes 331784 | tf_op jit(solution)/shard_map/ppermute | solution.py:208
  9.9 12.7 %collective-permute-start.1 = (bf16[16,3456]{1,0:T(8,128)(2,1)S(1)}, bf16[16,3456]{1,0:T(8,128)(2,1)S(1)}, u32[]{:S(2)}, u32[]{:S(2)}) collective-permute-start(bf16[16,3456]{1,0:T(8,128)(2,1)S(1)} %get-tuple-element.25.refs_0_), channel_id=1, source_target_pairs={{0,2},{1,3},{2,4},{3,5},{4,6},{5,7},{6,0},{7,1},{8,10},{9,11},{10,... | collective-permute-start | bytes 331784 | tf_op jit(solution)/shard_map/ppermute | solution.py:205
  12.0 22.8 %collective-permute-start.2 = (bf16[16,3456]{1,0:T(8,128)(2,1)S(1)}, bf16[16,3456]{1,0:T(8,128)(2,1)S(1)}, u32[]{:S(2)}, u32[]{:S(2)}) collective-permute-start(bf16[16,3456]{1,0:T(8,128)(2,1)S(1)} %get-tuple-element.25.refs_0_), channel_id=1, source_target_pairs={{0,4},{1,5},{2,6},{3,7},{4,0},{5,1},{6,2},{7,3},{8,12},{9,13},{10,... | collective-permute-start | bytes 331784 | tf_op jit(solution)/shard_map/ppermute | solution.py:205
  17.9 17.4 %collective-permute-start.3 = (bf16[16,3456]{1,0:T(8,128)(2,1)S(1)}, bf16[16,3456]{1,0:T(8,128)(2,1)S(1)}, u32[]{:S(2)}, u32[]{:S(2)}) collective-permute-start(bf16[16,3456]{1,0:T(8,128)(2,1)S(1)} %get-tuple-element.25.refs_0_), channel_id=1, source_target_pairs={{0,6},{1,7},{2,0},{3,1},{4,2},{5,3},{6,4},{7,5},{8,14},{9,15},{10,... | collective-permute-start | bytes 331784 | tf_op jit(solution)/shard_map/ppermute | solution.py:205
  22.1 14.7 %collective-permute-start.12 = (bf16[16,3456]{1,0:T(8,128)(2,1)S(1)}, bf16[16,3456]{1,0:T(8,128)(2,1)S(1)}, u32[]{:S(2)}, u32[]{:S(2)}) collective-permute-start(bf16[16,3456]{1,0:T(8,128)(2,1)S(1)} %collective-permute-done.8.refs_1_), channel_id=1, source_target_pairs={{0,1},{1,0},{2,3},{3,2},{4,5},{5,4},{6,7},{7,6},{8,9},{9,8},{10,11... | collective-permute-start | bytes 331784 | tf_op jit(solution)/shard_map/ppermute | solution.py:208
  22.1 14.7 %collective-permute-start.13 = (bf16[16,3456]{1,0:T(8,128)(2,1)S(1)}, bf16[16,3456]{1,0:T(8,128)(2,1)S(1)}, u32[]{:S(2)}, u32[]{:S(2)}) collective-permute-start(bf16[16,3456]{1,0:T(8,128)(2,1)S(1)} %collective-permute-done.9.refs_2_), channel_id=1, source_target_pairs={{0,1},{1,0},{2,3},{3,2},{4,5},{5,4},{6,7},{7,6},{8,9},{9,8},{10,11... | collective-permute-start | bytes 331784 | tf_op jit(solution)/shard_map/ppermute | solution.py:208
  22.6 14.7 %collective-permute-start.14 = (bf16[16,3456]{1,0:T(8,128)(2,1)S(1)}, bf16[16,3456]{1,0:T(8,128)(2,1)S(1)}, u32[]{:S(2)}, u32[]{:S(2)}) collective-permute-start(bf16[16,3456]{1,0:T(8,128)(2,1)S(1)} %collective-permute-done.10.refs_3_), channel_id=1, source_target_pairs={{0,1},{1,0},{2,3},{3,2},{4,5},{5,4},{6,7},{7,6},{8,9},{9,8},{10,11... | collective-permute-start | bytes 331784 | tf_op jit(solution)/shard_map/ppermute | solution.py:208
  34.8 4.7 %collective-permute-start.4 = (bf16[16,3456]{1,0:T(8,128)(2,1)S(1)}, bf16[16,3456]{1,0:T(8,128)(2,1)S(1)}, u32[]{:S(2)}, u32[]{:S(2)}) collective-permute-start(bf16[16,3456]{1,0:T(8,128)(2,1)S(1)} %get-tuple-element.25.refs_0_), channel_id=1, source_target_pairs={{0,1},{1,0},{2,3},{3,2},{4,5},{5,4},{6,7},{7,6},{8,9},{9,8},{10,11... | collective-permute-start | bytes 331784 | tf_op jit(solution)/shard_map/ppermute | solution.py:208
  35.3 34.9 %collective-permute-start = (bf16[64,6144]{1,0:T(8,128)(2,1)S(1)}, bf16[64,6144]{1,0:T(8,128)(2,1)S(1)}, u32[]{:S(2)}, u32[]{:S(2)}) collective-permute-start(bf16[64,6144]{1,0:T(8,128)(2,1)S(1)} %bitcast.13), channel_id=1, source_target_pairs={{0,8},{8,16},{16,24},{24,0},{1,9},{9,17},{17,25},{25,1},{2,10},{10... | collective-permute-start | bytes 2359304 | tf_op jit(solution)/shard_map/ppermute | solution.py:211
  36.8 2.7 %collective-permute-start.5 = (bf16[16,3456]{1,0:T(8,128)(2,1)S(1)}, bf16[16,3456]{1,0:T(8,128)(2,1)S(1)}, u32[]{:S(2)}, u32[]{:S(2)}) collective-permute-start(bf16[16,3456]{1,0:T(8,128)(2,1)S(1)} %collective-permute-done.1.refs_1_), channel_id=1, source_target_pairs={{0,1},{1,0},{2,3},{3,2},{4,5},{5,4},{6,7},{7,6},{8,9},{9,8},{10,11... | collective-permute-start | bytes 331784 | tf_op jit(solution)/shard_map/ppermute | solution.py:208
  36.8 2.7 %collective-permute-start.6 = (bf16[16,3456]{1,0:T(8,128)(2,1)S(1)}, bf16[16,3456]{1,0:T(8,128)(2,1)S(1)}, u32[]{:S(2)}, u32[]{:S(2)}) collective-permute-start(bf16[16,3456]{1,0:T(8,128)(2,1)S(1)} %collective-permute-done.2.refs_2_), channel_id=1, source_target_pairs={{0,1},{1,0},{2,3},{3,2},{4,5},{5,4},{6,7},{7,6},{8,9},{9,8},{10,11... | collective-permute-start | bytes 331784 | tf_op jit(solution)/shard_map/ppermute | solution.py:208
  37.3 2.2 %collective-permute-start.7 = (bf16[16,3456]{1,0:T(8,128)(2,1)S(1)}, bf16[16,3456]{1,0:T(8,128)(2,1)S(1)}, u32[]{:S(2)}, u32[]{:S(2)}) collective-permute-start(bf16[16,3456]{1,0:T(8,128)(2,1)S(1)} %collective-permute-done.3.refs_3_), channel_id=1, source_target_pairs={{0,1},{1,0},{2,3},{3,2},{4,5},{5,4},{6,7},{7,6},{8,9},{9,8},{10,11... | collective-permute-start | bytes 331784 | tf_op jit(solution)/shard_map/ppermute | solution.py:208
  44.7 5.7 %collective-permute-start.20 = (bf16[64,3456]{1,0:T(8,128)(2,1)S(1)}, bf16[64,3456]{1,0:T(8,128)(2,1)S(1)}, u32[]{:S(2)}, u32[]{:S(2)}) collective-permute-start(bf16[64,3456]{1,0:T(8,128)(2,1)S(1)} %get-tuple-element.40), channel_id=1, source_target_pairs={{0,1},{1,0},{2,3},{3,2},{4,5},{5,4},{6,7},{7,6},{8,9},{9,8},{10,11... | collective-permute-start | bytes 1327112 | tf_op jit(solution)/shard_map/ppermute | solution.py:208
  45.0 7.4 %collective-permute-start.16 = (bf16[16,3456]{1,0:T(8,128)(2,1)S(1)}, bf16[16,3456]{1,0:T(8,128)(2,1)S(1)}, u32[]{:S(2)}, u32[]{:S(2)}) collective-permute-start(bf16[16,3456]{1,0:T(8,128)(2,1)S(1)} %get-tuple-element.35), channel_id=1, source_target_pairs={{0,6},{1,7},{2,0},{3,1},{4,2},{5,3},{6,4},{7,5},{8,14},{9,15},{10,... | collective-permute-start | bytes 331784 | tf_op jit(solution)/shard_map/ppermute | solution.py:205
  45.1 14.3 %collective-permute-start.17 = (bf16[16,3456]{1,0:T(8,128)(2,1)S(1)}, bf16[16,3456]{1,0:T(8,128)(2,1)S(1)}, u32[]{:S(2)}, u32[]{:S(2)}) collective-permute-start(bf16[16,3456]{1,0:T(8,128)(2,1)S(1)} %get-tuple-element.36), channel_id=1, source_target_pairs={{0,4},{1,5},{2,6},{3,7},{4,0},{5,1},{6,2},{7,3},{8,12},{9,13},{10,... | collective-permute-start | bytes 331784 | tf_op jit(solution)/shard_map/ppermute | solution.py:205
  48.5 10.9 %collective-permute-start.18 = (bf16[16,3456]{1,0:T(8,128)(2,1)S(1)}, bf16[16,3456]{1,0:T(8,128)(2,1)S(1)}, u32[]{:S(2)}, u32[]{:S(2)}) collective-permute-start(bf16[16,3456]{1,0:T(8,128)(2,1)S(1)} %get-tuple-element.37), channel_id=1, source_target_pairs={{0,2},{1,3},{2,4},{3,5},{4,6},{5,7},{6,0},{7,1},{8,10},{9,11},{10,... | collective-permute-start | bytes 331784 | tf_op jit(solution)/shard_map/ppermute | solution.py:205
  50.5 10.5 %collective-permute-start.21 = (bf16[16,3456]{1,0:T(8,128)(2,1)S(1)}, bf16[16,3456]{1,0:T(8,128)(2,1)S(1)}, u32[]{:S(2)}, u32[]{:S(2)}) collective-permute-start(bf16[16,3456]{1,0:T(8,128)(2,1)S(1)} %get-tuple-element.42), channel_id=1, source_target_pairs={{0,6},{1,7},{2,0},{3,1},{4,2},{5,3},{6,4},{7,5},{8,14},{9,15},{10,... | collective-permute-start | bytes 331784 | tf_op jit(solution)/shard_map/ppermute | solution.py:205
  52.4 16.2 %collective-permute-start.22 = (bf16[16,3456]{1,0:T(8,128)(2,1)S(1)}, bf16[16,3456]{1,0:T(8,128)(2,1)S(1)}, u32[]{:S(2)}, u32[]{:S(2)}) collective-permute-start(bf16[16,3456]{1,0:T(8,128)(2,1)S(1)} %get-tuple-element.43), channel_id=1, source_target_pairs={{0,4},{1,5},{2,6},{3,7},{4,0},{5,1},{6,2},{7,3},{8,12},{9,13},{10,... | collective-permute-start | bytes 331784 | tf_op jit(solution)/shard_map/ppermute | solution.py:205
  59.4 9.2 %collective-permute-start.23 = (bf16[16,3456]{1,0:T(8,128)(2,1)S(1)}, bf16[16,3456]{1,0:T(8,128)(2,1)S(1)}, u32[]{:S(2)}, u32[]{:S(2)}) collective-permute-start(bf16[16,3456]{1,0:T(8,128)(2,1)S(1)} %get-tuple-element.44), channel_id=1, source_target_pairs={{0,2},{1,3},{2,4},{3,5},{4,6},{5,7},{6,0},{7,1},{8,10},{9,11},{10,... | collective-permute-start | bytes 331784 | tf_op jit(solution)/shard_map/ppermute | solution.py:205
  59.5 15.0 %collective-permute-start.19 = (bf16[16,3584]{1,0:T(8,128)(2,1)S(1)}, bf16[16,3584]{1,0:T(8,128)(2,1)S(1)}, u32[]{:S(2)}, u32[]{:S(2)}) collective-permute-start(bf16[16,3584]{1,0:T(8,128)(2,1)S(1)} %sum_chips.2), channel_id=1, source_target_pairs={{0,8},{8,16},{16,24},{24,0},{1,9},{9,17},{17,25},{25,1},{2,10},{10... | collective-permute-start | bytes 344072 | tf_op jit(solution)/shard_map/ppermute | solution.py:211
  68.7 5.8 %collective-permute-start.24 = (bf16[16,3456]{1,0:T(8,128)(2,1)S(1)}, bf16[16,3456]{1,0:T(8,128)(2,1)S(1)}, u32[]{:S(2)}, u32[]{:S(2)}) collective-permute-start(bf16[16,3456]{1,0:T(8,128)(2,1)S(1)} %sum_chips.3), channel_id=1, source_target_pairs={{0,8},{8,16},{16,24},{24,0},{1,9},{9,17},{17,25},{25,1},{2,10},{10... | collective-permute-start | bytes 331784 | tf_op jit(solution)/shard_map/ppermute | solution.py:211
  (5 other events, 17.0 us)

commit v2 on v1

--- a/solution.py
+++ b/solution.py
@@ -9,7 +9,7 @@
 MAIN = 16
 SLABS = 8
 CHUNKS = 2
-VMEM_LIMIT = 12 * 1024 * 1024
+VMEM_LIMIT = 8 * 1024 * 1024
 
 
 def params():
@@ -20,11 +20,25 @@
     return pl.CostEstimate(flops=flops, bytes_accessed=moved, transcendentals=0)
 
 
+def in_hbm(value):
+    return pltpu.with_memory_space_constraint(value, pltpu.HBM)
+
+
+def in_vmem(value):
+    return pltpu.with_memory_space_constraint(value, pltpu.VMEM)
+
+
 def whole(count):
     return [pl.BlockSpec(memory_space=pltpu.VMEM)] * count
 
 
-def pack_kernel(section_ref, ids_ref, probs_ref, tokens_ref, info_ref, *packed_refs):
+def pack_kernel(section_ref, ids_in, probs_in, tokens_in, info_ref, packed_ref, ids_ref, probs_ref, tokens_ref, sems):
+    pairs = ((ids_in, ids_ref), (probs_in, probs_ref), (tokens_in, tokens_ref))
+    copies = [pltpu.make_async_copy(a, b, sems.at[i]) for i, (a, b) in enumerate(pairs)]
+    for copy in copies:
+        copy.start()
+    copies[0].wait()
+    copies[1].wait()
     section = section_ref[0]
     hit = (ids_ref[...] == section).astype(jnp.float32)
     tokens_count = hit.shape[1]
@@ -42,18 +56,18 @@
     out_row = lax.broadcasted_iota(jnp.int32, (2 * MAIN, tokens_count), 0)
     wanted = jnp.where(out_row < MAIN, out_row, MAIN + (out_row - MAIN) // SLABS)
     placed = slot == wanted.astype(jnp.float32)
-    width = tokens_ref.shape[1] // CHUNKS
+    width = tokens_ref.shape[1]
     slab = width // SLABS
-    for c in range(CHUNKS):
-        rest = jnp.zeros((MAIN, slab), jnp.float32)
-        for k in range(SLABS):
-            keep = placed & ((out_row < MAIN) | (out_row % SLABS == k))
-            mark = jnp.where(keep, 1.0, 0.0).astype(jnp.bfloat16)
-            start = c * width + k * slab
-            got = jnp.dot(mark, tokens_ref[:, start : start + slab], preferred_element_type=jnp.float32)
-            packed_refs[c][:, k * slab : (k + 1) * slab] = got[:MAIN].astype(jnp.bfloat16)
-            rest = rest + got[MAIN:]
-        packed_refs[c][:, width:] = rest.astype(jnp.bfloat16)
+    copies[2].wait()
+    rest = jnp.zeros((MAIN, slab), jnp.float32)
+    for k in range(SLABS):
+        keep = placed & ((out_row < MAIN) | (out_row % SLABS == k))
+        mark = jnp.where(keep, 1.0, 0.0).astype(jnp.bfloat16)
+        part = slice(k * slab, (k + 1) * slab)
+        got = jnp.dot(mark, tokens_ref[:, part], preferred_element_type=jnp.float32)
+        packed_ref[:, part] = got[:MAIN].astype(jnp.bfloat16)
+        rest = rest + got[MAIN:]
+    packed_ref[:, width:] = rest.astype(jnp.bfloat16)
     high = weight.astype(jnp.bfloat16).astype(jnp.float32)
     middle = (weight - high).astype(jnp.bfloat16).astype(jnp.float32)
     low = weight - high - middle
@@ -70,17 +84,14 @@
 
 
 def fetch_kernel(after_ref, *refs):
-    count = len(refs) // 2
-    sources, targets, sems = refs[:count], refs[count : 2 * count], refs[-1]
+    done_ref, sems = refs[-2:]
+    done_ref[...] = jnp.zeros(done_ref.shape, done_ref.dtype)
     copies = []
-    for a in range(count):
-        rows = sources[a].shape[0]
-        step = rows // 8
+    for a, (source, target) in enumerate(zip(refs[:3], refs[3:])):
+        step = source.shape[0] // 8
         for i in range(8):
             part = pl.ds(i * step, step)
-            copies.append(
-                pltpu.make_async_copy(sources[a].at[part], targets[a].at[part], sems.at[a, i])
-            )
+            copies.append(pltpu.make_async_copy(source.at[part], target.at[part], sems.at[a, i]))
     for copy in copies:
         copy.start()
     for copy in copies:
@@ -95,36 +106,28 @@
     return (q == pair * SLABS + slab).astype(jnp.bfloat16)
 
 
-def gather_rows(block_refs, x_ref):
-    blocks = len(block_refs)
+def gather_rows(blocks, mine_ref, other_ref, x_ref):
     width = x_ref.shape[1]
     slab = width // SLABS
-    for b, ref in enumerate(block_refs):
-        x_ref[b * MAIN : (b + 1) * MAIN, :] = ref[:, :width]
-    rest = jnp.concatenate([ref[:, width:] for ref in block_refs], axis=0)
+    half = blocks // 2 * MAIN
+    x_ref[:half, :] = mine_ref[:, :width]
+    x_ref[half : 2 * half, :] = other_ref[:, :width]
+    rest = jnp.concatenate([mine_ref[:, width:], other_ref[:, width:]], axis=0)
     rest = jnp.dot(regroup(blocks, False), rest, preferred_element_type=jnp.float32).astype(jnp.bfloat16)
     for k in range(SLABS):
         x_ref[blocks * MAIN :, k * slab : (k + 1) * slab] = rest[k * 2 * blocks : (k + 1) * 2 * blocks]
 
 
-def first_kernel(blocks, chunk, *refs):
-    block_refs = refs[:blocks]
-    w_gate_ref, w_up_ref, gate_ref, up_ref, x_ref = refs[blocks:]
-    gather_rows(block_refs, x_ref)
-    depth = x_ref.shape[1]
-    part = slice(chunk * depth, (chunk + 1) * depth)
-    gate_ref[...] = jnp.dot(x_ref[...], w_gate_ref[part, :], preferred_element_type=jnp.float32)
-    up_ref[...] = jnp.dot(x_ref[...], w_up_ref[part, :], preferred_element_type=jnp.float32)
-
-
-def last_kernel(blocks, chunk, *refs):
-    block_refs = refs[:blocks]
-    w_gate_ref, w_up_ref, gate_ref, up_ref, hidden_ref, x_ref = refs[blocks:]
-    gather_rows(block_refs, x_ref)
-    depth = x_ref.shape[1]
-    part = slice(chunk * depth, (chunk + 1) * depth)
-    gate = gate_ref[...] + jnp.dot(x_ref[...], w_gate_ref[part, :], preferred_element_type=jnp.float32)
-    upper = up_ref[...] + jnp.dot(x_ref[...], w_up_ref[part, :], preferred_element_type=jnp.float32)
+def stack_kernel(blocks, *refs):
+    out_ref = refs[-1]
+    for b, ref in enumerate(refs[:blocks]):
+        out_ref[b * MAIN : (b + 1) * MAIN, :] = ref[...]
+
+
+def hidden_kernel(blocks, mine_ref, other_ref, w_gate_ref, w_up_ref, hidden_ref, x_ref):
+    gather_rows(blocks, mine_ref, other_ref, x_ref)
+    gate = jnp.dot(x_ref[...], w_gate_ref[...], preferred_element_type=jnp.float32)
+    upper = jnp.dot(x_ref[...], w_up_ref[...], preferred_element_type=jnp.float32)
     hidden_ref[...] = (gate / (1.0 + jnp.exp(-gate)) * upper).astype(jnp.bfloat16)
 
 
@@ -191,8 +194,7 @@
 
 def on_device(rows, expert_ids, gate_probs, w_gate, w_up, w_down):
     bf16, f32 = jnp.bfloat16, jnp.float32
-    tokens = rows[0]
-    count, model = tokens.shape
+    _, count, model = rows.shape
     hidden_units = w_gate.shape[2]
     shards = lax.axis_size("shard")
     sections = lax.axis_size("section")
@@ -211,52 +213,62 @@
         return lax.ppermute(value, "section", [(s, (s + 1) % sections) for s in range(sections)])
 
     section = lax.axis_index("section").astype(jnp.int32).reshape(1)
-    info, *packed = pl.pallas_call(
+    info, packed = pl.pallas_call(
         pack_kernel,
-        out_shape=[jax.ShapeDtypeStruct((MAIN, 128), bf16)]
-        + [jax.ShapeDtypeStruct((MAIN, wide), bf16)] * CHUNKS,
-        in_specs=[pl.BlockSpec(memory_space=pltpu.SMEM)] + whole(3),
-        out_specs=whole(1 + CHUNKS),
+        out_shape=[
+            jax.ShapeDtypeStruct((MAIN, 128), bf16),
+            jax.ShapeDtypeStruct((MAIN, model + model // SLABS), bf16),
+        ],
+        in_specs=[pl.BlockSpec(memory_space=pltpu.SMEM)] + [pl.BlockSpec(memory_space=pltpu.HBM)] * 3,
+        out_specs=whole(2),
+        scratch_shapes=[
+            pltpu.VMEM(expert_ids.shape[:0:-1], jnp.int32),
+            pltpu.VMEM(gate_probs.shape[:0:-1], f32),
+            pltpu.VMEM((count, model), bf16),
+            pltpu.SemaphoreType.DMA((3,)),
+        ],
         compiler_params=params(),
         cost_estimate=cost(0, 4 * count * model),
         name="pack",
-    )(section, expert_ids[0].T, gate_probs[0].T, tokens)
-
-    mine = [[packed[c]] + [along(packed[c], m) for m in range(1, chips)] for c in range(CHUNKS)]
-    rows_in = onward(tokens)
-
-    gate_w, up_w, down_w = pl.pallas_call(
+    )(section, in_hbm(expert_ids[0].T), in_hbm(gate_probs[0].T), in_hbm(rows[0]))
+
+    mine = [packed] + [along(packed, m) for m in range(1, chips)]
+
+    gate_w, up_w, down_w, done = pl.pallas_call(
         fetch_kernel,
         out_shape=[
             pltpu.VMEM((model, hidden_units), bf16),
             pltpu.VMEM((model, hidden_units), bf16),
             pltpu.VMEM((hidden_units, model), bf16),
+            jax.ShapeDtypeStruct((8, 128), f32),
         ],
-        in_specs=[pl.BlockSpec(memory_space=pl.ANY)] * 4,
-        out_specs=whole(3),
+        in_specs=[pl.BlockSpec(memory_space=pl.ANY)] + [pl.BlockSpec(memory_space=pltpu.HBM)] * 3,
+        out_specs=whole(4),
         scratch_shapes=[pltpu.SemaphoreType.DMA((3, 8))],
+        compiler_params=pltpu.CompilerParams(vmem_limit_bytes=12*1024*1024),
+        cost_estimate=cost(0, 3 * 2 * 2 * model * hidden_units),
+        name="fetch",
+    )(packed, in_hbm(w_gate[0]), in_hbm(w_up[0]), in_hbm(w_down[0]))
+    rows_in = onward(rows[0])
+
+    held = pl.pallas_call(
+        lambda *refs: stack_kernel(chips, *refs),
+        out_shape=jax.ShapeDtypeStruct((chips * MAIN, model + model // SLABS), bf16),
+        in_specs=whole(chips + 1),
+        out_specs=pl.BlockSpec(memory_space=pltpu.VMEM),
         compiler_params=params(),
-        cost_estimate=cost(0, 2 * 3 * 2 * model * hidden_units),
-        name="fetch",
-    )(packed[0], w_gate[0], w_up[0], w_down[0])
-
-    acc = jax.ShapeDtypeStruct((total_rows, hidden_units), f32)
-    state = []
-    for c in range(CHUNKS):
-        blocks = mine[c] + [swap(block) for block in mine[c]]
-        last = c == CHUNKS - 1
-        body = last_kernel if last else first_kernel
-        state = pl.pallas_call(
-            lambda *refs, body=body, c=c: body(shards, c, *refs),
-            out_shape=[jax.ShapeDtypeStruct((total_rows, hidden_units), bf16)] if last else [acc, acc],
-            in_specs=whole(shards + 2 + len(state)),
-            out_specs=whole(1 if last else 2),
-            scratch_shapes=[pltpu.VMEM((total_rows, width), bf16)],
-            compiler_params=params(),
-            cost_estimate=cost(4 * total_rows * width * hidden_units, 4 * width * hidden_units),
-            name="hidden" if last else "gate_up",
-        )(*blocks, gate_w, up_w, *state)
-    hidden = state[0]
+        name="stack",
+    )(*mine, done)
+    hidden = pl.pallas_call(
+        lambda *refs: hidden_kernel(shards, *refs),
+        out_shape=jax.ShapeDtypeStruct((total_rows, hidden_units), bf16),
+        in_specs=whole(4),
+        out_specs=pl.BlockSpec(memory_space=pltpu.VMEM),
+        scratch_shapes=[pltpu.VMEM((total_rows, model), bf16)],
+        compiler_params=params(),
+        cost_estimate=cost(4 * total_rows * model * hidden_units, 4 * model * hidden_units),
+        name="hidden",
+    )(held, swap(held), gate_w, up_w)
 
     halves = []
     for c in range(CHUNKS):

time: 76.1 us -> 65.2 us (0.86)
  starting transfers between devices: 33.8 us -> 26.2 us
  local copies, waits for them, and re-layouts: 2.49 us -> 0.01 us
  waiting for transfers between devices: 18.4 us -> 16.9 us
  Pallas kernels: 21 us -> 21.8 us
    ppermute x12 -> x9, starting transfers between devices: 27 us -> 20.9 us  [along(): lax.ppermute(value, 'shard', [(i, (i + 2 * steps) % shards) for i in rang...]
    unnamed x8 -> x2, local copies, waits for them, and re-layouts: 2.49 us -> 0.01 us
    ppermute x12 -> x9, waiting for transfers between devices: 14.2 us -> 11.9 us  [along(): lax.ppermute(value, 'shard', [(i, (i + 2 * steps) % shards) for i in rang...]
    ppermute x10 -> x3, starting transfers between devices: 2.3 us -> 0.71 us  [swap(): return lax.ppermute(value, 'shard', [(i, i ^ 1) for i in range(shards)])]
    pallas_call x1, Pallas kernels: 0.39 us -> 1.45 us  [on_device(): pl.pallas_call(pack_kernel, out_shape=[jax.ShapeDtypeStruct((MAIN, 128),...]
    ppermute x10 -> x3, waiting for transfers between devices: 0.05 us -> 0.86 us  [swap(): return lax.ppermute(value, 'shard', [(i, i ^ 1) for i in range(shards)])]
  transfers between devices with their start and end apart: 25 -> 15, of which waited for: 4 -> 5; matrix products, arithmetic and copies ran while one was open for 0% -> 0% of each run, Pallas kernels for 25% -> 29%
where the time goes in v2:
time: 65.2 us; the launch traced here: 65.1 us
  starting transfers between devices  26.2 us (40%)
  Pallas kernels  21.8 us (33%)
  waiting for transfers between devices  16.9 us (26%)
    ppermute x9, starting transfers between devices, along(): lax.ppermute(value, 'shard', [(i, (i + 2 * steps) % shards) for i in rang...  20.9 us
    pallas_call x1, Pallas kernels, on_device(): pl.pallas_call(fetch_kernel, out_shape=[pltpu.VMEM((model, hidden_units),...  12.1 us
    ppermute x9, waiting for transfers between devices, along(): lax.ppermute(value, 'shard', [(i, (i + 2 * steps) % shards) for i in rang...  11.9 us
    ppermute x3, starting transfers between devices, onward(): lax.ppermute(value, 'section', [(s, (s + 1) % sections) for s in range(se...  4.63 us
    ppermute x3, waiting for transfers between devices, onward(): lax.ppermute(value, 'section', [(s, (s + 1) % sections) for s in range(se...  4.16 us
    pallas_call x1, Pallas kernels, on_device(): pl.pallas_call(lambda *refs: hidden_kernel(shards, *refs), out_shape=jax....  4.02 us
    pallas_call x2, Pallas kernels, on_device(): pl.pallas_call(lambda *refs, c=c: down_kernel(shards, c, *refs), out_shap...  2.53 us
    pallas_call x1, Pallas kernels, on_device(): pl.pallas_call(pack_kernel, out_shape=[jax.ShapeDtypeStruct((MAIN, 128),...  1.45 us
  transfers between devices with their start and end apart: 15, of which 5 were waited for; matrix products, arithmetic and copies ran while one was open for 0% of the time, Pallas kernels for 29%

profile of v2, /device:TPU:0, one launch (start us, length us, event | category | flops | bytes accessed | tf_op | source)
XLA Modules:
  0.0 65.1 jit_solution(15220987903661954694)
XLA Ops:
  0.0 1.5 %pack.1 = (bf16[16,128]{1,0:T(8,128)(2,1)S(1)}, bf16[16,6912]{1,0:T(8,128)(2,1)S(1)}) custom-call(s32[1]{0:T(128)} %bitcast.1.section_ref, s32[2,64]{1,0:T(2,128)} %bitcast.17, f32[2,64]{1,0:T(2,128)} %bitcast.18, bf16[64,6144]{1,0:T(8,128)(2,1)} %bitcast.15), custom_call_target="tpu_custom_call" | custom-call | bytes 1572864 | tf_op jit(solution)/shard_map/pack/pallas_call | solution.py:216
  1.5 3.1 %collective-permute-start.1 = (bf16[16,6912]{1,0:T(8,128)(2,1)S(1)}, bf16[16,6912]{1,0:T(8,128)(2,1)S(1)}, u32[]{:S(2)}, u32[]{:S(2)}) collective-permute-start(bf16[16,6912]{1,0:T(8,128)(2,1)S(1)} %get-tuple-element.23.after_ref.refs_0_), channel_id=1, source_target_pairs={{0,2},{1,3},{2,4},{3,5},{4,6},{5,7},{6,0},{7,1},{8,10},{9,11},{10,... | collective-permute-start | bytes 663560 | tf_op jit(solution)/shard_map/ppermute | solution.py:207
  4.5 2.6 %collective-permute-start.2 = (bf16[16,6912]{1,0:T(8,128)(2,1)S(1)}, bf16[16,6912]{1,0:T(8,128)(2,1)S(1)}, u32[]{:S(2)}, u32[]{:S(2)}) collective-permute-start(bf16[16,6912]{1,0:T(8,128)(2,1)S(1)} %get-tuple-element.23.after_ref.refs_0_), channel_id=1, source_target_pairs={{0,4},{1,5},{2,6},{3,7},{4,0},{5,1},{6,2},{7,3},{8,12},{9,13},{10,... | collective-permute-start | bytes 663560 | tf_op jit(solution)/shard_map/ppermute | solution.py:207
  7.1 1.4 %collective-permute-start.3 = (bf16[16,6912]{1,0:T(8,128)(2,1)S(1)}, bf16[16,6912]{1,0:T(8,128)(2,1)S(1)}, u32[]{:S(2)}, u32[]{:S(2)}) collective-permute-start(bf16[16,6912]{1,0:T(8,128)(2,1)S(1)} %get-tuple-element.23.after_ref.refs_0_), channel_id=1, source_target_pairs={{0,6},{1,7},{2,0},{3,1},{4,2},{5,3},{6,4},{7,5},{8,14},{9,15},{10,... | collective-permute-start | bytes 663560 | tf_op jit(solution)/shard_map/ppermute | solution.py:207
  8.5 12.1 %fetch.1 = (bf16[6144,1024]{1,0:T(8,128)(2,1)S(1)}, bf16[6144,1024]{1,0:T(8,128)(2,1)S(1)}, bf16[1024,6144]{1,0:T(8,128)(2,1)S(1)}, f32[8,128]{1,0:T(8,128)S(1)}) custom-call(bf16[16,6912]{1,0:T(8,128)(2,1)S(1)} %get-tuple-element.23.after_ref.refs_0_, bf16[6144,1024]{1,0:T(8,128)(2,1)} %bitcast.12, bf16[6144,1024]{1,0:T(8,128)(2,1)} %bitcast.13, ...), custom_call_target="tpu_custom_call" | custom-call | bytes 75497472 | tf_op jit(solution)/shard_map/fetch/pallas_call | solution.py:237
  20.6 1.0 %collective-permute-done.2.refs_2_ = bf16[16,6912]{1,0:T(8,128)(2,1)S(1)} collective-permute-done((bf16[16,6912]{1,0:T(8,128)(2,1)S(1)}, bf16[16,6912]{1,0:T(8,128)(2,1)S(1)}, u32[]{:S(2)}, u32[]{:S(2)}) %collective-permute-start.2) | collective-permute-done | bytes 221216 | tf_op jit(solution)/shard_map/ppermute | solution.py:207
  21.8 1.5 %collective-permute-start = (bf16[64,6144]{1,0:T(8,128)(2,1)S(1)}, bf16[64,6144]{1,0:T(8,128)(2,1)S(1)}, u32[]{:S(2)}, u32[]{:S(2)}) collective-permute-start(bf16[64,6144]{1,0:T(8,128)(2,1)S(1)} %bitcast.16), channel_id=1, source_target_pairs={{0,8},{8,16},{16,24},{24,0},{1,9},{9,17},{17,25},{25,1},{2,10},{10... | collective-permute-start | bytes 2359304 | tf_op jit(solution)/shard_map/ppermute | solution.py:213
  23.3 0.9 %collective-permute-done.4.refs_1_ = bf16[64,6912]{1,0:T(8,128)(2,1)S(1)} collective-permute-done((bf16[64,6912]{1,0:T(8,128)(2,1)S(1)}, bf16[64,6912]{1,0:T(8,128)(2,1)S(1)}, u32[]{:S(2)}, u32[]{:S(2)}) %collective-permute-start.4) | collective-permute-done | bytes 884768 | tf_op jit(solution)/shard_map/ppermute | solution.py:210
  24.2 4.0 %hidden.1.refs_0_ = bf16[144,1024]{1,0:T(8,128)(2,1)S(1)} custom-call(bf16[64,6912]{1,0:T(8,128)(2,1)S(1)} %stack.1.refs_0_, bf16[64,6912]{1,0:T(8,128)(2,1)S(1)} %collective-permute-done.4.refs_1_, bf16[6144,1024]{1,0:T(8,128)(2,1)S(1)} %get-tuple-element.25.refs_2_, bf16[6144,1024]{1,0:T(8,128)(2,1)S(1)} %get-tuple-element.26.refs_3_), custom_call_target="tpu_custom_call" | custom-call | flops 3623878656 | bytes 25165824 | tf_op jit(solution)/shard_map/hidden/pallas_call | solution.py:262
  28.2 1.3 %down.2 = (f32[64,3456]{1,0:T(8,128)S(1)}, bf16[64,3456]{1,0:T(8,128)(2,1)S(1)}) custom-call(bf16[144,1024]{1,0:T(8,128)(2,1)S(1)} %hidden.1.refs_0_, bf16[1024,6144]{1,0:T(8,128)(2,1)S(1)} %get-tuple-element.27.refs_1_), custom_call_target="tpu_custom_call" | custom-call | flops 905969664 | bytes 6291456 | tf_op jit(solution)/shard_map/down/pallas_call | solution.py:275
  29.5 0.2 collective-permute-start.5
  29.7 1.3 %down.3 = (f32[64,3456]{1,0:T(8,128)S(1)}, bf16[64,3456]{1,0:T(8,128)(2,1)S(1)}) custom-call(bf16[144,1024]{1,0:T(8,128)(2,1)S(1)} %hidden.1.refs_0_, bf16[1024,6144]{1,0:T(8,128)(2,1)S(1)} %get-tuple-element.27.refs_1_), custom_call_target="tpu_custom_call" | custom-call | flops 905969664 | bytes 6291456 | tf_op jit(solution)/shard_map/down/pallas_call | solution.py:275
  30.9 0.4 collective-permute-start.10
  31.5 6.3 %collective-permute-start.6 = (bf16[16,3456]{1,0:T(8,128)(2,1)S(1)}, bf16[16,3456]{1,0:T(8,128)(2,1)S(1)}, u32[]{:S(2)}, u32[]{:S(2)}) collective-permute-start(bf16[16,3456]{1,0:T(8,128)(2,1)S(1)} %get-tuple-element.31), channel_id=1, source_target_pairs={{0,6},{1,7},{2,0},{3,1},{4,2},{5,3},{6,4},{7,5},{8,14},{9,15},{10,... | collective-permute-start | bytes 331784 | tf_op jit(solution)/shard_map/ppermute | solution.py:207
  37.7 0.4 collective-permute-start.7
  38.2 0.2 collective-permute-start.8
  38.5 3.7 %collective-permute-start.11 = (bf16[16,3456]{1,0:T(8,128)(2,1)S(1)}, bf16[16,3456]{1,0:T(8,128)(2,1)S(1)}, u32[]{:S(2)}, u32[]{:S(2)}) collective-permute-start(bf16[16,3456]{1,0:T(8,128)(2,1)S(1)} %get-tuple-element.38), channel_id=1, source_target_pairs={{0,6},{1,7},{2,0},{3,1},{4,2},{5,3},{6,4},{7,5},{8,14},{9,15},{10,... | collective-permute-start | bytes 331784 | tf_op jit(solution)/shard_map/ppermute | solution.py:207
  42.2 3.3 %collective-permute-start.12 = (bf16[16,3456]{1,0:T(8,128)(2,1)S(1)}, bf16[16,3456]{1,0:T(8,128)(2,1)S(1)}, u32[]{:S(2)}, u32[]{:S(2)}) collective-permute-start(bf16[16,3456]{1,0:T(8,128)(2,1)S(1)} %get-tuple-element.39), channel_id=1, source_target_pairs={{0,4},{1,5},{2,6},{3,7},{4,0},{5,1},{6,2},{7,3},{8,12},{9,13},{10,... | collective-permute-start | bytes 331784 | tf_op jit(solution)/shard_map/ppermute | solution.py:207
  45.4 4.5 %collective-permute-done.7.refs_2_ = bf16[16,3456]{1,0:T(8,128)(2,1)S(1)} collective-permute-done((bf16[16,3456]{1,0:T(8,128)(2,1)S(1)}, bf16[16,3456]{1,0:T(8,128)(2,1)S(1)}, u32[]{:S(2)}, u32[]{:S(2)}) %collective-permute-start.7) | collective-permute-done | bytes 110624 | tf_op jit(solution)/shard_map/ppermute | solution.py:207
  50.0 1.5 %collective-permute-start.9 = (bf16[16,3584]{1,0:T(8,128)(2,1)S(1)}, bf16[16,3584]{1,0:T(8,128)(2,1)S(1)}, u32[]{:S(2)}, u32[]{:S(2)}) collective-permute-start(bf16[16,3584]{1,0:T(8,128)(2,1)S(1)} %sum_chips.2), channel_id=1, source_target_pairs={{0,8},{8,16},{16,24},{24,0},{1,9},{9,17},{17,25},{25,1},{2,10},{10... | collective-permute-start | bytes 344072 | tf_op jit(solution)/shard_map/ppermute | solution.py:213
  51.5 6.3 %collective-permute-done.12.refs_2_ = bf16[16,3456]{1,0:T(8,128)(2,1)S(1)} collective-permute-done((bf16[16,3456]{1,0:T(8,128)(2,1)S(1)}, bf16[16,3456]{1,0:T(8,128)(2,1)S(1)}, u32[]{:S(2)}, u32[]{:S(2)}) %collective-permute-start.12) | collective-permute-done | bytes 110624 | tf_op jit(solution)/shard_map/ppermute | solution.py:207
  57.9 1.5 %collective-permute-start.14 = (bf16[16,3456]{1,0:T(8,128)(2,1)S(1)}, bf16[16,3456]{1,0:T(8,128)(2,1)S(1)}, u32[]{:S(2)}, u32[]{:S(2)}) collective-permute-start(bf16[16,3456]{1,0:T(8,128)(2,1)S(1)} %sum_chips.3), channel_id=1, source_target_pairs={{0,8},{8,16},{16,24},{24,0},{1,9},{9,17},{17,25},{25,1},{2,10},{10... | collective-permute-start | bytes 331784 | tf_op jit(solution)/shard_map/ppermute | solution.py:213
  59.5 4.2 %collective-permute-done.14.refs_1_ = bf16[16,3456]{1,0:T(8,128)(2,1)S(1)} collective-permute-done((bf16[16,3456]{1,0:T(8,128)(2,1)S(1)}, bf16[16,3456]{1,0:T(8,128)(2,1)S(1)}, u32[]{:S(2)}, u32[]{:S(2)}) %collective-permute-start.14) | collective-permute-done | bytes 110624 | tf_op jit(solution)/shard_map/ppermute | solution.py:213
  63.6 1.4 %combine.1 = bf16[64,6144]{1,0:T(8,128)(2,1)} custom-call(bf16[64,6144]{1,0:T(8,128)(2,1)S(1)} %collective-permute-done.rows_ref, bf16[16,3584]{1,0:T(8,128)(2,1)S(1)} %collective-permute-done.9.refs_0_, bf16[16,3456]{1,0:T(8,128)(2,1)S(1)} %collective-permute-done.14.refs_1_), custom_call_target="tpu_custom_call" | custom-call | tf_op jit(solution)/shard_map/combine/pallas_call | solution.py:310
  (19 shorter events, 0.5 us)
Async XLA Ops:
  1.5 19.1 %collective-permute-start.1 = (bf16[16,6912]{1,0:T(8,128)(2,1)S(1)}, bf16[16,6912]{1,0:T(8,128)(2,1)S(1)}, u32[]{:S(2)}, u32[]{:S(2)}) collective-permute-start(bf16[16,6912]{1,0:T(8,128)(2,1)S(1)} %get-tuple-element.23.after_ref.refs_0_), channel_id=1, source_target_pairs={{0,2},{1,3},{2,4},{3,5},{4,6},{5,7},{6,0},{7,1},{8,10},{9,11},{10,... | collective-permute-start | bytes 663560 | tf_op jit(solution)/shard_map/ppermute | solution.py:207
  4.5 17.1 %collective-permute-start.2 = (bf16[16,6912]{1,0:T(8,128)(2,1)S(1)}, bf16[16,6912]{1,0:T(8,128)(2,1)S(1)}, u32[]{:S(2)}, u32[]{:S(2)}) collective-permute-start(bf16[16,6912]{1,0:T(8,128)(2,1)S(1)} %get-tuple-element.23.after_ref.refs_0_), channel_id=1, source_target_pairs={{0,4},{1,5},{2,6},{3,7},{4,0},{5,1},{6,2},{7,3},{8,12},{9,13},{10,... | collective-permute-start | bytes 663560 | tf_op jit(solution)/shard_map/ppermute | solution.py:207
  7.1 14.5 %collective-permute-start.3 = (bf16[16,6912]{1,0:T(8,128)(2,1)S(1)}, bf16[16,6912]{1,0:T(8,128)(2,1)S(1)}, u32[]{:S(2)}, u32[]{:S(2)}) collective-permute-start(bf16[16,6912]{1,0:T(8,128)(2,1)S(1)} %get-tuple-element.23.after_ref.refs_0_), channel_id=1, source_target_pairs={{0,6},{1,7},{2,0},{3,1},{4,2},{5,3},{6,4},{7,5},{8,14},{9,15},{10,... | collective-permute-start | bytes 663560 | tf_op jit(solution)/shard_map/ppermute | solution.py:207
  8.5 13.3 %copy-start = (bf16[1,64,6144]{2,1,0:T(8,128)(2,1)S(1)}, bf16[1,64,6144]{2,1,0:T(8,128)(2,1)}, u32[]{:S(2)}) copy-start(bf16[1,64,6144]{2,1,0:T(8,128)(2,1)} %param.6) | copy-start | bytes 2359300
  21.7 2.5 %collective-permute-start.4 = (bf16[64,6912]{1,0:T(8,128)(2,1)S(1)}, bf16[64,6912]{1,0:T(8,128)(2,1)S(1)}, u32[]{:S(2)}, u32[]{:S(2)}) collective-permute-start(bf16[64,6912]{1,0:T(8,128)(2,1)S(1)} %stack.1.refs_0_), channel_id=1, source_target_pairs={{0,1},{1,0},{2,3},{3,2},{4,5},{5,4},{6,7},{7,6},{8,9},{9,8},{10,11... | collective-permute-start | bytes 2654216 | tf_op jit(solution)/shard_map/ppermute | solution.py:210
  21.8 37.7 %collective-permute-start = (bf16[64,6144]{1,0:T(8,128)(2,1)S(1)}, bf16[64,6144]{1,0:T(8,128)(2,1)S(1)}, u32[]{:S(2)}, u32[]{:S(2)}) collective-permute-start(bf16[64,6144]{1,0:T(8,128)(2,1)S(1)} %bitcast.16), channel_id=1, source_target_pairs={{0,8},{8,16},{16,24},{24,0},{1,9},{9,17},{17,25},{25,1},{2,10},{10... | collective-permute-start | bytes 2359304 | tf_op jit(solution)/shard_map/ppermute | solution.py:213
  29.5 1.9 %collective-permute-start.5 = (bf16[64,3456]{1,0:T(8,128)(2,1)S(1)}, bf16[64,3456]{1,0:T(8,128)(2,1)S(1)}, u32[]{:S(2)}, u32[]{:S(2)}) collective-permute-start(bf16[64,3456]{1,0:T(8,128)(2,1)S(1)} %get-tuple-element.29), channel_id=1, source_target_pairs={{0,1},{1,0},{2,3},{3,2},{4,5},{5,4},{6,7},{7,6},{8,9},{9,8},{10,11... | collective-permute-start | bytes 1327112 | tf_op jit(solution)/shard_map/ppermute | solution.py:210
  30.9 7.5 %collective-permute-start.10 = (bf16[64,3456]{1,0:T(8,128)(2,1)S(1)}, bf16[64,3456]{1,0:T(8,128)(2,1)S(1)}, u32[]{:S(2)}, u32[]{:S(2)}) collective-permute-start(bf16[64,3456]{1,0:T(8,128)(2,1)S(1)} %get-tuple-element.36), channel_id=1, source_target_pairs={{0,1},{1,0},{2,3},{3,2},{4,5},{5,4},{6,7},{7,6},{8,9},{9,8},{10,11... | collective-permute-start | bytes 1327112 | tf_op jit(solution)/shard_map/ppermute | solution.py:210
  31.5 10.7 %collective-permute-start.6 = (bf16[16,3456]{1,0:T(8,128)(2,1)S(1)}, bf16[16,3456]{1,0:T(8,128)(2,1)S(1)}, u32[]{:S(2)}, u32[]{:S(2)}) collective-permute-start(bf16[16,3456]{1,0:T(8,128)(2,1)S(1)} %get-tuple-element.31), channel_id=1, source_target_pairs={{0,6},{1,7},{2,0},{3,1},{4,2},{5,3},{6,4},{7,5},{8,14},{9,15},{10,... | collective-permute-start | bytes 331784 | tf_op jit(solution)/shard_map/ppermute | solution.py:207
  37.7 12.2 %collective-permute-start.7 = (bf16[16,3456]{1,0:T(8,128)(2,1)S(1)}, bf16[16,3456]{1,0:T(8,128)(2,1)S(1)}, u32[]{:S(2)}, u32[]{:S(2)}) collective-permute-start(bf16[16,3456]{1,0:T(8,128)(2,1)S(1)} %get-tuple-element.32), channel_id=1, source_target_pairs={{0,4},{1,5},{2,6},{3,7},{4,0},{5,1},{6,2},{7,3},{8,12},{9,13},{10,... | collective-permute-start | bytes 331784 | tf_op jit(solution)/shard_map/ppermute | solution.py:207
  38.2 11.8 %collective-permute-start.8 = (bf16[16,3456]{1,0:T(8,128)(2,1)S(1)}, bf16[16,3456]{1,0:T(8,128)(2,1)S(1)}, u32[]{:S(2)}, u32[]{:S(2)}) collective-permute-start(bf16[16,3456]{1,0:T(8,128)(2,1)S(1)} %get-tuple-element.33), channel_id=1, source_target_pairs={{0,2},{1,3},{2,4},{3,5},{4,6},{5,7},{6,0},{7,1},{8,10},{9,11},{10,... | collective-permute-start | bytes 331784 | tf_op jit(solution)/shard_map/ppermute | solution.py:207
  38.5 13.1 %collective-permute-start.11 = (bf16[16,3456]{1,0:T(8,128)(2,1)S(1)}, bf16[16,3456]{1,0:T(8,128)(2,1)S(1)}, u32[]{:S(2)}, u32[]{:S(2)}) collective-permute-start(bf16[16,3456]{1,0:T(8,128)(2,1)S(1)} %get-tuple-element.38), channel_id=1, source_target_pairs={{0,6},{1,7},{2,0},{3,1},{4,2},{5,3},{6,4},{7,5},{8,14},{9,15},{10,... | collective-permute-start | bytes 331784 | tf_op jit(solution)/shard_map/ppermute | solution.py:207
  42.2 15.7 %collective-permute-start.12 = (bf16[16,3456]{1,0:T(8,128)(2,1)S(1)}, bf16[16,3456]{1,0:T(8,128)(2,1)S(1)}, u32[]{:S(2)}, u32[]{:S(2)}) collective-permute-start(bf16[16,3456]{1,0:T(8,128)(2,1)S(1)} %get-tuple-element.39), channel_id=1, source_target_pairs={{0,4},{1,5},{2,6},{3,7},{4,0},{5,1},{6,2},{7,3},{8,12},{9,13},{10,... | collective-permute-start | bytes 331784 | tf_op jit(solution)/shard_map/ppermute | solution.py:207
  49.9 7.9 %collective-permute-start.13 = (bf16[16,3456]{1,0:T(8,128)(2,1)S(1)}, bf16[16,3456]{1,0:T(8,128)(2,1)S(1)}, u32[]{:S(2)}, u32[]{:S(2)}) collective-permute-start(bf16[16,3456]{1,0:T(8,128)(2,1)S(1)} %get-tuple-element.40), channel_id=1, source_target_pairs={{0,2},{1,3},{2,4},{3,5},{4,6},{5,7},{6,0},{7,1},{8,10},{9,11},{10,... | collective-permute-start | bytes 331784 | tf_op jit(solution)/shard_map/ppermute | solution.py:207
  50.0 13.6 %collective-permute-start.9 = (bf16[16,3584]{1,0:T(8,128)(2,1)S(1)}, bf16[16,3584]{1,0:T(8,128)(2,1)S(1)}, u32[]{:S(2)}, u32[]{:S(2)}) collective-permute-start(bf16[16,3584]{1,0:T(8,128)(2,1)S(1)} %sum_chips.2), channel_id=1, source_target_pairs={{0,8},{8,16},{16,24},{24,0},{1,9},{9,17},{17,25},{25,1},{2,10},{10... | collective-permute-start | bytes 344072 | tf_op jit(solution)/shard_map/ppermute | solution.py:213
  57.9 5.7 %collective-permute-start.14 = (bf16[16,3456]{1,0:T(8,128)(2,1)S(1)}, bf16[16,3456]{1,0:T(8,128)(2,1)S(1)}, u32[]{:S(2)}, u32[]{:S(2)}) collective-permute-start(bf16[16,3456]{1,0:T(8,128)(2,1)S(1)} %sum_chips.3), channel_id=1, source_target_pairs={{0,8},{8,16},{16,24},{24,0},{1,9},{9,17},{17,25},{25,1},{2,10},{10... | collective-permute-start | bytes 331784 | tf_op jit(solution)/shard_map/ppermute | solution.py:213

commit v3 on v2

--- a/solution.py
+++ b/solution.py
@@ -8,7 +8,7 @@
 CAP = 18
 MAIN = 16
 SLABS = 8
-CHUNKS = 2
+CHUNKS = (3, 3)
 VMEM_LIMIT = 8 * 1024 * 1024
 
 
@@ -26,6 +26,12 @@
 
 def in_vmem(value):
     return pltpu.with_memory_space_constraint(value, pltpu.VMEM)
+
+
+def spans(model):
+    step = model // sum(CHUNKS)
+    starts = [sum(CHUNKS[:c]) * step for c in range(len(CHUNKS))]
+    return [(start, size * step) for start, size in zip(starts, CHUNKS)]
 
 
 def whole(count):
@@ -106,13 +112,14 @@
     return (q == pair * SLABS + slab).astype(jnp.bfloat16)
 
 
-def gather_rows(blocks, mine_ref, other_ref, x_ref):
+def gather_rows(blocks, block_refs, x_ref):
     width = x_ref.shape[1]
     slab = width // SLABS
-    half = blocks // 2 * MAIN
-    x_ref[:half, :] = mine_ref[:, :width]
-    x_ref[half : 2 * half, :] = other_ref[:, :width]
-    rest = jnp.concatenate([mine_ref[:, width:], other_ref[:, width:]], axis=0)
+    row = 0
+    for ref in block_refs:
+        x_ref[row : row + ref.shape[0], :] = ref[:, :width]
+        row += ref.shape[0]
+    rest = jnp.concatenate([ref[:, width:] for ref in block_refs], axis=0)
     rest = jnp.dot(regroup(blocks, False), rest, preferred_element_type=jnp.float32).astype(jnp.bfloat16)
     for k in range(SLABS):
         x_ref[blocks * MAIN :, k * slab : (k + 1) * slab] = rest[k * 2 * blocks : (k + 1) * 2 * blocks]
@@ -124,8 +131,9 @@
         out_ref[b * MAIN : (b + 1) * MAIN, :] = ref[...]
 
 
-def hidden_kernel(blocks, mine_ref, other_ref, w_gate_ref, w_up_ref, hidden_ref, x_ref):
-    gather_rows(blocks, mine_ref, other_ref, x_ref)
+def hidden_kernel(blocks, w_gate_ref, w_up_ref, *refs):
+    block_refs, (hidden_ref, x_ref) = refs[:-2], refs[-2:]
+    gather_rows(blocks, block_refs, x_ref)
     gate = jnp.dot(x_ref[...], w_gate_ref[...], preferred_element_type=jnp.float32)
     upper = jnp.dot(x_ref[...], w_up_ref[...], preferred_element_type=jnp.float32)
     hidden_ref[...] = (gate / (1.0 + jnp.exp(-gate)) * upper).astype(jnp.bfloat16)
@@ -133,9 +141,9 @@
 
 def down_kernel(blocks, chunk, hidden_ref, w_down_ref, own_ref, other_ref):
     half = blocks // 2 * MAIN
-    width = w_down_ref.shape[1] // CHUNKS
+    start, width = spans(w_down_ref.shape[1])[chunk]
     slab = width // SLABS
-    part = slice(chunk * width, (chunk + 1) * width)
+    part = slice(start, start + width)
     got = jnp.dot(hidden_ref[...], w_down_ref[:, part], preferred_element_type=jnp.float32)
     main = blocks * MAIN
     own_ref[:, :width] = got[:half].astype(own_ref.dtype)
@@ -164,16 +172,12 @@
         out_ref[:, width:] = refs[parts][...]
 
 
-def final_kernel(rows_ref, *refs):
-    out_ref = refs[-1]
-    count = rows_ref.shape[0]
-    width = rows_ref.shape[1] // CHUNKS
-    slab = width // SLABS
-    wide = width + slab
-    token = lax.broadcasted_iota(jnp.int32, (count, MAIN), 0)
-    column = lax.broadcasted_iota(jnp.int32, (count, MAIN), 1)
+def place_kernel(received_ref, place_ref):
+    token = lax.broadcasted_iota(jnp.int32, (place_ref.shape[0], MAIN), 0)
+    column = lax.broadcasted_iota(jnp.int32, (place_ref.shape[0], MAIN), 1)
     unfold = (token % MAIN == column).astype(jnp.bfloat16)
-    info = jnp.dot(unfold, refs[0][:, wide:], preferred_element_type=jnp.float32)
+    wide = received_ref.shape[1] - 128
+    info = jnp.dot(unfold, received_ref[:, wide:], preferred_element_type=jnp.float32)
     token = lax.broadcasted_iota(jnp.int32, info.shape, 0)
     lane = lax.broadcasted_iota(jnp.int32, info.shape, 1)
     info = jnp.where(lane // 8 == token // MAIN, info, 0.0)
@@ -181,14 +185,28 @@
     weight = jnp.sum(jnp.where(lane % 8 == 0, 0.0, info), axis=1, keepdims=True)
     wanted = jnp.where(lane < MAIN, lane, MAIN + (lane - MAIN) // SLABS)
     placed = (slot == wanted.astype(jnp.float32)) & (lane < 2 * MAIN)
+    place_ref[...] = jnp.where(placed, weight, 0.0)
+
+
+def combine_kernel(chunks, *refs):
+    out_ref = refs[-1]
+    rows_ref, place_ref = refs[:2]
+    place = place_ref[...]
+    lane = lax.broadcasted_iota(jnp.int32, place.shape, 1)
+    weight = jnp.max(place, axis=1, keepdims=True)
+    model = rows_ref.shape[1]
     for k in range(SLABS):
-        keep = placed & ((lane < MAIN) | (lane % SLABS == k))
+        keep = (place > 0.0) & ((lane < MAIN) | (lane % SLABS == k))
         mark = jnp.where(keep, 1.0, 0.0).astype(jnp.bfloat16)[:, : 2 * MAIN]
-        for c in range(CHUNKS):
-            ref = refs[c]
-            values = jnp.concatenate([ref[:, k * slab : (k + 1) * slab], ref[:, width:wide]], axis=0)
+        for i, c in enumerate(chunks):
+            ref = refs[2 + i]
+            start, width = spans(model)[c]
+            slab = width // SLABS
+            values = jnp.concatenate(
+                [ref[:, k * slab : (k + 1) * slab], ref[:, width : width + slab]], axis=0
+            )
             moved = jnp.dot(mark, values, preferred_element_type=jnp.float32)
-            span = slice(c * width + k * slab, c * width + (k + 1) * slab)
+            span = slice(start + k * slab, start + (k + 1) * slab)
             out_ref[:, span] = (rows_ref[:, span].astype(jnp.float32) + weight * moved).astype(jnp.bfloat16)
 
 
@@ -199,8 +217,7 @@
     shards = lax.axis_size("shard")
     sections = lax.axis_size("section")
     chips = shards // 2
-    width = model // CHUNKS
-    wide = width + width // SLABS
+    wides = [width + width // SLABS for start, width in spans(model)]
     total_rows = shards * CAP
 
     def along(value, steps):
@@ -251,27 +268,30 @@
     )(packed, in_hbm(w_gate[0]), in_hbm(w_up[0]), in_hbm(w_down[0]))
     rows_in = onward(rows[0])
 
-    held = pl.pallas_call(
-        lambda *refs: stack_kernel(chips, *refs),
-        out_shape=jax.ShapeDtypeStruct((chips * MAIN, model + model // SLABS), bf16),
-        in_specs=whole(chips + 1),
-        out_specs=pl.BlockSpec(memory_space=pltpu.VMEM),
-        compiler_params=params(),
-        name="stack",
-    )(*mine, done)
+    def stack(*blocks):
+        return pl.pallas_call(
+            lambda *refs: stack_kernel(len(blocks), *refs),
+            out_shape=jax.ShapeDtypeStruct((len(blocks) * MAIN, model + model // SLABS), bf16),
+            in_specs=whole(len(blocks)) + [pl.BlockSpec(memory_space=pl.ANY)],
+            out_specs=pl.BlockSpec(memory_space=pltpu.VMEM),
+            compiler_params=params(),
+            name="stack",
+        )(*blocks, done)
+
+    held = [stack(*mine[: chips // 2]), stack(*mine[chips // 2 :])]
     hidden = pl.pallas_call(
         lambda *refs: hidden_kernel(shards, *refs),
         out_shape=jax.ShapeDtypeStruct((total_rows, hidden_units), bf16),
-        in_specs=whole(4),
+        in_specs=whole(6),
         out_specs=pl.BlockSpec(memory_space=pltpu.VMEM),
         scratch_shapes=[pltpu.VMEM((total_rows, model), bf16)],
         compiler_params=params(),
         cost_estimate=cost(4 * total_rows * model * hidden_units, 4 * model * hidden_units),
         name="hidden",
-    )(held, swap(held), gate_w, up_w)
+    )(gate_w, up_w, *held, *[swap(part) for part in held])
 
     halves = []
-    for c in range(CHUNKS):
+    for c, wide in enumerate(wides):
         own, other = pl.pallas_call(
             lambda *refs, c=c: down_kernel(shards, c, *refs),
             out_shape=[
@@ -281,12 +301,11 @@
             in_specs=whole(2),
             out_specs=whole(2),
             compiler_params=params(),
-            cost_estimate=cost(2 * total_rows * width * hidden_units, 2 * width * hidden_units),
             name="down",
         )(hidden, down_w)
         halves.append((own, swap(other)))
     arrived = []
-    for c, (own, other) in enumerate(halves):
+    for c, (wide, (own, other)) in enumerate(zip(wides, halves)):
         kept, *leaving = pl.pallas_call(
             add_kernel,
             out_shape=[jax.ShapeDtypeStruct((MAIN, wide), f32)]
@@ -307,14 +326,22 @@
             name="sum_chips",
         )(kept, *coming, *extra)
         arrived.append(onward(summed))
+    place = pl.pallas_call(
+        place_kernel,
+        out_shape=jax.ShapeDtypeStruct((count, 128), f32),
+        in_specs=whole(1),
+        out_specs=pl.BlockSpec(memory_space=pltpu.VMEM),
+        compiler_params=params(),
+        name="place",
+    )(arrived[0])
     out = pl.pallas_call(
-        final_kernel,
+        lambda *refs: combine_kernel(range(len(CHUNKS)), *refs),
         out_shape=jax.ShapeDtypeStruct((count, model), bf16),
-        in_specs=whole(1 + CHUNKS),
+        in_specs=whole(2 + len(CHUNKS)),
         out_specs=pl.BlockSpec(memory_space=pltpu.VMEM),
         compiler_params=params(),
         name="combine",
-    )(rows_in, *arrived)
+    )(rows_in, place, *arrived)
     return out[None]
 
 

time: 65.2 us -> 64.3 us (0.986)
  starting transfers between devices: 26.2 us -> 23.9 us
  waiting for transfers between devices: 16.9 us -> 18.2 us
    ppermute x9, starting transfers between devices: 20.9 us -> 17.8 us  [along(): lax.ppermute(value, 'shard', [(i, (i + 2 * steps) % shards) for i in rang...]
    ppermute x9, waiting for transfers between devices: 11.9 us -> 14.3 us  [along(): lax.ppermute(value, 'shard', [(i, (i + 2 * steps) % shards) for i in rang...]
    ppermute x3 -> x4, waiting for transfers between devices: 0.86 us -> 0.01 us  [swap(): return lax.ppermute(value, 'shard', [(i, i ^ 1) for i in range(shards)])]
    ppermute x3, starting transfers between devices: 4.63 us -> 5.31 us  [onward(): lax.ppermute(value, 'section', [(s, (s + 1) % sections) for s in range(se...]
    pallas_call x2 -> x4, Pallas kernels: 1.48 us -> 1.5 us  [the longest x1 1.23 us: on_device(): pl.pallas_call(lambda *refs: combine_kernel(range(len(CHUNKS)), *refs), o...]
  transfers between devices with their start and end apart: 15 -> 16, of which waited for: 5 -> 4; matrix products, arithmetic and copies ran while one was open for 0% -> 0% of each run, Pallas kernels for 29% -> 30%
where the time goes in v3:
time: 64.3 us; the launch traced here: 64.1 us
  starting transfers between devices  23.9 us (37%)
  Pallas kernels  21.9 us (34%)
  waiting for transfers between devices  18.2 us (28%)
    ppermute x9, starting transfers between devices, along(): lax.ppermute(value, 'shard', [(i, (i + 2 * steps) % shards) for i in rang...  17.8 us
    ppermute x9, waiting for transfers between devices, along(): lax.ppermute(value, 'shard', [(i, (i + 2 * steps) % shards) for i in rang...  14.3 us
    pallas_call x1, Pallas kernels, on_device(): pl.pallas_call(fetch_kernel, out_shape=[pltpu.VMEM((model, hidden_units),...  12.1 us
    ppermute x3, starting transfers between devices, onward(): lax.ppermute(value, 'section', [(s, (s + 1) % sections) for s in range(se...  5.31 us
    pallas_call x1, Pallas kernels, on_device(): pl.pallas_call(lambda *refs: hidden_kernel(shards, *refs), out_shape=jax....  4.02 us
    ppermute x3, waiting for transfers between devices, onward(): lax.ppermute(value, 'section', [(s, (s + 1) % sections) for s in range(se...  3.92 us
    pallas_call x2, Pallas kernels, on_device(): pl.pallas_call(lambda *refs, c=c: down_kernel(shards, c, *refs), out_shap...  2.53 us
    pallas_call x1, Pallas kernels, on_device(): pl.pallas_call(pack_kernel, out_shape=[jax.ShapeDtypeStruct((MAIN, 128),...  1.45 us
  transfers between devices with their start and end apart: 16, of which 4 were waited for; matrix products, arithmetic and copies ran while one was open for 0% of the time, Pallas kernels for 30%

profile of v3, /device:TPU:0, one launch (start us, length us, event | category | flops | bytes accessed | tf_op | source)
XLA Modules:
  0.0 64.1 jit_solution(3614909260458657788)
XLA Ops:
  0.0 1.5 %pack.1 = (bf16[16,128]{1,0:T(8,128)(2,1)S(1)}, bf16[16,6912]{1,0:T(8,128)(2,1)S(1)}) custom-call(s32[1]{0:T(128)} %bitcast.1.section_ref, s32[2,64]{1,0:T(2,128)} %bitcast.17, f32[2,64]{1,0:T(2,128)} %bitcast.18, bf16[64,6144]{1,0:T(8,128)(2,1)} %bitcast.15), custom_call_target="tpu_custom_call" | custom-call | bytes 1572864 | tf_op jit(solution)/shard_map/pack/pallas_call | solution.py:233
  1.5 4.1 %collective-permute-start.2 = (bf16[16,6912]{1,0:T(8,128)(2,1)S(1)}, bf16[16,6912]{1,0:T(8,128)(2,1)S(1)}, u32[]{:S(2)}, u32[]{:S(2)}) collective-permute-start(bf16[16,6912]{1,0:T(8,128)(2,1)S(1)} %get-tuple-element.23.after_ref.refs_0_), channel_id=1, source_target_pairs={{0,4},{1,5},{2,6},{3,7},{4,0},{5,1},{6,2},{7,3},{8,12},{9,13},{10,... | collective-permute-start | bytes 663560 | tf_op jit(solution)/shard_map/ppermute | solution.py:224
  5.6 1.3 %collective-permute-start.3 = (bf16[16,6912]{1,0:T(8,128)(2,1)S(1)}, bf16[16,6912]{1,0:T(8,128)(2,1)S(1)}, u32[]{:S(2)}, u32[]{:S(2)}) collective-permute-start(bf16[16,6912]{1,0:T(8,128)(2,1)S(1)} %get-tuple-element.23.after_ref.refs_0_), channel_id=1, source_target_pairs={{0,6},{1,7},{2,0},{3,1},{4,2},{5,3},{6,4},{7,5},{8,14},{9,15},{10,... | collective-permute-start | bytes 663560 | tf_op jit(solution)/shard_map/ppermute | solution.py:224
  6.9 0.7 %collective-permute-start.1 = (bf16[16,6912]{1,0:T(8,128)(2,1)S(1)}, bf16[16,6912]{1,0:T(8,128)(2,1)S(1)}, u32[]{:S(2)}, u32[]{:S(2)}) collective-permute-start(bf16[16,6912]{1,0:T(8,128)(2,1)S(1)} %get-tuple-element.23.after_ref.refs_0_), channel_id=1, source_target_pairs={{0,2},{1,3},{2,4},{3,5},{4,6},{5,7},{6,0},{7,1},{8,10},{9,11},{10,... | collective-permute-start | bytes 663560 | tf_op jit(solution)/shard_map/ppermute | solution.py:224
  7.6 12.1 %fetch.1 = (bf16[6144,1024]{1,0:T(8,128)(2,1)S(1)}, bf16[6144,1024]{1,0:T(8,128)(2,1)S(1)}, bf16[1024,6144]{1,0:T(8,128)(2,1)S(1)}, f32[8,128]{1,0:T(8,128)S(1)}) custom-call(bf16[16,6912]{1,0:T(8,128)(2,1)S(1)} %get-tuple-element.23.after_ref.refs_0_, bf16[6144,1024]{1,0:T(8,128)(2,1)} %bitcast.12, bf16[6144,1024]{1,0:T(8,128)(2,1)} %bitcast.13, ...), custom_call_target="tpu_custom_call" | custom-call | bytes 75497472 | tf_op jit(solution)/shard_map/fetch/pallas_call | solution.py:254
  19.8 1.9 %collective-permute-done.1.refs_1_ = bf16[16,6912]{1,0:T(8,128)(2,1)S(1)} collective-permute-done((bf16[16,6912]{1,0:T(8,128)(2,1)S(1)}, bf16[16,6912]{1,0:T(8,128)(2,1)S(1)}, u32[]{:S(2)}, u32[]{:S(2)}) %collective-permute-start.1) | collective-permute-done | bytes 221216 | tf_op jit(solution)/shard_map/ppermute | solution.py:224
  21.8 2.1 %collective-permute-start = (bf16[64,6144]{1,0:T(8,128)(2,1)S(1)}, bf16[64,6144]{1,0:T(8,128)(2,1)S(1)}, u32[]{:S(2)}, u32[]{:S(2)}) collective-permute-start(bf16[64,6144]{1,0:T(8,128)(2,1)S(1)} %bitcast.16), channel_id=1, source_target_pairs={{0,8},{8,16},{16,24},{24,0},{1,9},{9,17},{17,25},{25,1},{2,10},{10... | collective-permute-start | bytes 2359304 | tf_op jit(solution)/shard_map/ppermute | solution.py:230
  23.9 4.0 %hidden.1.refs_0_ = bf16[144,1024]{1,0:T(8,128)(2,1)S(1)} custom-call(bf16[6144,1024]{1,0:T(8,128)(2,1)S(1)} %get-tuple-element.24.refs_0_, bf16[6144,1024]{1,0:T(8,128)(2,1)S(1)} %get-tuple-element.25.refs_1_, bf16[32,6912]{1,0:T(8,128)(2,1)S(1)} %stack.2.refs_2_, bf16[32,6912]{1,0:T(8,128)(2,1)S(1)} %stack.3.refs_3_, ...), custom_call_target="tpu_custom_call" | custom-call | flops 3623878656 | bytes 25165824 | tf_op jit(solution)/shard_map/hidden/pallas_call | solution.py:282
  27.9 1.3 %down.2 = (f32[64,3456]{1,0:T(8,128)S(1)}, bf16[64,3456]{1,0:T(8,128)(2,1)S(1)}) custom-call(bf16[144,1024]{1,0:T(8,128)(2,1)S(1)} %hidden.1.refs_0_, bf16[1024,6144]{1,0:T(8,128)(2,1)S(1)} %get-tuple-element.27.refs_1_), custom_call_target="tpu_custom_call" | custom-call | tf_op jit(solution)/shard_map/down/pallas_call | solution.py:295
  29.3 1.3 %down.3 = (f32[64,3456]{1,0:T(8,128)S(1)}, bf16[64,3456]{1,0:T(8,128)(2,1)S(1)}) custom-call(bf16[144,1024]{1,0:T(8,128)(2,1)S(1)} %hidden.1.refs_0_, bf16[1024,6144]{1,0:T(8,128)(2,1)S(1)} %get-tuple-element.27.refs_1_), custom_call_target="tpu_custom_call" | custom-call | tf_op jit(solution)/shard_map/down/pallas_call | solution.py:295
  30.6 0.6 collective-permute-start.11
  31.2 2.8 %collective-permute-start.7 = (bf16[16,3456]{1,0:T(8,128)(2,1)S(1)}, bf16[16,3456]{1,0:T(8,128)(2,1)S(1)}, u32[]{:S(2)}, u32[]{:S(2)}) collective-permute-start(bf16[16,3456]{1,0:T(8,128)(2,1)S(1)} %get-tuple-element.31), channel_id=1, source_target_pairs={{0,6},{1,7},{2,0},{3,1},{4,2},{5,3},{6,4},{7,5},{8,14},{9,15},{10,... | collective-permute-start | bytes 331784 | tf_op jit(solution)/shard_map/ppermute | solution.py:224
  34.0 3.2 %collective-permute-start.8 = (bf16[16,3456]{1,0:T(8,128)(2,1)S(1)}, bf16[16,3456]{1,0:T(8,128)(2,1)S(1)}, u32[]{:S(2)}, u32[]{:S(2)}) collective-permute-start(bf16[16,3456]{1,0:T(8,128)(2,1)S(1)} %get-tuple-element.32), channel_id=1, source_target_pairs={{0,4},{1,5},{2,6},{3,7},{4,0},{5,1},{6,2},{7,3},{8,12},{9,13},{10,... | collective-permute-start | bytes 331784 | tf_op jit(solution)/shard_map/ppermute | solution.py:224
  37.2 1.9 %collective-permute-start.9 = (bf16[16,3456]{1,0:T(8,128)(2,1)S(1)}, bf16[16,3456]{1,0:T(8,128)(2,1)S(1)}, u32[]{:S(2)}, u32[]{:S(2)}) collective-permute-start(bf16[16,3456]{1,0:T(8,128)(2,1)S(1)} %get-tuple-element.33), channel_id=1, source_target_pairs={{0,2},{1,3},{2,4},{3,5},{4,6},{5,7},{6,0},{7,1},{8,10},{9,11},{10,... | collective-permute-start | bytes 331784 | tf_op jit(solution)/shard_map/ppermute | solution.py:224
  39.2 0.1 add_cores.3
  39.3 1.9 %collective-permute-start.12 = (bf16[16,3456]{1,0:T(8,128)(2,1)S(1)}, bf16[16,3456]{1,0:T(8,128)(2,1)S(1)}, u32[]{:S(2)}, u32[]{:S(2)}) collective-permute-start(bf16[16,3456]{1,0:T(8,128)(2,1)S(1)} %get-tuple-element.38), channel_id=1, source_target_pairs={{0,6},{1,7},{2,0},{3,1},{4,2},{5,3},{6,4},{7,5},{8,14},{9,15},{10,... | collective-permute-start | bytes 331784 | tf_op jit(solution)/shard_map/ppermute | solution.py:224
  41.2 1.8 %collective-permute-start.13 = (bf16[16,3456]{1,0:T(8,128)(2,1)S(1)}, bf16[16,3456]{1,0:T(8,128)(2,1)S(1)}, u32[]{:S(2)}, u32[]{:S(2)}) collective-permute-start(bf16[16,3456]{1,0:T(8,128)(2,1)S(1)} %get-tuple-element.39), channel_id=1, source_target_pairs={{0,4},{1,5},{2,6},{3,7},{4,0},{5,1},{6,2},{7,3},{8,12},{9,13},{10,... | collective-permute-start | bytes 331784 | tf_op jit(solution)/shard_map/ppermute | solution.py:224
  43.0 5.2 %collective-permute-done.8.refs_2_ = bf16[16,3456]{1,0:T(8,128)(2,1)S(1)} collective-permute-done((bf16[16,3456]{1,0:T(8,128)(2,1)S(1)}, bf16[16,3456]{1,0:T(8,128)(2,1)S(1)}, u32[]{:S(2)}, u32[]{:S(2)}) %collective-permute-start.8) | collective-permute-done | bytes 110624 | tf_op jit(solution)/shard_map/ppermute | solution.py:224
  48.3 1.7 %collective-permute-start.10 = (bf16[16,3584]{1,0:T(8,128)(2,1)S(1)}, bf16[16,3584]{1,0:T(8,128)(2,1)S(1)}, u32[]{:S(2)}, u32[]{:S(2)}) collective-permute-start(bf16[16,3584]{1,0:T(8,128)(2,1)S(1)} %sum_chips.2), channel_id=1, source_target_pairs={{0,8},{8,16},{16,24},{24,0},{1,9},{9,17},{17,25},{25,1},{2,10},{10... | collective-permute-start | bytes 344072 | tf_op jit(solution)/shard_map/ppermute | solution.py:230
  50.0 7.1 %collective-permute-done.13.refs_2_ = bf16[16,3456]{1,0:T(8,128)(2,1)S(1)} collective-permute-done((bf16[16,3456]{1,0:T(8,128)(2,1)S(1)}, bf16[16,3456]{1,0:T(8,128)(2,1)S(1)}, u32[]{:S(2)}, u32[]{:S(2)}) %collective-permute-start.13) | collective-permute-done | bytes 110624 | tf_op jit(solution)/shard_map/ppermute | solution.py:224
  57.2 1.5 %collective-permute-start.15 = (bf16[16,3456]{1,0:T(8,128)(2,1)S(1)}, bf16[16,3456]{1,0:T(8,128)(2,1)S(1)}, u32[]{:S(2)}, u32[]{:S(2)}) collective-permute-start(bf16[16,3456]{1,0:T(8,128)(2,1)S(1)} %sum_chips.3), channel_id=1, source_target_pairs={{0,8},{8,16},{16,24},{24,0},{1,9},{9,17},{17,25},{25,1},{2,10},{10... | collective-permute-start | bytes 331784 | tf_op jit(solution)/shard_map/ppermute | solution.py:230
  58.7 0.2 place.1.refs_1_
  59.0 3.9 %collective-permute-done.15.refs_3_ = bf16[16,3456]{1,0:T(8,128)(2,1)S(1)} collective-permute-done((bf16[16,3456]{1,0:T(8,128)(2,1)S(1)}, bf16[16,3456]{1,0:T(8,128)(2,1)S(1)}, u32[]{:S(2)}, u32[]{:S(2)}) %collective-permute-start.15) | collective-permute-done | bytes 110624 | tf_op jit(solution)/shard_map/ppermute | solution.py:230
  62.9 1.2 %combine.1 = bf16[64,6144]{1,0:T(8,128)(2,1)} custom-call(bf16[64,6144]{1,0:T(8,128)(2,1)S(1)} %collective-permute-done.refs_0_, f32[64,128]{1,0:T(8,128)S(1)} %place.1.refs_1_, bf16[16,3584]{1,0:T(8,128)(2,1)S(1)} %collective-permute-done.10.received_ref.refs_2_, bf16[16,3456]{1,0:T(8,128)(2,1)S(1)} %collective-permute-done.15.refs_3_), custom_call_target="tpu_custom_call" | custom-call | tf_op jit(solution)/shard_map/combine/pallas_call | solution.py:337
  (23 shorter events, 0.5 us)
Async XLA Ops:
  1.5 18.2 %collective-permute-start.2 = (bf16[16,6912]{1,0:T(8,128)(2,1)S(1)}, bf16[16,6912]{1,0:T(8,128)(2,1)S(1)}, u32[]{:S(2)}, u32[]{:S(2)}) collective-permute-start(bf16[16,6912]{1,0:T(8,128)(2,1)S(1)} %get-tuple-element.23.after_ref.refs_0_), channel_id=1, source_target_pairs={{0,4},{1,5},{2,6},{3,7},{4,0},{5,1},{6,2},{7,3},{8,12},{9,13},{10,... | collective-permute-start | bytes 663560 | tf_op jit(solution)/shard_map/ppermute | solution.py:224
  5.6 14.1 %collective-permute-start.3 = (bf16[16,6912]{1,0:T(8,128)(2,1)S(1)}, bf16[16,6912]{1,0:T(8,128)(2,1)S(1)}, u32[]{:S(2)}, u32[]{:S(2)}) collective-permute-start(bf16[16,6912]{1,0:T(8,128)(2,1)S(1)} %get-tuple-element.23.after_ref.refs_0_), channel_id=1, source_target_pairs={{0,6},{1,7},{2,0},{3,1},{4,2},{5,3},{6,4},{7,5},{8,14},{9,15},{10,... | collective-permute-start | bytes 663560 | tf_op jit(solution)/shard_map/ppermute | solution.py:224
  6.9 14.8 %collective-permute-start.1 = (bf16[16,6912]{1,0:T(8,128)(2,1)S(1)}, bf16[16,6912]{1,0:T(8,128)(2,1)S(1)}, u32[]{:S(2)}, u32[]{:S(2)}) collective-permute-start(bf16[16,6912]{1,0:T(8,128)(2,1)S(1)} %get-tuple-element.23.after_ref.refs_0_), channel_id=1, source_target_pairs={{0,2},{1,3},{2,4},{3,5},{4,6},{5,7},{6,0},{7,1},{8,10},{9,11},{10,... | collective-permute-start | bytes 663560 | tf_op jit(solution)/shard_map/ppermute | solution.py:224
  7.6 14.2 %copy-start = (bf16[1,64,6144]{2,1,0:T(8,128)(2,1)S(1)}, bf16[1,64,6144]{2,1,0:T(8,128)(2,1)}, u32[]{:S(2)}) copy-start(bf16[1,64,6144]{2,1,0:T(8,128)(2,1)} %param.6) | copy-start | bytes 2359300
  19.7 4.2 %collective-permute-start.5 = (bf16[32,6912]{1,0:T(8,128)(2,1)S(1)}, bf16[32,6912]{1,0:T(8,128)(2,1)S(1)}, u32[]{:S(2)}, u32[]{:S(2)}) collective-permute-start(bf16[32,6912]{1,0:T(8,128)(2,1)S(1)} %stack.3.refs_3_), channel_id=1, source_target_pairs={{0,1},{1,0},{2,3},{3,2},{4,5},{5,4},{6,7},{7,6},{8,9},{9,8},{10,11... | collective-permute-start | bytes 1327112 | tf_op jit(solution)/shard_map/ppermute | solution.py:227
  21.7 2.2 %collective-permute-start.4 = (bf16[32,6912]{1,0:T(8,128)(2,1)S(1)}, bf16[32,6912]{1,0:T(8,128)(2,1)S(1)}, u32[]{:S(2)}, u32[]{:S(2)}) collective-permute-start(bf16[32,6912]{1,0:T(8,128)(2,1)S(1)} %stack.2.refs_2_), channel_id=1, source_target_pairs={{0,1},{1,0},{2,3},{3,2},{4,5},{5,4},{6,7},{7,6},{8,9},{9,8},{10,11... | collective-permute-start | bytes 1327112 | tf_op jit(solution)/shard_map/ppermute | solution.py:227
  21.8 37.2 %collective-permute-start = (bf16[64,6144]{1,0:T(8,128)(2,1)S(1)}, bf16[64,6144]{1,0:T(8,128)(2,1)S(1)}, u32[]{:S(2)}, u32[]{:S(2)}) collective-permute-start(bf16[64,6144]{1,0:T(8,128)(2,1)S(1)} %bitcast.16), channel_id=1, source_target_pairs={{0,8},{8,16},{16,24},{24,0},{1,9},{9,17},{17,25},{25,1},{2,10},{10... | collective-permute-start | bytes 2359304 | tf_op jit(solution)/shard_map/ppermute | solution.py:230
  29.2 1.9 %collective-permute-start.6 = (bf16[64,3456]{1,0:T(8,128)(2,1)S(1)}, bf16[64,3456]{1,0:T(8,128)(2,1)S(1)}, u32[]{:S(2)}, u32[]{:S(2)}) collective-permute-start(bf16[64,3456]{1,0:T(8,128)(2,1)S(1)} %get-tuple-element.29), channel_id=1, source_target_pairs={{0,1},{1,0},{2,3},{3,2},{4,5},{5,4},{6,7},{7,6},{8,9},{9,8},{10,11... | collective-permute-start | bytes 1327112 | tf_op jit(solution)/shard_map/ppermute | solution.py:227
  30.6 8.6 %collective-permute-start.11 = (bf16[64,3456]{1,0:T(8,128)(2,1)S(1)}, bf16[64,3456]{1,0:T(8,128)(2,1)S(1)}, u32[]{:S(2)}, u32[]{:S(2)}) collective-permute-start(bf16[64,3456]{1,0:T(8,128)(2,1)S(1)} %get-tuple-element.36), channel_id=1, source_target_pairs={{0,1},{1,0},{2,3},{3,2},{4,5},{5,4},{6,7},{7,6},{8,9},{9,8},{10,11... | collective-permute-start | bytes 1327112 | tf_op jit(solution)/shard_map/ppermute | solution.py:227
  31.2 10.0 %collective-permute-start.7 = (bf16[16,3456]{1,0:T(8,128)(2,1)S(1)}, bf16[16,3456]{1,0:T(8,128)(2,1)S(1)}, u32[]{:S(2)}, u32[]{:S(2)}) collective-permute-start(bf16[16,3456]{1,0:T(8,128)(2,1)S(1)} %get-tuple-element.31), channel_id=1, source_target_pairs={{0,6},{1,7},{2,0},{3,1},{4,2},{5,3},{6,4},{7,5},{8,14},{9,15},{10,... | collective-permute-start | bytes 331784 | tf_op jit(solution)/shard_map/ppermute | solution.py:224
  34.0 14.3 %collective-permute-start.8 = (bf16[16,3456]{1,0:T(8,128)(2,1)S(1)}, bf16[16,3456]{1,0:T(8,128)(2,1)S(1)}, u32[]{:S(2)}, u32[]{:S(2)}) collective-permute-start(bf16[16,3456]{1,0:T(8,128)(2,1)S(1)} %get-tuple-element.32), channel_id=1, source_target_pairs={{0,4},{1,5},{2,6},{3,7},{4,0},{5,1},{6,2},{7,3},{8,12},{9,13},{10,... | collective-permute-start | bytes 331784 | tf_op jit(solution)/shard_map/ppermute | solution.py:224
  37.2 11.1 %collective-permute-start.9 = (bf16[16,3456]{1,0:T(8,128)(2,1)S(1)}, bf16[16,3456]{1,0:T(8,128)(2,1)S(1)}, u32[]{:S(2)}, u32[]{:S(2)}) collective-permute-start(bf16[16,3456]{1,0:T(8,128)(2,1)S(1)} %get-tuple-element.33), channel_id=1, source_target_pairs={{0,2},{1,3},{2,4},{3,5},{4,6},{5,7},{6,0},{7,1},{8,10},{9,11},{10,... | collective-permute-start | bytes 331784 | tf_op jit(solution)/shard_map/ppermute | solution.py:224
  39.3 10.7 %collective-permute-start.12 = (bf16[16,3456]{1,0:T(8,128)(2,1)S(1)}, bf16[16,3456]{1,0:T(8,128)(2,1)S(1)}, u32[]{:S(2)}, u32[]{:S(2)}) collective-permute-start(bf16[16,3456]{1,0:T(8,128)(2,1)S(1)} %get-tuple-element.38), channel_id=1, source_target_pairs={{0,6},{1,7},{2,0},{3,1},{4,2},{5,3},{6,4},{7,5},{8,14},{9,15},{10,... | collective-permute-start | bytes 331784 | tf_op jit(solution)/shard_map/ppermute | solution.py:224
  41.2 15.9 %collective-permute-start.13 = (bf16[16,3456]{1,0:T(8,128)(2,1)S(1)}, bf16[16,3456]{1,0:T(8,128)(2,1)S(1)}, u32[]{:S(2)}, u32[]{:S(2)}) collective-permute-start(bf16[16,3456]{1,0:T(8,128)(2,1)S(1)} %get-tuple-element.39), channel_id=1, source_target_pairs={{0,4},{1,5},{2,6},{3,7},{4,0},{5,1},{6,2},{7,3},{8,12},{9,13},{10,... | collective-permute-start | bytes 331784 | tf_op jit(solution)/shard_map/ppermute | solution.py:224
  48.3 8.9 %collective-permute-start.14 = (bf16[16,3456]{1,0:T(8,128)(2,1)S(1)}, bf16[16,3456]{1,0:T(8,128)(2,1)S(1)}, u32[]{:S(2)}, u32[]{:S(2)}) collective-permute-start(bf16[16,3456]{1,0:T(8,128)(2,1)S(1)} %get-tuple-element.40), channel_id=1, source_target_pairs={{0,2},{1,3},{2,4},{3,5},{4,6},{5,7},{6,0},{7,1},{8,10},{9,11},{10,... | collective-permute-start | bytes 331784 | tf_op jit(solution)/shard_map/ppermute | solution.py:224
  48.3 10.4 %collective-permute-start.10 = (bf16[16,3584]{1,0:T(8,128)(2,1)S(1)}, bf16[16,3584]{1,0:T(8,128)(2,1)S(1)}, u32[]{:S(2)}, u32[]{:S(2)}) collective-permute-start(bf16[16,3584]{1,0:T(8,128)(2,1)S(1)} %sum_chips.2), channel_id=1, source_target_pairs={{0,8},{8,16},{16,24},{24,0},{1,9},{9,17},{17,25},{25,1},{2,10},{10... | collective-permute-start | bytes 344072 | tf_op jit(solution)/shard_map/ppermute | solution.py:230
  57.2 5.7 %collective-permute-start.15 = (bf16[16,3456]{1,0:T(8,128)(2,1)S(1)}, bf16[16,3456]{1,0:T(8,128)(2,1)S(1)}, u32[]{:S(2)}, u32[]{:S(2)}) collective-permute-start(bf16[16,3456]{1,0:T(8,128)(2,1)S(1)} %sum_chips.3), channel_id=1, source_target_pairs={{0,8},{8,16},{16,24},{24,0},{1,9},{9,17},{17,25},{25,1},{2,10},{10... | collective-permute-start | bytes 331784 | tf_op jit(solution)/shard_map/ppermute | solution.py:230

commit v4 on v3

--- a/solution.py
+++ b/solution.py
@@ -155,10 +155,13 @@
     other_ref[:, width:] = rest[half:].astype(jnp.bfloat16)
 
 
-def add_kernel(own_ref, other_ref, *out_refs):
+def add_kernel(own_ref, other_ref, info_ref, *out_refs):
     total = own_ref[...].astype(jnp.float32) + other_ref[...].astype(jnp.float32)
+    wide = total.shape[1]
     for m, ref in enumerate(out_refs):
-        ref[...] = total[m * MAIN : (m + 1) * MAIN].astype(ref.dtype)
+        ref[:, :wide] = total[m * MAIN : (m + 1) * MAIN].astype(ref.dtype)
+        if ref.shape[1] > wide:
+            ref[:, wide:] = info_ref[...]
 
 
 def sum_kernel(parts, *refs):
@@ -172,12 +175,14 @@
         out_ref[:, width:] = refs[parts][...]
 
 
-def place_kernel(received_ref, place_ref):
-    token = lax.broadcasted_iota(jnp.int32, (place_ref.shape[0], MAIN), 0)
-    column = lax.broadcasted_iota(jnp.int32, (place_ref.shape[0], MAIN), 1)
+def combine_kernel(rows_ref, *refs):
+    first_refs, last_refs, out_ref = refs[: len(CHUNKS) - 1], refs[len(CHUNKS) - 1 : -1], refs[-1]
+    count, model = rows_ref.shape
+    token = lax.broadcasted_iota(jnp.int32, (count, MAIN), 0)
+    column = lax.broadcasted_iota(jnp.int32, (count, MAIN), 1)
     unfold = (token % MAIN == column).astype(jnp.bfloat16)
-    wide = received_ref.shape[1] - 128
-    info = jnp.dot(unfold, received_ref[:, wide:], preferred_element_type=jnp.float32)
+    wide = last_refs[0].shape[1] - 128
+    info = jnp.dot(unfold, last_refs[0][:, wide:], preferred_element_type=jnp.float32)
     token = lax.broadcasted_iota(jnp.int32, info.shape, 0)
     lane = lax.broadcasted_iota(jnp.int32, info.shape, 1)
     info = jnp.where(lane // 8 == token // MAIN, info, 0.0)
@@ -185,22 +190,14 @@
     weight = jnp.sum(jnp.where(lane % 8 == 0, 0.0, info), axis=1, keepdims=True)
     wanted = jnp.where(lane < MAIN, lane, MAIN + (lane - MAIN) // SLABS)
     placed = (slot == wanted.astype(jnp.float32)) & (lane < 2 * MAIN)
-    place_ref[...] = jnp.where(placed, weight, 0.0)
-
-
-def combine_kernel(chunks, *refs):
-    out_ref = refs[-1]
-    rows_ref, place_ref = refs[:2]
-    place = place_ref[...]
-    lane = lax.broadcasted_iota(jnp.int32, place.shape, 1)
-    weight = jnp.max(place, axis=1, keepdims=True)
-    model = rows_ref.shape[1]
+    total = jnp.zeros((MAIN, wide), jnp.float32)
+    for ref in last_refs:
+        total = total + ref[:, :wide].astype(jnp.float32)
+    sums = [*first_refs, total.astype(jnp.bfloat16)]
     for k in range(SLABS):
-        keep = (place > 0.0) & ((lane < MAIN) | (lane % SLABS == k))
+        keep = placed & ((lane < MAIN) | (lane % SLABS == k))
         mark = jnp.where(keep, 1.0, 0.0).astype(jnp.bfloat16)[:, : 2 * MAIN]
-        for i, c in enumerate(chunks):
-            ref = refs[2 + i]
-            start, width = spans(model)[c]
+        for ref, (start, width) in zip(sums, spans(model)):
             slab = width // SLABS
             values = jnp.concatenate(
                 [ref[:, k * slab : (k + 1) * slab], ref[:, width : width + slab]], axis=0
@@ -219,6 +216,14 @@
     chips = shards // 2
     wides = [width + width // SLABS for start, width in spans(model)]
     total_rows = shards * CAP
+
+    def across(value, steps):
+        pairs = [
+            (s * shards + i, (s + 1) % sections * shards + (i + 2 * steps) % shards)
+            for s in range(sections)
+            for i in range(shards)
+        ]
+        return lax.ppermute(value, ("section", "shard"), pairs)
 
     def along(value, steps):
         return lax.ppermute(value, "shard", [(i, (i + 2 * steps) % shards) for i in range(shards)])
@@ -306,17 +311,21 @@
         halves.append((own, swap(other)))
     arrived = []
     for c, (wide, (own, other)) in enumerate(zip(wides, halves)):
+        last = c == len(CHUNKS) - 1
         kept, *leaving = pl.pallas_call(
             add_kernel,
-            out_shape=[jax.ShapeDtypeStruct((MAIN, wide), f32)]
-            + [jax.ShapeDtypeStruct((MAIN, wide), bf16)] * (chips - 1),
-            in_specs=whole(2),
+            out_shape=[jax.ShapeDtypeStruct((MAIN, wide + 128 * last), bf16 if last else f32)]
+            + [jax.ShapeDtypeStruct((MAIN, wide + 128 * last), bf16)] * (chips - 1),
+            in_specs=whole(3),
             out_specs=whole(chips),
             compiler_params=params(),
             name="add_cores",
-        )(own, other)
+        )(own, other, info)
+        if last:
+            arrived += [across(block, -m) for m, block in enumerate((kept, *leaving))]
+            break
         coming = [along(block, -m) for m, block in enumerate(leaving, 1)]
-        extra = [info] if c == 0 else []
+        extra = []
         summed = pl.pallas_call(
             lambda *refs: sum_kernel(chips, *refs),
             out_shape=jax.ShapeDtypeStruct((MAIN, wide + 128 * len(extra)), bf16),
@@ -326,22 +335,14 @@
             name="sum_chips",
         )(kept, *coming, *extra)
         arrived.append(onward(summed))
-    place = pl.pallas_call(
-        place_kernel,
-        out_shape=jax.ShapeDtypeStruct((count, 128), f32),
-        in_specs=whole(1),
-        out_specs=pl.BlockSpec(memory_space=pltpu.VMEM),
-        compiler_params=params(),
-        name="place",
-    )(arrived[0])
     out = pl.pallas_call(
-        lambda *refs: combine_kernel(range(len(CHUNKS)), *refs),
+        combine_kernel,
         out_shape=jax.ShapeDtypeStruct((count, model), bf16),
-        in_specs=whole(2 + len(CHUNKS)),
+        in_specs=whole(len(CHUNKS) + chips),
         out_specs=pl.BlockSpec(memory_space=pltpu.VMEM),
         compiler_params=params(),
         name="combine",
-    )(rows_in, place, *arrived)
+    )(rows_in, *arrived)
     return out[None]
 
 

time: 64.3 us -> 61.7 us (0.960)
  waiting for transfers between devices: 18.2 us -> 15.4 us
    ppermute x0 -> x4, waiting for transfers between devices: none -> 8.23 us  [across(): return lax.ppermute(value, ('section', 'shard'), pairs)]
    ppermute x9 -> x6, waiting for transfers between devices: 14.3 us -> 6.49 us  [along(): lax.ppermute(value, 'shard', [(i, (i + 2 * steps) % shards) for i in rang...]
    ppermute x0 -> x4, starting transfers between devices: none -> 5.67 us  [across(): return lax.ppermute(value, ('section', 'shard'), pairs)]
    ppermute x9 -> x6, starting transfers between devices: 17.8 us -> 14.1 us  [along(): lax.ppermute(value, 'shard', [(i, (i + 2 * steps) % shards) for i in rang...]
    ppermute x3 -> x2, waiting for transfers between devices: 3.92 us -> 0.71 us  [onward(): lax.ppermute(value, 'section', [(s, (s + 1) % sections) for s in range(se...]
    ppermute x3 -> x2, starting transfers between devices: 5.31 us -> 3.64 us  [onward(): lax.ppermute(value, 'section', [(s, (s + 1) % sections) for s in range(se...]
    pallas_call x4 -> x3, Pallas kernels: 1.62 us -> 1.61 us  [the longest x1 1.44 us: on_device(): pl.pallas_call(combine_kernel, out_shape=jax.ShapeDtypeStruct((count, mod...]
  transfers between devices with their start and end apart: 16 -> 16, of which waited for: 4 -> 4; matrix products, arithmetic and copies ran while one was open for 0% -> 0% of each run, Pallas kernels for 30% -> 31%
where the time goes in v4:
time: 61.7 us; the launch traced here: 61.5 us
  starting transfers between devices  24.2 us (39%)
  Pallas kernels  21.8 us (35%)
  waiting for transfers between devices  15.4 us (25%)
    ppermute x6, starting transfers between devices, along(): lax.ppermute(value, 'shard', [(i, (i + 2 * steps) % shards) for i in rang...  14.1 us
    pallas_call x1, Pallas kernels, on_device(): pl.pallas_call(fetch_kernel, out_shape=[pltpu.VMEM((model, hidden_units),...  12.1 us
    ppermute x4, waiting for transfers between devices, across(): return lax.ppermute(value, ('section', 'shard'), pairs)  8.23 us
    ppermute x6, waiting for transfers between devices, along(): lax.ppermute(value, 'shard', [(i, (i + 2 * steps) % shards) for i in rang...  6.49 us
    ppermute x4, starting transfers between devices, across(): return lax.ppermute(value, ('section', 'shard'), pairs)  5.67 us
    pallas_call x1, Pallas kernels, on_device(): pl.pallas_call(lambda *refs: hidden_kernel(shards, *refs), out_shape=jax....  4.02 us
    ppermute x2, starting transfers between devices, onward(): lax.ppermute(value, 'section', [(s, (s + 1) % sections) for s in range(se...  3.64 us
    pallas_call x2, Pallas kernels, on_device(): pl.pallas_call(lambda *refs, c=c: down_kernel(shards, c, *refs), out_shap...  2.53 us
  transfers between devices with their start and end apart: 16, of which 4 were waited for; matrix products, arithmetic and copies ran while one was open for 0% of the time, Pallas kernels for 31%

profile of v4, /device:TPU:0, one launch (start us, length us, event | category | flops | bytes accessed | tf_op | source)
XLA Modules:
  0.0 61.5 jit_solution(2553736374170996763)
XLA Ops:
  0.0 1.5 %pack.1 = (bf16[16,128]{1,0:T(8,128)(2,1)S(1)}, bf16[16,6912]{1,0:T(8,128)(2,1)S(1)}) custom-call(s32[1]{0:T(128)} %bitcast.1.section_ref, s32[2,64]{1,0:T(2,128)} %bitcast.17, f32[2,64]{1,0:T(2,128)} %bitcast.18, bf16[64,6144]{1,0:T(8,128)(2,1)} %bitcast.15), custom_call_target="tpu_custom_call" | custom-call | bytes 1572864 | tf_op jit(solution)/shard_map/pack/pallas_call | solution.py:238
  1.5 4.1 %collective-permute-start.2 = (bf16[16,6912]{1,0:T(8,128)(2,1)S(1)}, bf16[16,6912]{1,0:T(8,128)(2,1)S(1)}, u32[]{:S(2)}, u32[]{:S(2)}) collective-permute-start(bf16[16,6912]{1,0:T(8,128)(2,1)S(1)} %get-tuple-element.23.after_ref.refs_0_), channel_id=1, source_target_pairs={{0,4},{1,5},{2,6},{3,7},{4,0},{5,1},{6,2},{7,3},{8,12},{9,13},{10,... | collective-permute-start | bytes 663560 | tf_op jit(solution)/shard_map/ppermute | solution.py:229
  5.6 1.3 %collective-permute-start.3 = (bf16[16,6912]{1,0:T(8,128)(2,1)S(1)}, bf16[16,6912]{1,0:T(8,128)(2,1)S(1)}, u32[]{:S(2)}, u32[]{:S(2)}) collective-permute-start(bf16[16,6912]{1,0:T(8,128)(2,1)S(1)} %get-tuple-element.23.after_ref.refs_0_), channel_id=1, source_target_pairs={{0,6},{1,7},{2,0},{3,1},{4,2},{5,3},{6,4},{7,5},{8,14},{9,15},{10,... | collective-permute-start | bytes 663560 | tf_op jit(solution)/shard_map/ppermute | solution.py:229
  6.9 0.7 %collective-permute-start.1 = (bf16[16,6912]{1,0:T(8,128)(2,1)S(1)}, bf16[16,6912]{1,0:T(8,128)(2,1)S(1)}, u32[]{:S(2)}, u32[]{:S(2)}) collective-permute-start(bf16[16,6912]{1,0:T(8,128)(2,1)S(1)} %get-tuple-element.23.after_ref.refs_0_), channel_id=1, source_target_pairs={{0,2},{1,3},{2,4},{3,5},{4,6},{5,7},{6,0},{7,1},{8,10},{9,11},{10,... | collective-permute-start | bytes 663560 | tf_op jit(solution)/shard_map/ppermute | solution.py:229
  7.6 12.1 %fetch.1 = (bf16[6144,1024]{1,0:T(8,128)(2,1)S(1)}, bf16[6144,1024]{1,0:T(8,128)(2,1)S(1)}, bf16[1024,6144]{1,0:T(8,128)(2,1)S(1)}, f32[8,128]{1,0:T(8,128)S(1)}) custom-call(bf16[16,6912]{1,0:T(8,128)(2,1)S(1)} %get-tuple-element.23.after_ref.refs_0_, bf16[6144,1024]{1,0:T(8,128)(2,1)} %bitcast.12, bf16[6144,1024]{1,0:T(8,128)(2,1)} %bitcast.13, ...), custom_call_target="tpu_custom_call" | custom-call | bytes 75497472 | tf_op jit(solution)/shard_map/fetch/pallas_call | solution.py:259
  19.8 1.9 %collective-permute-done.1.refs_1_ = bf16[16,6912]{1,0:T(8,128)(2,1)S(1)} collective-permute-done((bf16[16,6912]{1,0:T(8,128)(2,1)S(1)}, bf16[16,6912]{1,0:T(8,128)(2,1)S(1)}, u32[]{:S(2)}, u32[]{:S(2)}) %collective-permute-start.1) | collective-permute-done | bytes 221216 | tf_op jit(solution)/shard_map/ppermute | solution.py:229
  21.8 2.1 %collective-permute-start = (bf16[64,6144]{1,0:T(8,128)(2,1)S(1)}, bf16[64,6144]{1,0:T(8,128)(2,1)S(1)}, u32[]{:S(2)}, u32[]{:S(2)}) collective-permute-start(bf16[64,6144]{1,0:T(8,128)(2,1)S(1)} %bitcast.16), channel_id=1, source_target_pairs={{0,8},{8,16},{16,24},{24,0},{1,9},{9,17},{17,25},{25,1},{2,10},{10... | collective-permute-start | bytes 2359304 | tf_op jit(solution)/shard_map/ppermute | solution.py:235
  23.9 4.0 %hidden.1.refs_0_ = bf16[144,1024]{1,0:T(8,128)(2,1)S(1)} custom-call(bf16[6144,1024]{1,0:T(8,128)(2,1)S(1)} %get-tuple-element.24.refs_0_, bf16[6144,1024]{1,0:T(8,128)(2,1)S(1)} %get-tuple-element.25.refs_1_, bf16[32,6912]{1,0:T(8,128)(2,1)S(1)} %stack.2.refs_2_, bf16[32,6912]{1,0:T(8,128)(2,1)S(1)} %stack.3.refs_3_, ...), custom_call_target="tpu_custom_call" | custom-call | flops 3623878656 | bytes 25165824 | tf_op jit(solution)/shard_map/hidden/pallas_call | solution.py:287
  27.9 1.3 %down.2 = (f32[64,3456]{1,0:T(8,128)S(1)}, bf16[64,3456]{1,0:T(8,128)(2,1)S(1)}) custom-call(bf16[144,1024]{1,0:T(8,128)(2,1)S(1)} %hidden.1.refs_0_, bf16[1024,6144]{1,0:T(8,128)(2,1)S(1)} %get-tuple-element.27.refs_1_), custom_call_target="tpu_custom_call" | custom-call | tf_op jit(solution)/shard_map/down/pallas_call | solution.py:300
  29.3 1.3 %down.3 = (f32[64,3456]{1,0:T(8,128)S(1)}, bf16[64,3456]{1,0:T(8,128)(2,1)S(1)}) custom-call(bf16[144,1024]{1,0:T(8,128)(2,1)S(1)} %hidden.1.refs_0_, bf16[1024,6144]{1,0:T(8,128)(2,1)S(1)} %get-tuple-element.27.refs_1_), custom_call_target="tpu_custom_call" | custom-call | tf_op jit(solution)/shard_map/down/pallas_call | solution.py:300
  30.6 0.6 collective-permute-start.11
  31.1 0.1 add_cores.2
  31.2 2.8 %collective-permute-start.7 = (bf16[16,3456]{1,0:T(8,128)(2,1)S(1)}, bf16[16,3456]{1,0:T(8,128)(2,1)S(1)}, u32[]{:S(2)}, u32[]{:S(2)}) collective-permute-start(bf16[16,3456]{1,0:T(8,128)(2,1)S(1)} %get-tuple-element.32), channel_id=1, source_target_pairs={{0,6},{1,7},{2,0},{3,1},{4,2},{5,3},{6,4},{7,5},{8,14},{9,15},{10,... | collective-permute-start | bytes 331784 | tf_op jit(solution)/shard_map/ppermute | solution.py:229
  34.0 3.2 %collective-permute-start.8 = (bf16[16,3456]{1,0:T(8,128)(2,1)S(1)}, bf16[16,3456]{1,0:T(8,128)(2,1)S(1)}, u32[]{:S(2)}, u32[]{:S(2)}) collective-permute-start(bf16[16,3456]{1,0:T(8,128)(2,1)S(1)} %get-tuple-element.33), channel_id=1, source_target_pairs={{0,4},{1,5},{2,6},{3,7},{4,0},{5,1},{6,2},{7,3},{8,12},{9,13},{10,... | collective-permute-start | bytes 331784 | tf_op jit(solution)/shard_map/ppermute | solution.py:229
  37.2 1.9 %collective-permute-start.9 = (bf16[16,3456]{1,0:T(8,128)(2,1)S(1)}, bf16[16,3456]{1,0:T(8,128)(2,1)S(1)}, u32[]{:S(2)}, u32[]{:S(2)}) collective-permute-start(bf16[16,3456]{1,0:T(8,128)(2,1)S(1)} %get-tuple-element.34), channel_id=1, source_target_pairs={{0,2},{1,3},{2,4},{3,5},{4,6},{5,7},{6,0},{7,1},{8,10},{9,11},{10,... | collective-permute-start | bytes 331784 | tf_op jit(solution)/shard_map/ppermute | solution.py:229
  39.3 1.5 %collective-permute-start.12 = (bf16[16,3584]{1,0:T(8,128)(2,1)S(1)}, bf16[16,3584]{1,0:T(8,128)(2,1)S(1)}, u32[]{:S(2)}, u32[]{:S(2)}) collective-permute-start(bf16[16,3584]{1,0:T(8,128)(2,1)S(1)} %get-tuple-element.37), channel_id=1, source_target_pairs={{0,8},{1,9},{2,10},{3,11},{4,12},{5,13},{6,14},{7,15},{8,16},{9,17... | collective-permute-start | bytes 344072 | tf_op jit(solution)/shard_map/ppermute | solution.py:226
  40.8 2.8 %collective-permute-start.13 = (bf16[16,3584]{1,0:T(8,128)(2,1)S(1)}, bf16[16,3584]{1,0:T(8,128)(2,1)S(1)}, u32[]{:S(2)}, u32[]{:S(2)}) collective-permute-start(bf16[16,3584]{1,0:T(8,128)(2,1)S(1)} %get-tuple-element.38), channel_id=1, source_target_pairs={{0,14},{1,15},{2,8},{3,9},{4,10},{5,11},{6,12},{7,13},{8,22},{9,23... | collective-permute-start | bytes 344072 | tf_op jit(solution)/shard_map/ppermute | solution.py:226
  43.6 4.6 %collective-permute-done.8.refs_2_ = bf16[16,3456]{1,0:T(8,128)(2,1)S(1)} collective-permute-done((bf16[16,3456]{1,0:T(8,128)(2,1)S(1)}, bf16[16,3456]{1,0:T(8,128)(2,1)S(1)}, u32[]{:S(2)}, u32[]{:S(2)}) %collective-permute-start.8) | collective-permute-done | bytes 110624 | tf_op jit(solution)/shard_map/ppermute | solution.py:229
  48.2 0.6 collective-permute-start.14
  48.8 0.7 %collective-permute-start.15 = (bf16[16,3584]{1,0:T(8,128)(2,1)S(1)}, bf16[16,3584]{1,0:T(8,128)(2,1)S(1)}, u32[]{:S(2)}, u32[]{:S(2)}) collective-permute-start(bf16[16,3584]{1,0:T(8,128)(2,1)S(1)} %get-tuple-element.40), channel_id=1, source_target_pairs={{0,10},{1,11},{2,12},{3,13},{4,14},{5,15},{6,8},{7,9},{8,18},{9,19... | collective-permute-start | bytes 344072 | tf_op jit(solution)/shard_map/ppermute | solution.py:226
  49.6 1.5 %collective-permute-start.10 = (bf16[16,3456]{1,0:T(8,128)(2,1)S(1)}, bf16[16,3456]{1,0:T(8,128)(2,1)S(1)}, u32[]{:S(2)}, u32[]{:S(2)}) collective-permute-start(bf16[16,3456]{1,0:T(8,128)(2,1)S(1)} %sum_chips.1), channel_id=1, source_target_pairs={{0,8},{8,16},{16,24},{24,0},{1,9},{9,17},{17,25},{25,1},{2,10},{10... | collective-permute-start | bytes 331784 | tf_op jit(solution)/shard_map/ppermute | solution.py:235
  51.2 8.2 %collective-permute-done.14.refs_3_ = bf16[16,3584]{1,0:T(8,128)(2,1)S(1)} collective-permute-done((bf16[16,3584]{1,0:T(8,128)(2,1)S(1)}, bf16[16,3584]{1,0:T(8,128)(2,1)S(1)}, u32[]{:S(2)}, u32[]{:S(2)}) %collective-permute-start.14) | collective-permute-done | bytes 114720 | tf_op jit(solution)/shard_map/ppermute | solution.py:226
  59.4 0.7 %collective-permute-done.10.refs_0_ = bf16[16,3456]{1,0:T(8,128)(2,1)S(1)} collective-permute-done((bf16[16,3456]{1,0:T(8,128)(2,1)S(1)}, bf16[16,3456]{1,0:T(8,128)(2,1)S(1)}, u32[]{:S(2)}, u32[]{:S(2)}) %collective-permute-start.10) | collective-permute-done | bytes 110624 | tf_op jit(solution)/shard_map/ppermute | solution.py:235
  60.1 1.4 %combine.1 = bf16[64,6144]{1,0:T(8,128)(2,1)} custom-call(bf16[64,6144]{1,0:T(8,128)(2,1)S(1)} %collective-permute-done.rows_ref, bf16[16,3456]{1,0:T(8,128)(2,1)S(1)} %collective-permute-done.10.refs_0_, bf16[16,3584]{1,0:T(8,128)(2,1)S(1)} %collective-permute-done.12.refs_1_, bf16[16,3584]{1,0:T(8,128)(2,1)S(1)} %collective-permute-done.13.refs_2_, ...), custom_call_target="tpu_custom_call" | custom-call | tf_op jit(solution)/shard_map/combine/pallas_call | solution.py:338
  (21 shorter events, 0.5 us)
Async XLA Ops:
  1.5 18.2 %collective-permute-start.2 = (bf16[16,6912]{1,0:T(8,128)(2,1)S(1)}, bf16[16,6912]{1,0:T(8,128)(2,1)S(1)}, u32[]{:S(2)}, u32[]{:S(2)}) collective-permute-start(bf16[16,6912]{1,0:T(8,128)(2,1)S(1)} %get-tuple-element.23.after_ref.refs_0_), channel_id=1, source_target_pairs={{0,4},{1,5},{2,6},{3,7},{4,0},{5,1},{6,2},{7,3},{8,12},{9,13},{10,... | collective-permute-start | bytes 663560 | tf_op jit(solution)/shard_map/ppermute | solution.py:229
  5.6 14.1 %collective-permute-start.3 = (bf16[16,6912]{1,0:T(8,128)(2,1)S(1)}, bf16[16,6912]{1,0:T(8,128)(2,1)S(1)}, u32[]{:S(2)}, u32[]{:S(2)}) collective-permute-start(bf16[16,6912]{1,0:T(8,128)(2,1)S(1)} %get-tuple-element.23.after_ref.refs_0_), channel_id=1, source_target_pairs={{0,6},{1,7},{2,0},{3,1},{4,2},{5,3},{6,4},{7,5},{8,14},{9,15},{10,... | collective-permute-start | bytes 663560 | tf_op jit(solution)/shard_map/ppermute | solution.py:229
  6.9 14.8 %collective-permute-start.1 = (bf16[16,6912]{1,0:T(8,128)(2,1)S(1)}, bf16[16,6912]{1,0:T(8,128)(2,1)S(1)}, u32[]{:S(2)}, u32[]{:S(2)}) collective-permute-start(bf16[16,6912]{1,0:T(8,128)(2,1)S(1)} %get-tuple-element.23.after_ref.refs_0_), channel_id=1, source_target_pairs={{0,2},{1,3},{2,4},{3,5},{4,6},{5,7},{6,0},{7,1},{8,10},{9,11},{10,... | collective-permute-start | bytes 663560 | tf_op jit(solution)/shard_map/ppermute | solution.py:229
  7.6 14.2 %copy-start = (bf16[1,64,6144]{2,1,0:T(8,128)(2,1)S(1)}, bf16[1,64,6144]{2,1,0:T(8,128)(2,1)}, u32[]{:S(2)}) copy-start(bf16[1,64,6144]{2,1,0:T(8,128)(2,1)} %param.6) | copy-start | bytes 2359300
  19.7 4.2 %collective-permute-start.5 = (bf16[32,6912]{1,0:T(8,128)(2,1)S(1)}, bf16[32,6912]{1,0:T(8,128)(2,1)S(1)}, u32[]{:S(2)}, u32[]{:S(2)}) collective-permute-start(bf16[32,6912]{1,0:T(8,128)(2,1)S(1)} %stack.3.refs_3_), channel_id=1, source_target_pairs={{0,1},{1,0},{2,3},{3,2},{4,5},{5,4},{6,7},{7,6},{8,9},{9,8},{10,11... | collective-permute-start | bytes 1327112 | tf_op jit(solution)/shard_map/ppermute | solution.py:232
  21.7 2.2 %collective-permute-start.4 = (bf16[32,6912]{1,0:T(8,128)(2,1)S(1)}, bf16[32,6912]{1,0:T(8,128)(2,1)S(1)}, u32[]{:S(2)}, u32[]{:S(2)}) collective-permute-start(bf16[32,6912]{1,0:T(8,128)(2,1)S(1)} %stack.2.refs_2_), channel_id=1, source_target_pairs={{0,1},{1,0},{2,3},{3,2},{4,5},{5,4},{6,7},{7,6},{8,9},{9,8},{10,11... | collective-permute-start | bytes 1327112 | tf_op jit(solution)/shard_map/ppermute | solution.py:232
  21.8 27.8 %collective-permute-start = (bf16[64,6144]{1,0:T(8,128)(2,1)S(1)}, bf16[64,6144]{1,0:T(8,128)(2,1)S(1)}, u32[]{:S(2)}, u32[]{:S(2)}) collective-permute-start(bf16[64,6144]{1,0:T(8,128)(2,1)S(1)} %bitcast.16), channel_id=1, source_target_pairs={{0,8},{8,16},{16,24},{24,0},{1,9},{9,17},{17,25},{25,1},{2,10},{10... | collective-permute-start | bytes 2359304 | tf_op jit(solution)/shard_map/ppermute | solution.py:235
  29.2 1.9 %collective-permute-start.6 = (bf16[64,3456]{1,0:T(8,128)(2,1)S(1)}, bf16[64,3456]{1,0:T(8,128)(2,1)S(1)}, u32[]{:S(2)}, u32[]{:S(2)}) collective-permute-start(bf16[64,3456]{1,0:T(8,128)(2,1)S(1)} %get-tuple-element.29), channel_id=1, source_target_pairs={{0,1},{1,0},{2,3},{3,2},{4,5},{5,4},{6,7},{7,6},{8,9},{9,8},{10,11... | collective-permute-start | bytes 1327112 | tf_op jit(solution)/shard_map/ppermute | solution.py:232
  30.6 8.6 %collective-permute-start.11 = (bf16[64,3456]{1,0:T(8,128)(2,1)S(1)}, bf16[64,3456]{1,0:T(8,128)(2,1)S(1)}, u32[]{:S(2)}, u32[]{:S(2)}) collective-permute-start(bf16[64,3456]{1,0:T(8,128)(2,1)S(1)} %get-tuple-element.36), channel_id=1, source_target_pairs={{0,1},{1,0},{2,3},{3,2},{4,5},{5,4},{6,7},{7,6},{8,9},{9,8},{10,11... | collective-permute-start | bytes 1327112 | tf_op jit(solution)/shard_map/ppermute | solution.py:232
  31.2 9.6 %collective-permute-start.7 = (bf16[16,3456]{1,0:T(8,128)(2,1)S(1)}, bf16[16,3456]{1,0:T(8,128)(2,1)S(1)}, u32[]{:S(2)}, u32[]{:S(2)}) collective-permute-start(bf16[16,3456]{1,0:T(8,128)(2,1)S(1)} %get-tuple-element.32), channel_id=1, source_target_pairs={{0,6},{1,7},{2,0},{3,1},{4,2},{5,3},{6,4},{7,5},{8,14},{9,15},{10,... | collective-permute-start | bytes 331784 | tf_op jit(solution)/shard_map/ppermute | solution.py:229
  34.0 14.2 %collective-permute-start.8 = (bf16[16,3456]{1,0:T(8,128)(2,1)S(1)}, bf16[16,3456]{1,0:T(8,128)(2,1)S(1)}, u32[]{:S(2)}, u32[]{:S(2)}) collective-permute-start(bf16[16,3456]{1,0:T(8,128)(2,1)S(1)} %get-tuple-element.33), channel_id=1, source_target_pairs={{0,4},{1,5},{2,6},{3,7},{4,0},{5,1},{6,2},{7,3},{8,12},{9,13},{10,... | collective-permute-start | bytes 331784 | tf_op jit(solution)/shard_map/ppermute | solution.py:229
  37.2 11.6 %collective-permute-start.9 = (bf16[16,3456]{1,0:T(8,128)(2,1)S(1)}, bf16[16,3456]{1,0:T(8,128)(2,1)S(1)}, u32[]{:S(2)}, u32[]{:S(2)}) collective-permute-start(bf16[16,3456]{1,0:T(8,128)(2,1)S(1)} %get-tuple-element.34), channel_id=1, source_target_pairs={{0,2},{1,3},{2,4},{3,5},{4,6},{5,7},{6,0},{7,1},{8,10},{9,11},{10,... | collective-permute-start | bytes 331784 | tf_op jit(solution)/shard_map/ppermute | solution.py:229
  39.3 11.9 %collective-permute-start.12 = (bf16[16,3584]{1,0:T(8,128)(2,1)S(1)}, bf16[16,3584]{1,0:T(8,128)(2,1)S(1)}, u32[]{:S(2)}, u32[]{:S(2)}) collective-permute-start(bf16[16,3584]{1,0:T(8,128)(2,1)S(1)} %get-tuple-element.37), channel_id=1, source_target_pairs={{0,8},{1,9},{2,10},{3,11},{4,12},{5,13},{6,14},{7,15},{8,16},{9,17... | collective-permute-start | bytes 344072 | tf_op jit(solution)/shard_map/ppermute | solution.py:226
  40.8 10.3 %collective-permute-start.13 = (bf16[16,3584]{1,0:T(8,128)(2,1)S(1)}, bf16[16,3584]{1,0:T(8,128)(2,1)S(1)}, u32[]{:S(2)}, u32[]{:S(2)}) collective-permute-start(bf16[16,3584]{1,0:T(8,128)(2,1)S(1)} %get-tuple-element.38), channel_id=1, source_target_pairs={{0,14},{1,15},{2,8},{3,9},{4,10},{5,11},{6,12},{7,13},{8,22},{9,23... | collective-permute-start | bytes 344072 | tf_op jit(solution)/shard_map/ppermute | solution.py:226
  48.2 11.2 %collective-permute-start.14 = (bf16[16,3584]{1,0:T(8,128)(2,1)S(1)}, bf16[16,3584]{1,0:T(8,128)(2,1)S(1)}, u32[]{:S(2)}, u32[]{:S(2)}) collective-permute-start(bf16[16,3584]{1,0:T(8,128)(2,1)S(1)} %get-tuple-element.39), channel_id=1, source_target_pairs={{0,12},{1,13},{2,14},{3,15},{4,8},{5,9},{6,10},{7,11},{8,20},{9,21... | collective-permute-start | bytes 344072 | tf_op jit(solution)/shard_map/ppermute | solution.py:226
  48.8 10.6 %collective-permute-start.15 = (bf16[16,3584]{1,0:T(8,128)(2,1)S(1)}, bf16[16,3584]{1,0:T(8,128)(2,1)S(1)}, u32[]{:S(2)}, u32[]{:S(2)}) collective-permute-start(bf16[16,3584]{1,0:T(8,128)(2,1)S(1)} %get-tuple-element.40), channel_id=1, source_target_pairs={{0,10},{1,11},{2,12},{3,13},{4,14},{5,15},{6,8},{7,9},{8,18},{9,19... | collective-permute-start | bytes 344072 | tf_op jit(solution)/shard_map/ppermute | solution.py:226
  49.6 10.5 %collective-permute-start.10 = (bf16[16,3456]{1,0:T(8,128)(2,1)S(1)}, bf16[16,3456]{1,0:T(8,128)(2,1)S(1)}, u32[]{:S(2)}, u32[]{:S(2)}) collective-permute-start(bf16[16,3456]{1,0:T(8,128)(2,1)S(1)} %sum_chips.1), channel_id=1, source_target_pairs={{0,8},{8,16},{16,24},{24,0},{1,9},{9,17},{17,25},{25,1},{2,10},{10... | collective-permute-start | bytes 331784 | tf_op jit(solution)/shard_map/ppermute | solution.py:235

commit v5 on v4

--- a/solution.py
+++ b/solution.py
@@ -217,16 +217,16 @@
     wides = [width + width // SLABS for start, width in spans(model)]
     total_rows = shards * CAP
 
-    def across(value, steps):
+    def across(value, flip):
         pairs = [
-            (s * shards + i, (s + 1) % sections * shards + (i + 2 * steps) % shards)
+            (s * shards + i, (s + 1) % sections * shards + (i ^ (2 * flip)))
             for s in range(sections)
             for i in range(shards)
         ]
         return lax.ppermute(value, ("section", "shard"), pairs)
 
-    def along(value, steps):
-        return lax.ppermute(value, "shard", [(i, (i + 2 * steps) % shards) for i in range(shards)])
+    def along(value, flip):
+        return lax.ppermute(value, "shard", [(i, i ^ (2 * flip)) for i in range(shards)])
 
     def swap(value):
         return lax.ppermute(value, "shard", [(i, i ^ 1) for i in range(shards)])
@@ -322,9 +322,9 @@
             name="add_cores",
         )(own, other, info)
         if last:
-            arrived += [across(block, -m) for m, block in enumerate((kept, *leaving))]
+            arrived += [across(block, m) for m, block in enumerate((kept, *leaving))]
             break
-        coming = [along(block, -m) for m, block in enumerate(leaving, 1)]
+        coming = [along(leaving[m - 1], m) for m in (chips - 1, *range(1, chips - 1))]
         extra = []
         summed = pl.pallas_call(
             lambda *refs: sum_kernel(chips, *refs),

time: 61.7 us -> 59.4 us (0.963)
  waiting for transfers between devices: 15.4 us -> 9.91 us
  starting transfers between devices: 24.2 us -> 27.4 us
    ppermute x4, starting transfers between devices: 5.67 us -> 10.3 us  [across(): return lax.ppermute(value, ('section', 'shard'), pairs)]
    ppermute x4, waiting for transfers between devices: 8.23 us -> 4.83 us  [across(): return lax.ppermute(value, ('section', 'shard'), pairs)]
    ppermute x6, waiting for transfers between devices: 6.49 us -> 3.41 us  [along(): lax.ppermute(value, 'shard', [(i, i ^ 2 * flip) for i in range(shards)])]
    ppermute x6, starting transfers between devices: 14.1 us -> 12.8 us  [along(): lax.ppermute(value, 'shard', [(i, i ^ 2 * flip) for i in range(shards)])]
    ppermute x2, waiting for transfers between devices: 0.71 us -> 1.67 us  [onward(): lax.ppermute(value, 'section', [(s, (s + 1) % sections) for s in range(se...]
  transfers between devices with their start and end apart: 16 -> 16, of which waited for: 4 -> 5; matrix products, arithmetic and copies ran while one was open for 0% -> 0% of each run, Pallas kernels for 31% -> 32%
where the time goes in v5:
time: 59.4 us; the launch traced here: 59.2 us
  starting transfers between devices  27.4 us (46%)
  Pallas kernels  21.8 us (37%)
  waiting for transfers between devices  9.91 us (17%)
    ppermute x6, starting transfers between devices, along(): lax.ppermute(value, 'shard', [(i, i ^ 2 * flip) for i in range(shards)])  12.8 us
    pallas_call x1, Pallas kernels, on_device(): pl.pallas_call(fetch_kernel, out_shape=[pltpu.VMEM((model, hidden_units),...  12.1 us
    ppermute x4, starting transfers between devices, across(): return lax.ppermute(value, ('section', 'shard'), pairs)  10.3 us
    ppermute x4, waiting for transfers between devices, across(): return lax.ppermute(value, ('section', 'shard'), pairs)  4.83 us
    pallas_call x1, Pallas kernels, on_device(): pl.pallas_call(lambda *refs: hidden_kernel(shards, *refs), out_shape=jax....  4.02 us
    ppermute x6, waiting for transfers between devices, along(): lax.ppermute(value, 'shard', [(i, i ^ 2 * flip) for i in range(shards)])  3.41 us
    ppermute x2, starting transfers between devices, onward(): lax.ppermute(value, 'section', [(s, (s + 1) % sections) for s in range(se...  3.38 us
    pallas_call x2, Pallas kernels, on_device(): pl.pallas_call(lambda *refs, c=c: down_kernel(shards, c, *refs), out_shap...  2.53 us
  transfers between devices with their start and end apart: 16, of which 5 were waited for; matrix products, arithmetic and copies ran while one was open for 0% of the time, Pallas kernels for 32%

profile of v5, /device:TPU:0, one launch (start us, length us, event | category | flops | bytes accessed | tf_op | source)
XLA Modules:
  0.0 59.2 jit_solution(1369920741996105637)
XLA Ops:
  0.0 1.5 %pack.1 = (bf16[16,128]{1,0:T(8,128)(2,1)S(1)}, bf16[16,6912]{1,0:T(8,128)(2,1)S(1)}) custom-call(s32[1]{0:T(128)} %bitcast.1.section_ref, s32[2,64]{1,0:T(2,128)} %bitcast.17, f32[2,64]{1,0:T(2,128)} %bitcast.18, bf16[64,6144]{1,0:T(8,128)(2,1)} %bitcast.15), custom_call_target="tpu_custom_call" | custom-call | bytes 1572864 | tf_op jit(solution)/shard_map/pack/pallas_call | solution.py:238
  1.5 4.1 %collective-permute-start.2 = (bf16[16,6912]{1,0:T(8,128)(2,1)S(1)}, bf16[16,6912]{1,0:T(8,128)(2,1)S(1)}, u32[]{:S(2)}, u32[]{:S(2)}) collective-permute-start(bf16[16,6912]{1,0:T(8,128)(2,1)S(1)} %get-tuple-element.23.after_ref.refs_0_), channel_id=1, source_target_pairs={{0,4},{1,5},{2,6},{3,7},{4,0},{5,1},{6,2},{7,3},{8,12},{9,13},{10,... | collective-permute-start | bytes 663560 | tf_op jit(solution)/shard_map/ppermute | solution.py:229
  5.6 1.3 %collective-permute-start.3 = (bf16[16,6912]{1,0:T(8,128)(2,1)S(1)}, bf16[16,6912]{1,0:T(8,128)(2,1)S(1)}, u32[]{:S(2)}, u32[]{:S(2)}) collective-permute-start(bf16[16,6912]{1,0:T(8,128)(2,1)S(1)} %get-tuple-element.23.after_ref.refs_0_), channel_id=1, source_target_pairs={{0,6},{1,7},{2,4},{3,5},{4,2},{5,3},{6,0},{7,1},{8,14},{9,15},{10,... | collective-permute-start | bytes 663560 | tf_op jit(solution)/shard_map/ppermute | solution.py:229
  6.9 0.2 collective-permute-start.1
  7.1 12.1 %fetch.1 = (bf16[6144,1024]{1,0:T(8,128)(2,1)S(1)}, bf16[6144,1024]{1,0:T(8,128)(2,1)S(1)}, bf16[1024,6144]{1,0:T(8,128)(2,1)S(1)}, f32[8,128]{1,0:T(8,128)S(1)}) custom-call(bf16[16,6912]{1,0:T(8,128)(2,1)S(1)} %get-tuple-element.23.after_ref.refs_0_, bf16[6144,1024]{1,0:T(8,128)(2,1)} %bitcast.12, bf16[6144,1024]{1,0:T(8,128)(2,1)} %bitcast.13, ...), custom_call_target="tpu_custom_call" | custom-call | bytes 75497472 | tf_op jit(solution)/shard_map/fetch/pallas_call | solution.py:259
  19.2 2.1 %collective-permute-done.2.refs_0_ = bf16[16,6912]{1,0:T(8,128)(2,1)S(1)} collective-permute-done((bf16[16,6912]{1,0:T(8,128)(2,1)S(1)}, bf16[16,6912]{1,0:T(8,128)(2,1)S(1)}, u32[]{:S(2)}, u32[]{:S(2)}) %collective-permute-start.2) | collective-permute-done | bytes 221216 | tf_op jit(solution)/shard_map/ppermute | solution.py:229
  21.5 0.4 collective-permute-done.1.refs_1_
  22.1 1.8 %collective-permute-start = (bf16[64,6144]{1,0:T(8,128)(2,1)S(1)}, bf16[64,6144]{1,0:T(8,128)(2,1)S(1)}, u32[]{:S(2)}, u32[]{:S(2)}) collective-permute-start(bf16[64,6144]{1,0:T(8,128)(2,1)S(1)} %bitcast.16), channel_id=1, source_target_pairs={{0,8},{8,16},{16,24},{24,0},{1,9},{9,17},{17,25},{25,1},{2,10},{10... | collective-permute-start | bytes 2359304 | tf_op jit(solution)/shard_map/ppermute | solution.py:235
  23.9 4.0 %hidden.1.refs_0_ = bf16[144,1024]{1,0:T(8,128)(2,1)S(1)} custom-call(bf16[6144,1024]{1,0:T(8,128)(2,1)S(1)} %get-tuple-element.24.refs_0_, bf16[6144,1024]{1,0:T(8,128)(2,1)S(1)} %get-tuple-element.25.refs_1_, bf16[32,6912]{1,0:T(8,128)(2,1)S(1)} %stack.2.refs_2_, bf16[32,6912]{1,0:T(8,128)(2,1)S(1)} %stack.3.refs_3_, ...), custom_call_target="tpu_custom_call" | custom-call | flops 3623878656 | bytes 25165824 | tf_op jit(solution)/shard_map/hidden/pallas_call | solution.py:287
  27.9 1.3 %down.2 = (f32[64,3456]{1,0:T(8,128)S(1)}, bf16[64,3456]{1,0:T(8,128)(2,1)S(1)}) custom-call(bf16[144,1024]{1,0:T(8,128)(2,1)S(1)} %hidden.1.refs_0_, bf16[1024,6144]{1,0:T(8,128)(2,1)S(1)} %get-tuple-element.27.refs_1_), custom_call_target="tpu_custom_call" | custom-call | tf_op jit(solution)/shard_map/down/pallas_call | solution.py:300
  29.2 0.2 collective-permute-start.6
  29.4 1.3 %down.3 = (f32[64,3456]{1,0:T(8,128)S(1)}, bf16[64,3456]{1,0:T(8,128)(2,1)S(1)}) custom-call(bf16[144,1024]{1,0:T(8,128)(2,1)S(1)} %hidden.1.refs_0_, bf16[1024,6144]{1,0:T(8,128)(2,1)S(1)} %get-tuple-element.27.refs_1_), custom_call_target="tpu_custom_call" | custom-call | tf_op jit(solution)/shard_map/down/pallas_call | solution.py:300
  30.7 0.5 collective-permute-start.11
  31.2 3.4 %collective-permute-start.7 = (bf16[16,3456]{1,0:T(8,128)(2,1)S(1)}, bf16[16,3456]{1,0:T(8,128)(2,1)S(1)}, u32[]{:S(2)}, u32[]{:S(2)}) collective-permute-start(bf16[16,3456]{1,0:T(8,128)(2,1)S(1)} %get-tuple-element.32), channel_id=1, source_target_pairs={{0,6},{1,7},{2,4},{3,5},{4,2},{5,3},{6,0},{7,1},{8,14},{9,15},{10,... | collective-permute-start | bytes 331784 | tf_op jit(solution)/shard_map/ppermute | solution.py:229
  34.6 3.7 %collective-permute-start.8 = (bf16[16,3456]{1,0:T(8,128)(2,1)S(1)}, bf16[16,3456]{1,0:T(8,128)(2,1)S(1)}, u32[]{:S(2)}, u32[]{:S(2)}) collective-permute-start(bf16[16,3456]{1,0:T(8,128)(2,1)S(1)} %get-tuple-element.33), channel_id=1, source_target_pairs={{0,2},{1,3},{2,0},{3,1},{4,6},{5,7},{6,4},{7,5},{8,10},{9,11},{10,... | collective-permute-start | bytes 331784 | tf_op jit(solution)/shard_map/ppermute | solution.py:229
  38.5 1.5 %collective-permute-start.12 = (bf16[16,3584]{1,0:T(8,128)(2,1)S(1)}, bf16[16,3584]{1,0:T(8,128)(2,1)S(1)}, u32[]{:S(2)}, u32[]{:S(2)}) collective-permute-start(bf16[16,3584]{1,0:T(8,128)(2,1)S(1)} %get-tuple-element.37), channel_id=1, source_target_pairs={{0,8},{1,9},{2,10},{3,11},{4,12},{5,13},{6,14},{7,15},{8,16},{9,17... | collective-permute-start | bytes 344072 | tf_op jit(solution)/shard_map/ppermute | solution.py:226
  40.0 3.0 %collective-permute-start.13 = (bf16[16,3584]{1,0:T(8,128)(2,1)S(1)}, bf16[16,3584]{1,0:T(8,128)(2,1)S(1)}, u32[]{:S(2)}, u32[]{:S(2)}) collective-permute-start(bf16[16,3584]{1,0:T(8,128)(2,1)S(1)} %get-tuple-element.38), channel_id=1, source_target_pairs={{0,10},{1,11},{2,8},{3,9},{4,14},{5,15},{6,12},{7,13},{8,18},{9,19... | collective-permute-start | bytes 344072 | tf_op jit(solution)/shard_map/ppermute | solution.py:226
  43.0 2.4 %collective-permute-start.14 = (bf16[16,3584]{1,0:T(8,128)(2,1)S(1)}, bf16[16,3584]{1,0:T(8,128)(2,1)S(1)}, u32[]{:S(2)}, u32[]{:S(2)}) collective-permute-start(bf16[16,3584]{1,0:T(8,128)(2,1)S(1)} %get-tuple-element.39), channel_id=1, source_target_pairs={{0,12},{1,13},{2,14},{3,15},{4,8},{5,9},{6,10},{7,11},{8,20},{9,21... | collective-permute-start | bytes 344072 | tf_op jit(solution)/shard_map/ppermute | solution.py:226
  45.4 0.9 %collective-permute-done.9.refs_3_ = bf16[16,3456]{1,0:T(8,128)(2,1)S(1)} collective-permute-done((bf16[16,3456]{1,0:T(8,128)(2,1)S(1)}, bf16[16,3456]{1,0:T(8,128)(2,1)S(1)}, u32[]{:S(2)}, u32[]{:S(2)}) %collective-permute-start.9) | collective-permute-done | bytes 110624 | tf_op jit(solution)/shard_map/ppermute | solution.py:229
  46.3 3.4 %collective-permute-start.15 = (bf16[16,3584]{1,0:T(8,128)(2,1)S(1)}, bf16[16,3584]{1,0:T(8,128)(2,1)S(1)}, u32[]{:S(2)}, u32[]{:S(2)}) collective-permute-start(bf16[16,3584]{1,0:T(8,128)(2,1)S(1)} %get-tuple-element.40), channel_id=1, source_target_pairs={{0,14},{1,15},{2,12},{3,13},{4,10},{5,11},{6,8},{7,9},{8,22},{9,23... | collective-permute-start | bytes 344072 | tf_op jit(solution)/shard_map/ppermute | solution.py:226
  49.8 1.5 %collective-permute-start.10 = (bf16[16,3456]{1,0:T(8,128)(2,1)S(1)}, bf16[16,3456]{1,0:T(8,128)(2,1)S(1)}, u32[]{:S(2)}, u32[]{:S(2)}) collective-permute-start(bf16[16,3456]{1,0:T(8,128)(2,1)S(1)} %sum_chips.1), channel_id=1, source_target_pairs={{0,8},{8,16},{16,24},{24,0},{1,9},{9,17},{17,25},{25,1},{2,10},{10... | collective-permute-start | bytes 331784 | tf_op jit(solution)/shard_map/ppermute | solution.py:235
  51.3 4.8 %collective-permute-done.14.refs_3_ = bf16[16,3584]{1,0:T(8,128)(2,1)S(1)} collective-permute-done((bf16[16,3584]{1,0:T(8,128)(2,1)S(1)}, bf16[16,3584]{1,0:T(8,128)(2,1)S(1)}, u32[]{:S(2)}, u32[]{:S(2)}) %collective-permute-start.14) | collective-permute-done | bytes 114720 | tf_op jit(solution)/shard_map/ppermute | solution.py:226
  56.1 1.7 %collective-permute-done.10.refs_0_ = bf16[16,3456]{1,0:T(8,128)(2,1)S(1)} collective-permute-done((bf16[16,3456]{1,0:T(8,128)(2,1)S(1)}, bf16[16,3456]{1,0:T(8,128)(2,1)S(1)}, u32[]{:S(2)}, u32[]{:S(2)}) %collective-permute-start.10) | collective-permute-done | bytes 110624 | tf_op jit(solution)/shard_map/ppermute | solution.py:235
  57.8 1.4 %combine.1 = bf16[64,6144]{1,0:T(8,128)(2,1)} custom-call(bf16[64,6144]{1,0:T(8,128)(2,1)S(1)} %collective-permute-done.rows_ref, bf16[16,3456]{1,0:T(8,128)(2,1)S(1)} %collective-permute-done.10.refs_0_, bf16[16,3584]{1,0:T(8,128)(2,1)S(1)} %collective-permute-done.12.refs_1_, bf16[16,3584]{1,0:T(8,128)(2,1)S(1)} %collective-permute-done.13.refs_2_, ...), custom_call_target="tpu_custom_call" | custom-call | tf_op jit(solution)/shard_map/combine/pallas_call | solution.py:338
  (21 shorter events, 0.6 us)
Async XLA Ops:
  1.5 19.9 %collective-permute-start.2 = (bf16[16,6912]{1,0:T(8,128)(2,1)S(1)}, bf16[16,6912]{1,0:T(8,128)(2,1)S(1)}, u32[]{:S(2)}, u32[]{:S(2)}) collective-permute-start(bf16[16,6912]{1,0:T(8,128)(2,1)S(1)} %get-tuple-element.23.after_ref.refs_0_), channel_id=1, source_target_pairs={{0,4},{1,5},{2,6},{3,7},{4,0},{5,1},{6,2},{7,3},{8,12},{9,13},{10,... | collective-permute-start | bytes 663560 | tf_op jit(solution)/shard_map/ppermute | solution.py:229
  5.6 15.8 %collective-permute-start.3 = (bf16[16,6912]{1,0:T(8,128)(2,1)S(1)}, bf16[16,6912]{1,0:T(8,128)(2,1)S(1)}, u32[]{:S(2)}, u32[]{:S(2)}) collective-permute-start(bf16[16,6912]{1,0:T(8,128)(2,1)S(1)} %get-tuple-element.23.after_ref.refs_0_), channel_id=1, source_target_pairs={{0,6},{1,7},{2,4},{3,5},{4,2},{5,3},{6,0},{7,1},{8,14},{9,15},{10,... | collective-permute-start | bytes 663560 | tf_op jit(solution)/shard_map/ppermute | solution.py:229
  6.9 14.9 %collective-permute-start.1 = (bf16[16,6912]{1,0:T(8,128)(2,1)S(1)}, bf16[16,6912]{1,0:T(8,128)(2,1)S(1)}, u32[]{:S(2)}, u32[]{:S(2)}) collective-permute-start(bf16[16,6912]{1,0:T(8,128)(2,1)S(1)} %get-tuple-element.23.after_ref.refs_0_), channel_id=1, source_target_pairs={{0,2},{1,3},{2,0},{3,1},{4,6},{5,7},{6,4},{7,5},{8,10},{9,11},{10,... | collective-permute-start | bytes 663560 | tf_op jit(solution)/shard_map/ppermute | solution.py:229
  7.1 14.9 %copy-start = (bf16[1,64,6144]{2,1,0:T(8,128)(2,1)S(1)}, bf16[1,64,6144]{2,1,0:T(8,128)(2,1)}, u32[]{:S(2)}) copy-start(bf16[1,64,6144]{2,1,0:T(8,128)(2,1)} %param.6) | copy-start | bytes 2359300
  21.4 2.5 %collective-permute-start.5 = (bf16[32,6912]{1,0:T(8,128)(2,1)S(1)}, bf16[32,6912]{1,0:T(8,128)(2,1)S(1)}, u32[]{:S(2)}, u32[]{:S(2)}) collective-permute-start(bf16[32,6912]{1,0:T(8,128)(2,1)S(1)} %stack.3.refs_3_), channel_id=1, source_target_pairs={{0,1},{1,0},{2,3},{3,2},{4,5},{5,4},{6,7},{7,6},{8,9},{9,8},{10,11... | collective-permute-start | bytes 1327112 | tf_op jit(solution)/shard_map/ppermute | solution.py:232
  21.9 2.0 %collective-permute-start.4 = (bf16[32,6912]{1,0:T(8,128)(2,1)S(1)}, bf16[32,6912]{1,0:T(8,128)(2,1)S(1)}, u32[]{:S(2)}, u32[]{:S(2)}) collective-permute-start(bf16[32,6912]{1,0:T(8,128)(2,1)S(1)} %stack.2.refs_2_), channel_id=1, source_target_pairs={{0,1},{1,0},{2,3},{3,2},{4,5},{5,4},{6,7},{7,6},{8,9},{9,8},{10,11... | collective-permute-start | bytes 1327112 | tf_op jit(solution)/shard_map/ppermute | solution.py:232
  22.1 27.7 %collective-permute-start = (bf16[64,6144]{1,0:T(8,128)(2,1)S(1)}, bf16[64,6144]{1,0:T(8,128)(2,1)S(1)}, u32[]{:S(2)}, u32[]{:S(2)}) collective-permute-start(bf16[64,6144]{1,0:T(8,128)(2,1)S(1)} %bitcast.16), channel_id=1, source_target_pairs={{0,8},{8,16},{16,24},{24,0},{1,9},{9,17},{17,25},{25,1},{2,10},{10... | collective-permute-start | bytes 2359304 | tf_op jit(solution)/shard_map/ppermute | solution.py:235
  29.2 1.9 %collective-permute-start.6 = (bf16[64,3456]{1,0:T(8,128)(2,1)S(1)}, bf16[64,3456]{1,0:T(8,128)(2,1)S(1)}, u32[]{:S(2)}, u32[]{:S(2)}) collective-permute-start(bf16[64,3456]{1,0:T(8,128)(2,1)S(1)} %get-tuple-element.29), channel_id=1, source_target_pairs={{0,1},{1,0},{2,3},{3,2},{4,5},{5,4},{6,7},{7,6},{8,9},{9,8},{10,11... | collective-permute-start | bytes 1327112 | tf_op jit(solution)/shard_map/ppermute | solution.py:232
  30.7 7.7 %collective-permute-start.11 = (bf16[64,3456]{1,0:T(8,128)(2,1)S(1)}, bf16[64,3456]{1,0:T(8,128)(2,1)S(1)}, u32[]{:S(2)}, u32[]{:S(2)}) collective-permute-start(bf16[64,3456]{1,0:T(8,128)(2,1)S(1)} %get-tuple-element.36), channel_id=1, source_target_pairs={{0,1},{1,0},{2,3},{3,2},{4,5},{5,4},{6,7},{7,6},{8,9},{9,8},{10,11... | collective-permute-start | bytes 1327112 | tf_op jit(solution)/shard_map/ppermute | solution.py:232
  31.2 8.8 %collective-permute-start.7 = (bf16[16,3456]{1,0:T(8,128)(2,1)S(1)}, bf16[16,3456]{1,0:T(8,128)(2,1)S(1)}, u32[]{:S(2)}, u32[]{:S(2)}) collective-permute-start(bf16[16,3456]{1,0:T(8,128)(2,1)S(1)} %get-tuple-element.32), channel_id=1, source_target_pairs={{0,6},{1,7},{2,4},{3,5},{4,2},{5,3},{6,0},{7,1},{8,14},{9,15},{10,... | collective-permute-start | bytes 331784 | tf_op jit(solution)/shard_map/ppermute | solution.py:229
  34.6 8.3 %collective-permute-start.8 = (bf16[16,3456]{1,0:T(8,128)(2,1)S(1)}, bf16[16,3456]{1,0:T(8,128)(2,1)S(1)}, u32[]{:S(2)}, u32[]{:S(2)}) collective-permute-start(bf16[16,3456]{1,0:T(8,128)(2,1)S(1)} %get-tuple-element.33), channel_id=1, source_target_pairs={{0,2},{1,3},{2,0},{3,1},{4,6},{5,7},{6,4},{7,5},{8,10},{9,11},{10,... | collective-permute-start | bytes 331784 | tf_op jit(solution)/shard_map/ppermute | solution.py:229
  38.4 7.9 %collective-permute-start.9 = (bf16[16,3456]{1,0:T(8,128)(2,1)S(1)}, bf16[16,3456]{1,0:T(8,128)(2,1)S(1)}, u32[]{:S(2)}, u32[]{:S(2)}) collective-permute-start(bf16[16,3456]{1,0:T(8,128)(2,1)S(1)} %get-tuple-element.34), channel_id=1, source_target_pairs={{0,4},{1,5},{2,6},{3,7},{4,0},{5,1},{6,2},{7,3},{8,12},{9,13},{10,... | collective-permute-start | bytes 331784 | tf_op jit(solution)/shard_map/ppermute | solution.py:229
  38.5 12.9 %collective-permute-start.12 = (bf16[16,3584]{1,0:T(8,128)(2,1)S(1)}, bf16[16,3584]{1,0:T(8,128)(2,1)S(1)}, u32[]{:S(2)}, u32[]{:S(2)}) collective-permute-start(bf16[16,3584]{1,0:T(8,128)(2,1)S(1)} %get-tuple-element.37), channel_id=1, source_target_pairs={{0,8},{1,9},{2,10},{3,11},{4,12},{5,13},{6,14},{7,15},{8,16},{9,17... | collective-permute-start | bytes 344072 | tf_op jit(solution)/shard_map/ppermute | solution.py:226
  40.0 11.3 %collective-permute-start.13 = (bf16[16,3584]{1,0:T(8,128)(2,1)S(1)}, bf16[16,3584]{1,0:T(8,128)(2,1)S(1)}, u32[]{:S(2)}, u32[]{:S(2)}) collective-permute-start(bf16[16,3584]{1,0:T(8,128)(2,1)S(1)} %get-tuple-element.38), channel_id=1, source_target_pairs={{0,10},{1,11},{2,8},{3,9},{4,14},{5,15},{6,12},{7,13},{8,18},{9,19... | collective-permute-start | bytes 344072 | tf_op jit(solution)/shard_map/ppermute | solution.py:226
  43.0 13.2 %collective-permute-start.14 = (bf16[16,3584]{1,0:T(8,128)(2,1)S(1)}, bf16[16,3584]{1,0:T(8,128)(2,1)S(1)}, u32[]{:S(2)}, u32[]{:S(2)}) collective-permute-start(bf16[16,3584]{1,0:T(8,128)(2,1)S(1)} %get-tuple-element.39), channel_id=1, source_target_pairs={{0,12},{1,13},{2,14},{3,15},{4,8},{5,9},{6,10},{7,11},{8,20},{9,21... | collective-permute-start | bytes 344072 | tf_op jit(solution)/shard_map/ppermute | solution.py:226
  46.3 9.9 %collective-permute-start.15 = (bf16[16,3584]{1,0:T(8,128)(2,1)S(1)}, bf16[16,3584]{1,0:T(8,128)(2,1)S(1)}, u32[]{:S(2)}, u32[]{:S(2)}) collective-permute-start(bf16[16,3584]{1,0:T(8,128)(2,1)S(1)} %get-tuple-element.40), channel_id=1, source_target_pairs={{0,14},{1,15},{2,12},{3,13},{4,10},{5,11},{6,8},{7,9},{8,22},{9,23... | collective-permute-start | bytes 344072 | tf_op jit(solution)/shard_map/ppermute | solution.py:226
  49.8 8.0 %collective-permute-start.10 = (bf16[16,3456]{1,0:T(8,128)(2,1)S(1)}, bf16[16,3456]{1,0:T(8,128)(2,1)S(1)}, u32[]{:S(2)}, u32[]{:S(2)}) collective-permute-start(bf16[16,3456]{1,0:T(8,128)(2,1)S(1)} %sum_chips.1), channel_id=1, source_target_pairs={{0,8},{8,16},{16,24},{24,0},{1,9},{9,17},{17,25},{25,1},{2,10},{10... | collective-permute-start | bytes 331784 | tf_op jit(solution)/shard_map/ppermute | solution.py:235

commit v6 on v5

--- a/solution.py
+++ b/solution.py
@@ -315,7 +315,7 @@
         kept, *leaving = pl.pallas_call(
             add_kernel,
             out_shape=[jax.ShapeDtypeStruct((MAIN, wide + 128 * last), bf16 if last else f32)]
-            + [jax.ShapeDtypeStruct((MAIN, wide + 128 * last), bf16)] * (chips - 1),
+            + [jax.ShapeDtypeStruct((MAIN, wide), bf16)] * (chips - 1),
             in_specs=whole(3),
             out_specs=whole(chips),
             compiler_params=params(),

time: 59.4 us -> 59.1 us (level)
  no operation moved by 1% of the time
where the time goes in v6:
time: 59.1 us; the launch traced here: 59 us
  starting transfers between devices  27.4 us (46%)
  Pallas kernels  21.8 us (37%)
  waiting for transfers between devices  9.65 us (16%)
    ppermute x6, starting transfers between devices, along(): lax.ppermute(value, 'shard', [(i, i ^ 2 * flip) for i in range(shards)])  12.8 us
    pallas_call x1, Pallas kernels, on_device(): pl.pallas_call(fetch_kernel, out_shape=[pltpu.VMEM((model, hidden_units),...  12.1 us
    ppermute x4, starting transfers between devices, across(): return lax.ppermute(value, ('section', 'shard'), pairs)  10.3 us
    ppermute x4, waiting for transfers between devices, across(): return lax.ppermute(value, ('section', 'shard'), pairs)  4.57 us
    pallas_call x1, Pallas kernels, on_device(): pl.pallas_call(lambda *refs: hidden_kernel(shards, *refs), out_shape=jax....  4.02 us
    ppermute x6, waiting for transfers between devices, along(): lax.ppermute(value, 'shard', [(i, i ^ 2 * flip) for i in range(shards)])  3.41 us
    ppermute x2, starting transfers between devices, onward(): lax.ppermute(value, 'section', [(s, (s + 1) % sections) for s in range(se...  3.38 us
    pallas_call x2, Pallas kernels, on_device(): pl.pallas_call(lambda *refs, c=c: down_kernel(shards, c, *refs), out_shap...  2.53 us
  transfers between devices with their start and end apart: 16, of which 5 were waited for; matrix products, arithmetic and copies ran while one was open for 0% of the time, Pallas kernels for 32%

profile of v6, /device:TPU:0, one launch (start us, length us, event | category | flops | bytes accessed | tf_op | source)
XLA Modules:
  0.0 59.0 jit_solution(16900998568023730066)
XLA Ops:
  0.0 1.5 %pack.1 = (bf16[16,128]{1,0:T(8,128)(2,1)S(1)}, bf16[16,6912]{1,0:T(8,128)(2,1)S(1)}) custom-call(s32[1]{0:T(128)} %bitcast.1.section_ref, s32[2,64]{1,0:T(2,128)} %bitcast.17, f32[2,64]{1,0:T(2,128)} %bitcast.18, bf16[64,6144]{1,0:T(8,128)(2,1)} %bitcast.15), custom_call_target="tpu_custom_call" | custom-call | bytes 1572864 | tf_op jit(solution)/shard_map/pack/pallas_call | solution.py:238
  1.5 4.1 %collective-permute-start.2 = (bf16[16,6912]{1,0:T(8,128)(2,1)S(1)}, bf16[16,6912]{1,0:T(8,128)(2,1)S(1)}, u32[]{:S(2)}, u32[]{:S(2)}) collective-permute-start(bf16[16,6912]{1,0:T(8,128)(2,1)S(1)} %get-tuple-element.23.after_ref.refs_0_), channel_id=1, source_target_pairs={{0,4},{1,5},{2,6},{3,7},{4,0},{5,1},{6,2},{7,3},{8,12},{9,13},{10,... | collective-permute-start | bytes 663560 | tf_op jit(solution)/shard_map/ppermute | solution.py:229
  5.6 1.3 %collective-permute-start.3 = (bf16[16,6912]{1,0:T(8,128)(2,1)S(1)}, bf16[16,6912]{1,0:T(8,128)(2,1)S(1)}, u32[]{:S(2)}, u32[]{:S(2)}) collective-permute-start(bf16[16,6912]{1,0:T(8,128)(2,1)S(1)} %get-tuple-element.23.after_ref.refs_0_), channel_id=1, source_target_pairs={{0,6},{1,7},{2,4},{3,5},{4,2},{5,3},{6,0},{7,1},{8,14},{9,15},{10,... | collective-permute-start | bytes 663560 | tf_op jit(solution)/shard_map/ppermute | solution.py:229
  6.9 0.2 collective-permute-start.1
  7.1 12.1 %fetch.1 = (bf16[6144,1024]{1,0:T(8,128)(2,1)S(1)}, bf16[6144,1024]{1,0:T(8,128)(2,1)S(1)}, bf16[1024,6144]{1,0:T(8,128)(2,1)S(1)}, f32[8,128]{1,0:T(8,128)S(1)}) custom-call(bf16[16,6912]{1,0:T(8,128)(2,1)S(1)} %get-tuple-element.23.after_ref.refs_0_, bf16[6144,1024]{1,0:T(8,128)(2,1)} %bitcast.12, bf16[6144,1024]{1,0:T(8,128)(2,1)} %bitcast.13, ...), custom_call_target="tpu_custom_call" | custom-call | bytes 75497472 | tf_op jit(solution)/shard_map/fetch/pallas_call | solution.py:259
  19.2 2.1 %collective-permute-done.2.refs_0_ = bf16[16,6912]{1,0:T(8,128)(2,1)S(1)} collective-permute-done((bf16[16,6912]{1,0:T(8,128)(2,1)S(1)}, bf16[16,6912]{1,0:T(8,128)(2,1)S(1)}, u32[]{:S(2)}, u32[]{:S(2)}) %collective-permute-start.2) | collective-permute-done | bytes 221216 | tf_op jit(solution)/shard_map/ppermute | solution.py:229
  21.5 0.4 collective-permute-done.1.refs_1_
  22.1 1.8 %collective-permute-start = (bf16[64,6144]{1,0:T(8,128)(2,1)S(1)}, bf16[64,6144]{1,0:T(8,128)(2,1)S(1)}, u32[]{:S(2)}, u32[]{:S(2)}) collective-permute-start(bf16[64,6144]{1,0:T(8,128)(2,1)S(1)} %bitcast.16), channel_id=1, source_target_pairs={{0,8},{8,16},{16,24},{24,0},{1,9},{9,17},{17,25},{25,1},{2,10},{10... | collective-permute-start | bytes 2359304 | tf_op jit(solution)/shard_map/ppermute | solution.py:235
  23.9 4.0 %hidden.1.refs_0_ = bf16[144,1024]{1,0:T(8,128)(2,1)S(1)} custom-call(bf16[6144,1024]{1,0:T(8,128)(2,1)S(1)} %get-tuple-element.24.refs_0_, bf16[6144,1024]{1,0:T(8,128)(2,1)S(1)} %get-tuple-element.25.refs_1_, bf16[32,6912]{1,0:T(8,128)(2,1)S(1)} %stack.2.refs_2_, bf16[32,6912]{1,0:T(8,128)(2,1)S(1)} %stack.3.refs_3_, ...), custom_call_target="tpu_custom_call" | custom-call | flops 3623878656 | bytes 25165824 | tf_op jit(solution)/shard_map/hidden/pallas_call | solution.py:287
  27.9 1.3 %down.2 = (f32[64,3456]{1,0:T(8,128)S(1)}, bf16[64,3456]{1,0:T(8,128)(2,1)S(1)}) custom-call(bf16[144,1024]{1,0:T(8,128)(2,1)S(1)} %hidden.1.refs_0_, bf16[1024,6144]{1,0:T(8,128)(2,1)S(1)} %get-tuple-element.27.refs_1_), custom_call_target="tpu_custom_call" | custom-call | tf_op jit(solution)/shard_map/down/pallas_call | solution.py:300
  29.2 0.2 collective-permute-start.6
  29.4 1.3 %down.3 = (f32[64,3456]{1,0:T(8,128)S(1)}, bf16[64,3456]{1,0:T(8,128)(2,1)S(1)}) custom-call(bf16[144,1024]{1,0:T(8,128)(2,1)S(1)} %hidden.1.refs_0_, bf16[1024,6144]{1,0:T(8,128)(2,1)S(1)} %get-tuple-element.27.refs_1_), custom_call_target="tpu_custom_call" | custom-call | tf_op jit(solution)/shard_map/down/pallas_call | solution.py:300
  30.7 0.5 collective-permute-start.11
  31.2 3.4 %collective-permute-start.7 = (bf16[16,3456]{1,0:T(8,128)(2,1)S(1)}, bf16[16,3456]{1,0:T(8,128)(2,1)S(1)}, u32[]{:S(2)}, u32[]{:S(2)}) collective-permute-start(bf16[16,3456]{1,0:T(8,128)(2,1)S(1)} %get-tuple-element.32), channel_id=1, source_target_pairs={{0,6},{1,7},{2,4},{3,5},{4,2},{5,3},{6,0},{7,1},{8,14},{9,15},{10,... | collective-permute-start | bytes 331784 | tf_op jit(solution)/shard_map/ppermute | solution.py:229
  34.6 3.7 %collective-permute-start.8 = (bf16[16,3456]{1,0:T(8,128)(2,1)S(1)}, bf16[16,3456]{1,0:T(8,128)(2,1)S(1)}, u32[]{:S(2)}, u32[]{:S(2)}) collective-permute-start(bf16[16,3456]{1,0:T(8,128)(2,1)S(1)} %get-tuple-element.33), channel_id=1, source_target_pairs={{0,2},{1,3},{2,0},{3,1},{4,6},{5,7},{6,4},{7,5},{8,10},{9,11},{10,... | collective-permute-start | bytes 331784 | tf_op jit(solution)/shard_map/ppermute | solution.py:229
  38.5 1.5 %collective-permute-start.12 = (bf16[16,3584]{1,0:T(8,128)(2,1)S(1)}, bf16[16,3584]{1,0:T(8,128)(2,1)S(1)}, u32[]{:S(2)}, u32[]{:S(2)}) collective-permute-start(bf16[16,3584]{1,0:T(8,128)(2,1)S(1)} %get-tuple-element.37), channel_id=1, source_target_pairs={{0,8},{1,9},{2,10},{3,11},{4,12},{5,13},{6,14},{7,15},{8,16},{9,17... | collective-permute-start | bytes 344072 | tf_op jit(solution)/shard_map/ppermute | solution.py:226
  40.0 3.0 %collective-permute-start.13 = (bf16[16,3456]{1,0:T(8,128)(2,1)S(1)}, bf16[16,3456]{1,0:T(8,128)(2,1)S(1)}, u32[]{:S(2)}, u32[]{:S(2)}) collective-permute-start(bf16[16,3456]{1,0:T(8,128)(2,1)S(1)} %get-tuple-element.38), channel_id=1, source_target_pairs={{0,10},{1,11},{2,8},{3,9},{4,14},{5,15},{6,12},{7,13},{8,18},{9,19... | collective-permute-start | bytes 331784 | tf_op jit(solution)/shard_map/ppermute | solution.py:226
  43.0 2.4 %collective-permute-start.14 = (bf16[16,3456]{1,0:T(8,128)(2,1)S(1)}, bf16[16,3456]{1,0:T(8,128)(2,1)S(1)}, u32[]{:S(2)}, u32[]{:S(2)}) collective-permute-start(bf16[16,3456]{1,0:T(8,128)(2,1)S(1)} %get-tuple-element.39), channel_id=1, source_target_pairs={{0,12},{1,13},{2,14},{3,15},{4,8},{5,9},{6,10},{7,11},{8,20},{9,21... | collective-permute-start | bytes 331784 | tf_op jit(solution)/shard_map/ppermute | solution.py:226
  45.4 0.9 %collective-permute-done.9.refs_3_ = bf16[16,3456]{1,0:T(8,128)(2,1)S(1)} collective-permute-done((bf16[16,3456]{1,0:T(8,128)(2,1)S(1)}, bf16[16,3456]{1,0:T(8,128)(2,1)S(1)}, u32[]{:S(2)}, u32[]{:S(2)}) %collective-permute-start.9) | collective-permute-done | bytes 110624 | tf_op jit(solution)/shard_map/ppermute | solution.py:229
  46.3 3.4 %collective-permute-start.15 = (bf16[16,3456]{1,0:T(8,128)(2,1)S(1)}, bf16[16,3456]{1,0:T(8,128)(2,1)S(1)}, u32[]{:S(2)}, u32[]{:S(2)}) collective-permute-start(bf16[16,3456]{1,0:T(8,128)(2,1)S(1)} %get-tuple-element.40), channel_id=1, source_target_pairs={{0,14},{1,15},{2,12},{3,13},{4,10},{5,11},{6,8},{7,9},{8,22},{9,23... | collective-permute-start | bytes 331784 | tf_op jit(solution)/shard_map/ppermute | solution.py:226
  49.8 1.5 %collective-permute-start.10 = (bf16[16,3456]{1,0:T(8,128)(2,1)S(1)}, bf16[16,3456]{1,0:T(8,128)(2,1)S(1)}, u32[]{:S(2)}, u32[]{:S(2)}) collective-permute-start(bf16[16,3456]{1,0:T(8,128)(2,1)S(1)} %sum_chips.1), channel_id=1, source_target_pairs={{0,8},{8,16},{16,24},{24,0},{1,9},{9,17},{17,25},{25,1},{2,10},{10... | collective-permute-start | bytes 331784 | tf_op jit(solution)/shard_map/ppermute | solution.py:235
  51.3 4.6 %collective-permute-done.14.refs_3_ = bf16[16,3456]{1,0:T(8,128)(2,1)S(1)} collective-permute-done((bf16[16,3456]{1,0:T(8,128)(2,1)S(1)}, bf16[16,3456]{1,0:T(8,128)(2,1)S(1)}, u32[]{:S(2)}, u32[]{:S(2)}) %collective-permute-start.14) | collective-permute-done | bytes 110624 | tf_op jit(solution)/shard_map/ppermute | solution.py:226
  55.9 1.7 %collective-permute-done.10.refs_0_ = bf16[16,3456]{1,0:T(8,128)(2,1)S(1)} collective-permute-done((bf16[16,3456]{1,0:T(8,128)(2,1)S(1)}, bf16[16,3456]{1,0:T(8,128)(2,1)S(1)}, u32[]{:S(2)}, u32[]{:S(2)}) %collective-permute-start.10) | collective-permute-done | bytes 110624 | tf_op jit(solution)/shard_map/ppermute | solution.py:235
  57.5 1.4 %combine.1 = bf16[64,6144]{1,0:T(8,128)(2,1)} custom-call(bf16[64,6144]{1,0:T(8,128)(2,1)S(1)} %collective-permute-done.rows_ref, bf16[16,3456]{1,0:T(8,128)(2,1)S(1)} %collective-permute-done.10.refs_0_, bf16[16,3584]{1,0:T(8,128)(2,1)S(1)} %collective-permute-done.12.refs_1_, bf16[16,3456]{1,0:T(8,128)(2,1)S(1)} %collective-permute-done.13.refs_2_, ...), custom_call_target="tpu_custom_call" | custom-call | tf_op jit(solution)/shard_map/combine/pallas_call | solution.py:338
  (21 shorter events, 0.6 us)
Async XLA Ops:
  1.5 19.9 %collective-permute-start.2 = (bf16[16,6912]{1,0:T(8,128)(2,1)S(1)}, bf16[16,6912]{1,0:T(8,128)(2,1)S(1)}, u32[]{:S(2)}, u32[]{:S(2)}) collective-permute-start(bf16[16,6912]{1,0:T(8,128)(2,1)S(1)} %get-tuple-element.23.after_ref.refs_0_), channel_id=1, source_target_pairs={{0,4},{1,5},{2,6},{3,7},{4,0},{5,1},{6,2},{7,3},{8,12},{9,13},{10,... | collective-permute-start | bytes 663560 | tf_op jit(solution)/shard_map/ppermute | solution.py:229
  5.6 15.8 %collective-permute-start.3 = (bf16[16,6912]{1,0:T(8,128)(2,1)S(1)}, bf16[16,6912]{1,0:T(8,128)(2,1)S(1)}, u32[]{:S(2)}, u32[]{:S(2)}) collective-permute-start(bf16[16,6912]{1,0:T(8,128)(2,1)S(1)} %get-tuple-element.23.after_ref.refs_0_), channel_id=1, source_target_pairs={{0,6},{1,7},{2,4},{3,5},{4,2},{5,3},{6,0},{7,1},{8,14},{9,15},{10,... | collective-permute-start | bytes 663560 | tf_op jit(solution)/shard_map/ppermute | solution.py:229
  6.9 14.9 %collective-permute-start.1 = (bf16[16,6912]{1,0:T(8,128)(2,1)S(1)}, bf16[16,6912]{1,0:T(8,128)(2,1)S(1)}, u32[]{:S(2)}, u32[]{:S(2)}) collective-permute-start(bf16[16,6912]{1,0:T(8,128)(2,1)S(1)} %get-tuple-element.23.after_ref.refs_0_), channel_id=1, source_target_pairs={{0,2},{1,3},{2,0},{3,1},{4,6},{5,7},{6,4},{7,5},{8,10},{9,11},{10,... | collective-permute-start | bytes 663560 | tf_op jit(solution)/shard_map/ppermute | solution.py:229
  7.1 14.9 %copy-start = (bf16[1,64,6144]{2,1,0:T(8,128)(2,1)S(1)}, bf16[1,64,6144]{2,1,0:T(8,128)(2,1)}, u32[]{:S(2)}) copy-start(bf16[1,64,6144]{2,1,0:T(8,128)(2,1)} %param.6) | copy-start | bytes 2359300
  21.4 2.5 %collective-permute-start.5 = (bf16[32,6912]{1,0:T(8,128)(2,1)S(1)}, bf16[32,6912]{1,0:T(8,128)(2,1)S(1)}, u32[]{:S(2)}, u32[]{:S(2)}) collective-permute-start(bf16[32,6912]{1,0:T(8,128)(2,1)S(1)} %stack.3.refs_3_), channel_id=1, source_target_pairs={{0,1},{1,0},{2,3},{3,2},{4,5},{5,4},{6,7},{7,6},{8,9},{9,8},{10,11... | collective-permute-start | bytes 1327112 | tf_op jit(solution)/shard_map/ppermute | solution.py:232
  21.9 2.0 %collective-permute-start.4 = (bf16[32,6912]{1,0:T(8,128)(2,1)S(1)}, bf16[32,6912]{1,0:T(8,128)(2,1)S(1)}, u32[]{:S(2)}, u32[]{:S(2)}) collective-permute-start(bf16[32,6912]{1,0:T(8,128)(2,1)S(1)} %stack.2.refs_2_), channel_id=1, source_target_pairs={{0,1},{1,0},{2,3},{3,2},{4,5},{5,4},{6,7},{7,6},{8,9},{9,8},{10,11... | collective-permute-start | bytes 1327112 | tf_op jit(solution)/shard_map/ppermute | solution.py:232
  22.1 27.7 %collective-permute-start = (bf16[64,6144]{1,0:T(8,128)(2,1)S(1)}, bf16[64,6144]{1,0:T(8,128)(2,1)S(1)}, u32[]{:S(2)}, u32[]{:S(2)}) collective-permute-start(bf16[64,6144]{1,0:T(8,128)(2,1)S(1)} %bitcast.16), channel_id=1, source_target_pairs={{0,8},{8,16},{16,24},{24,0},{1,9},{9,17},{17,25},{25,1},{2,10},{10... | collective-permute-start | bytes 2359304 | tf_op jit(solution)/shard_map/ppermute | solution.py:235
  29.2 1.9 %collective-permute-start.6 = (bf16[64,3456]{1,0:T(8,128)(2,1)S(1)}, bf16[64,3456]{1,0:T(8,128)(2,1)S(1)}, u32[]{:S(2)}, u32[]{:S(2)}) collective-permute-start(bf16[64,3456]{1,0:T(8,128)(2,1)S(1)} %get-tuple-element.29), channel_id=1, source_target_pairs={{0,1},{1,0},{2,3},{3,2},{4,5},{5,4},{6,7},{7,6},{8,9},{9,8},{10,11... | collective-permute-start | bytes 1327112 | tf_op jit(solution)/shard_map/ppermute | solution.py:232
  30.7 7.7 %collective-permute-start.11 = (bf16[64,3456]{1,0:T(8,128)(2,1)S(1)}, bf16[64,3456]{1,0:T(8,128)(2,1)S(1)}, u32[]{:S(2)}, u32[]{:S(2)}) collective-permute-start(bf16[64,3456]{1,0:T(8,128)(2,1)S(1)} %get-tuple-element.36), channel_id=1, source_target_pairs={{0,1},{1,0},{2,3},{3,2},{4,5},{5,4},{6,7},{7,6},{8,9},{9,8},{10,11... | collective-permute-start | bytes 1327112 | tf_op jit(solution)/shard_map/ppermute | solution.py:232
  31.2 8.8 %collective-permute-start.7 = (bf16[16,3456]{1,0:T(8,128)(2,1)S(1)}, bf16[16,3456]{1,0:T(8,128)(2,1)S(1)}, u32[]{:S(2)}, u32[]{:S(2)}) collective-permute-start(bf16[16,3456]{1,0:T(8,128)(2,1)S(1)} %get-tuple-element.32), channel_id=1, source_target_pairs={{0,6},{1,7},{2,4},{3,5},{4,2},{5,3},{6,0},{7,1},{8,14},{9,15},{10,... | collective-permute-start | bytes 331784 | tf_op jit(solution)/shard_map/ppermute | solution.py:229
  34.6 8.3 %collective-permute-start.8 = (bf16[16,3456]{1,0:T(8,128)(2,1)S(1)}, bf16[16,3456]{1,0:T(8,128)(2,1)S(1)}, u32[]{:S(2)}, u32[]{:S(2)}) collective-permute-start(bf16[16,3456]{1,0:T(8,128)(2,1)S(1)} %get-tuple-element.33), channel_id=1, source_target_pairs={{0,2},{1,3},{2,0},{3,1},{4,6},{5,7},{6,4},{7,5},{8,10},{9,11},{10,... | collective-permute-start | bytes 331784 | tf_op jit(solution)/shard_map/ppermute | solution.py:229
  38.4 7.9 %collective-permute-start.9 = (bf16[16,3456]{1,0:T(8,128)(2,1)S(1)}, bf16[16,3456]{1,0:T(8,128)(2,1)S(1)}, u32[]{:S(2)}, u32[]{:S(2)}) collective-permute-start(bf16[16,3456]{1,0:T(8,128)(2,1)S(1)} %get-tuple-element.34), channel_id=1, source_target_pairs={{0,4},{1,5},{2,6},{3,7},{4,0},{5,1},{6,2},{7,3},{8,12},{9,13},{10,... | collective-permute-start | bytes 331784 | tf_op jit(solution)/shard_map/ppermute | solution.py:229
  38.5 17.4 %collective-permute-start.12 = (bf16[16,3584]{1,0:T(8,128)(2,1)S(1)}, bf16[16,3584]{1,0:T(8,128)(2,1)S(1)}, u32[]{:S(2)}, u32[]{:S(2)}) collective-permute-start(bf16[16,3584]{1,0:T(8,128)(2,1)S(1)} %get-tuple-element.37), channel_id=1, source_target_pairs={{0,8},{1,9},{2,10},{3,11},{4,12},{5,13},{6,14},{7,15},{8,16},{9,17... | collective-permute-start | bytes 344072 | tf_op jit(solution)/shard_map/ppermute | solution.py:226
  40.0 11.3 %collective-permute-start.13 = (bf16[16,3456]{1,0:T(8,128)(2,1)S(1)}, bf16[16,3456]{1,0:T(8,128)(2,1)S(1)}, u32[]{:S(2)}, u32[]{:S(2)}) collective-permute-start(bf16[16,3456]{1,0:T(8,128)(2,1)S(1)} %get-tuple-element.38), channel_id=1, source_target_pairs={{0,10},{1,11},{2,8},{3,9},{4,14},{5,15},{6,12},{7,13},{8,18},{9,19... | collective-permute-start | bytes 331784 | tf_op jit(solution)/shard_map/ppermute | solution.py:226
  43.0 12.9 %collective-permute-start.14 = (bf16[16,3456]{1,0:T(8,128)(2,1)S(1)}, bf16[16,3456]{1,0:T(8,128)(2,1)S(1)}, u32[]{:S(2)}, u32[]{:S(2)}) collective-permute-start(bf16[16,3456]{1,0:T(8,128)(2,1)S(1)} %get-tuple-element.39), channel_id=1, source_target_pairs={{0,12},{1,13},{2,14},{3,15},{4,8},{5,9},{6,10},{7,11},{8,20},{9,21... | collective-permute-start | bytes 331784 | tf_op jit(solution)/shard_map/ppermute | solution.py:226
  46.3 9.6 %collective-permute-start.15 = (bf16[16,3456]{1,0:T(8,128)(2,1)S(1)}, bf16[16,3456]{1,0:T(8,128)(2,1)S(1)}, u32[]{:S(2)}, u32[]{:S(2)}) collective-permute-start(bf16[16,3456]{1,0:T(8,128)(2,1)S(1)} %get-tuple-element.40), channel_id=1, source_target_pairs={{0,14},{1,15},{2,12},{3,13},{4,10},{5,11},{6,8},{7,9},{8,22},{9,23... | collective-permute-start | bytes 331784 | tf_op jit(solution)/shard_map/ppermute | solution.py:226
  49.8 7.8 %collective-permute-start.10 = (bf16[16,3456]{1,0:T(8,128)(2,1)S(1)}, bf16[16,3456]{1,0:T(8,128)(2,1)S(1)}, u32[]{:S(2)}, u32[]{:S(2)}) collective-permute-start(bf16[16,3456]{1,0:T(8,128)(2,1)S(1)} %sum_chips.1), channel_id=1, source_target_pairs={{0,8},{8,16},{16,24},{24,0},{1,9},{9,17},{17,25},{25,1},{2,10},{10... | collective-permute-start | bytes 331784 | tf_op jit(solution)/shard_map/ppermute | solution.py:235
